TPU v7x, 256 devices: a whole 4x4x8 slice. The times are simulated.
256 devices in a mesh: dp: 16 (over x, y), expert: 16 (over z, core).
Axes of the slice: x: 4, y: 4, z: 8, core: 2. Of those that a mesh axis runs over, the one named last changes fastest.
Arguments:
- tokens: bfloat16 [40960, 2048], P(('dp', 'expert')), may hold values from -24 to 24
- out_grads: bfloat16 [40960, 2048], P(('dp', 'expert')), may hold values from -6 to 6
- expert_ids: int32 [40960, 1], P(('dp', 'expert')), may hold values from 0 to 15; in each aligned block of 160 rows (0 to 159, 160 to 319, ...) at most 30 rows name the same one
- w_gate_up: bfloat16 [16, 2048, 1536], P('expert'), may hold values from -0.125 to 0.125
- w_down_t: bfloat16 [16, 2048, 768], P('expert'), may hold values from -0.21875 to 0.21875
Outputs:
- token_grads: bfloat16 [40960, 2048], P(('dp', 'expert'))
- grad_gate_up: bfloat16 [16, 2048, 1536], P('expert', 'dp')
- grad_down_t: bfloat16 [16, 2048, 768], P('expert', 'dp')
Inputs may be any that keep to these rules, and one draw needn't show every extreme that they name: `expert_ids`: within one device's 160 rows (an aligned block) no expert is named more than 30 times; in some blocks one expert is named exactly 30 times.
All inputs are finite; a program needn't handle non-finite values.
Results may differ from a plain program's by a relative error of at most 0.02.
Values may be sent and summed in bfloat16 or wider, within the bound.
No kernel may reach another device: no remote copies, remote signals or barrier semaphores. Data moves between devices by JAX's collectives and lax.ppermute only.
A program may use at most 128 MiB of HBM per device.

v0:
```python
import jax
import jax.numpy as jnp
from jax import lax
from jax.experimental import pallas as pl
from jax.experimental.pallas import tpu as pltpu
from jax.sharding import PartitionSpec as P

SLOTS = 32
SIDE = 4
LANE = 128
CHUNKS = 4
SMALL = pl.CostEstimate(flops=1000000, bytes_accessed=100000, transcendentals=0)


def token_slots(routed):
    rows = routed.shape[0]
    places = jnp.arange(rows, dtype=jnp.int32)
    same = (routed[:, None] == routed[None, :]) & (places[:, None] < places[None, :])
    return jnp.sum(same.astype(jnp.int32), axis=0)


def one_hot_rows(target, count):
    spots = jnp.arange(count, dtype=jnp.int32)
    return (spots[:, None] == target[None, :]).astype(jnp.bfloat16)


def feature_blocks(ref, table, f, chunk):
    pair = [
        ref[:, pl.ds(pl.multiple_of(table[f, 2 * chunk + k] * LANE, LANE), LANE)] for k in range(2)
    ]
    return jnp.concatenate(pair, axis=1)


def lanes(chunk):
    return pl.ds(pl.multiple_of(chunk * (2 * LANE), 2 * LANE), 2 * LANE)


def dot32(left, right):
    return jnp.dot(left, right, preferred_element_type=jnp.float32)


def product(left, right):
    return dot32(left, right).astype(jnp.bfloat16)


def flow_parts(f, per, split):
    low, high = f * per, (f + 1) * per
    parts = []
    if low < split:
        parts.append((True, low, min(high, split) - low, 0))
    if high > split:
        begin = max(low, split)
        parts.append((False, begin - split, high - begin, begin - low))
    return parts


def join_copies(places, pieces, to_ref, sems):
    copies = []
    for d, piece in enumerate(pieces):
        for k in range(2):
            row = pl.multiple_of(places[2 * d + k] * SLOTS, SLOTS)
            copies.append(
                pltpu.make_async_copy(piece.at[k], to_ref.at[pl.ds(row, SLOTS)], sems.at[2 * d + k])
            )
    return copies


def join_kernel(places, *refs):
    *pieces, out_ref, sems = refs
    copies = join_copies(places, pieces, out_ref, sems)
    for copy in copies:
        copy.start()
    for copy in copies:
        copy.wait()


def join(places, pieces):
    width = pieces[0].shape[2]
    rows = 2 * len(pieces) * SLOTS
    return pl.pallas_call(
        join_kernel,
        in_specs=[pl.BlockSpec(memory_space=pltpu.SMEM)] + [pl.BlockSpec(memory_space=pl.ANY)] * len(pieces),
        out_specs=pl.BlockSpec(memory_space=pltpu.VMEM),
        out_shape=jax.ShapeDtypeStruct((rows, width), jnp.bfloat16),
        scratch_shapes=[pltpu.SemaphoreType.DMA((2 * len(pieces),))],
        compiler_params=pltpu.CompilerParams(vmem_limit_bytes=16 * 1024 * 1024),
        cost_estimate=SMALL,
        name="join",
    )(places, *pieces)


def dgate_up_kernel(places, table, w_ref, a_ref, s_ref, hid_ref, *refs):
    *pieces, dy_ref, out_ref, give_ref, sems = refs
    copies = join_copies(places, pieces, dy_ref, sems)
    for copy in copies:
        copy.start()
    for copy in copies:
        copy.wait()
    start = hid_ref.shape[0] - give_ref.shape[0]

    def give(chunk, carry):
        give_ref[:, lanes(chunk)] = product(hid_ref[start:, :], feature_blocks(dy_ref, table, 3, chunk))
        return carry

    lax.fori_loop(0, CHUNKS, give, 0)
    tile = 256

    def dhidden_tile(i, carry):
        part = pl.ds(pl.multiple_of(i * tile, tile), tile)
        dhidden = lax.dot_general(
            w_ref[part, :], dy_ref[...], (((1,), (1,)), ((), ())), preferred_element_type=jnp.float32
        )
        out_ref[0, part] = (dhidden * a_ref[part, :]).astype(jnp.bfloat16)
        out_ref[1, part] = (dhidden * s_ref[part, :]).astype(jnp.bfloat16)
        return carry

    lax.fori_loop(0, w_ref.shape[0] // tile, dhidden_tile, 0)


def make_dgate_up(places, table, w_out_t, slope, silu, hidden, pieces):
    ff, width = w_out_t.shape
    rows = 2 * len(pieces) * SLOTS
    per = 3 * ff // 4
    whole = pl.BlockSpec(memory_space=pltpu.VMEM)
    small = pl.BlockSpec(memory_space=pltpu.SMEM)
    return pl.pallas_call(
        dgate_up_kernel,
        in_specs=[small] * 2 + [whole] * 4 + [pl.BlockSpec(memory_space=pl.ANY)] * len(pieces),
        out_specs=[whole] * 3,
        out_shape=[
            jax.ShapeDtypeStruct((rows, width), jnp.bfloat16),
            jax.ShapeDtypeStruct((2, ff, rows), jnp.bfloat16),
            jax.ShapeDtypeStruct((per, 2 * CHUNKS * LANE), jnp.bfloat16),
        ],
        scratch_shapes=[pltpu.SemaphoreType.DMA((2 * len(pieces),))],
        compiler_params=pltpu.CompilerParams(vmem_limit_bytes=24 * 1024 * 1024),
        cost_estimate=SMALL,
        name="dgate_up",
    )(places, table, w_out_t, slope, silu, hidden, *pieces)


def gives_kernel(flows, table, dgu_ref, hid_ref, x_ref, dy_ref, *refs):
    n = len(flows)
    outs, stages, sems = refs[:n], refs[n : 2 * n], refs[2 * n]
    per = outs[0].shape[0]

    def copy(i, chunk):
        return pltpu.make_async_copy(
            stages[i].at[:, lanes(chunk)], outs[i].at[:, lanes(chunk)], sems.at[i, chunk]
        )

    for i, f in enumerate(flows):

        def body(chunk, carry):
            for from_dgu, first, count, row in flow_parts(f, per, dgu_ref.shape[0]):
                left, right = (dgu_ref, x_ref) if from_dgu else (hid_ref, dy_ref)
                stages[i][row : row + count, lanes(chunk)] = product(
                    left[first : first + count, :], feature_blocks(right, table, f, chunk)
                )
            copy(i, chunk).start()
            return carry

        lax.fori_loop(0, CHUNKS, body, 0)
    for i in range(n):
        for chunk in range(CHUNKS):
            copy(i, chunk).wait()


def make_gives(flows, table, dgu, hidden, rows_x, rows_dy):
    per = (dgu.shape[0] + hidden.shape[0]) // 4
    size = (per, 2 * CHUNKS * LANE)
    whole = pl.BlockSpec(memory_space=pltpu.VMEM)
    return pl.pallas_call(
        lambda *refs: gives_kernel(flows, *refs),
        in_specs=[pl.BlockSpec(memory_space=pltpu.SMEM)] + [whole] * 4,
        out_specs=[pl.BlockSpec(memory_space=pl.ANY)] * len(flows),
        out_shape=[jax.ShapeDtypeStruct(size, jnp.bfloat16)] * len(flows),
        scratch_shapes=[pltpu.VMEM(size, jnp.bfloat16)] * len(flows)
        + [pltpu.SemaphoreType.DMA((len(flows), CHUNKS))],
        compiler_params=pltpu.CompilerParams(vmem_limit_bytes=16 * 1024 * 1024),
        cost_estimate=SMALL,
        name="give",
    )(table, dgu, hidden, rows_x, rows_dy)


def merge_kernel(f, table, got_ref, *refs):
    *sides, give_ref, keep_ref = refs
    per = give_ref.shape[0]
    half = CHUNKS // 2
    for out, base in ((give_ref, 0), (keep_ref, half)):

        def body(i, carry):
            chunk = base + i
            for k, (_, first, count, row) in enumerate(flow_parts(f, per, 8 * per // 3)):
                total = dot32(
                    sides[2 * k][first : first + count, :], feature_blocks(sides[2 * k + 1], table, f, chunk)
                )
                total += got_ref[row : row + count, lanes(chunk)].astype(jnp.float32)
                out[row : row + count, lanes(i)] = total.astype(jnp.bfloat16)
            return carry

        lax.fori_loop(0, half, body, 0)


def merge(f, table, got, dgu, hidden, rows_x, rows_dy):
    per = got.shape[0]
    sides = []
    for from_dgu, *_ in flow_parts(f, per, dgu.shape[0]):
        sides += [dgu, rows_x] if from_dgu else [hidden, rows_dy]
    whole = pl.BlockSpec(memory_space=pltpu.VMEM)
    return pl.pallas_call(
        lambda *refs: merge_kernel(f, *refs),
        in_specs=[pl.BlockSpec(memory_space=pltpu.SMEM)] + [whole] * (1 + len(sides)),
        out_specs=[whole] * 2,
        out_shape=[jax.ShapeDtypeStruct((per, CHUNKS * LANE), jnp.bfloat16)] * 2,
        compiler_params=pltpu.CompilerParams(vmem_limit_bytes=12 * 1024 * 1024),
        cost_estimate=SMALL,
        name="merge",
    )(table, got, *sides)


def finish_kernel(*refs):
    *parts, up_ref, down_ref = refs
    n = len(parts) // 2
    total = jnp.concatenate(
        [parts[i][...].astype(jnp.float32) + parts[n + i][...].astype(jnp.float32) for i in range(n)], axis=0
    )
    split = up_ref.shape[1]
    up_ref[...] = total[:split].T.astype(jnp.bfloat16)
    down_ref[...] = total[split:].T.astype(jnp.bfloat16)


def finish(keeps, gots):
    per, lane = keeps[0].shape
    whole = pl.BlockSpec(memory_space=pltpu.VMEM)
    return pl.pallas_call(
        finish_kernel,
        in_specs=[whole] * 8,
        out_specs=[whole] * 2,
        out_shape=[
            jax.ShapeDtypeStruct((lane, 8 * per // 3), jnp.bfloat16),
            jax.ShapeDtypeStruct((lane, 4 * per // 3), jnp.bfloat16),
        ],
        compiler_params=pltpu.CompilerParams(vmem_limit_bytes=12 * 1024 * 1024),
        cost_estimate=SMALL,
        name="finish",
    )(*keeps, *gots)


def mate(i, odd):
    return (3 - i) if odd else (i ^ 1)


def pair_perm(axis, odd):
    return [
        (x * SIDE + y, mate(x, odd) * SIDE + y if axis == 0 else x * SIDE + mate(y, odd))
        for x in range(SIDE)
        for y in range(SIDE)
    ]


FLOWS = ((0, False), (0, True), (1, False), (1, True))


def first_table(at, axis, odd):
    a, b = at[axis], at[1 - axis]

    def kept(i):
        return [mate(i, not odd), i]

    minor = jnp.stack(kept(mate(b, odd)) + kept(b)).astype(jnp.int32)

    def blocks(i):
        major = jnp.stack(kept(i)).astype(jnp.int32)
        ids = major[:, None] * SIDE + minor[None, :] if axis == 0 else minor[None, :] * SIDE + major[:, None]
        return ids.reshape(-1)

    return blocks(mate(a, odd)), blocks(a)


def local(tokens, out_grads, expert_ids, w_gate_up, w_down_t):
    num_experts = lax.axis_size("expert")
    chips = num_experts // 2
    width = tokens.shape[1]
    ff = w_down_t.shape[2]
    rows = num_experts * SLOTS
    place = lax.axis_index("expert")
    chip, core = place // 2, place % 2
    routed = expert_ids[:, 0]
    slots = token_slots(routed)
    relative = ((routed // 2 - chip + chips) % chips) * SLOTS + slots
    own = routed % 2 == core
    mine_rows = one_hot_rows(jnp.where(own, relative, -1), chips * SLOTS)
    other_rows = one_hot_rows(jnp.where(own, -1, relative), chips * SLOTS)
    distance = jnp.arange(chips, dtype=jnp.int32)
    places = (
        ((chip - distance + chips) % chips)[:, None] * 2
        + jnp.array([0, 1], jnp.int32)[None, :] * (1 - 2 * core)
        + core
    ).reshape(-1)

    def send(values):
        def pack(table):
            packed = jnp.dot(table, values, preferred_element_type=jnp.float32)
            return packed.astype(jnp.bfloat16).reshape(chips, SLOTS, width)

        other = lax.ppermute(pack(other_rows), "expert", [(i, i ^ 1) for i in range(num_experts)])
        both = jnp.stack([pack(mine_rows), other], axis=1)
        pieces = [both[0]] + [None] * (chips - 1)
        for d in (4, 3, 5, 2, 6, 1, 7):
            pieces[d] = lax.ppermute(
                both[d], "expert", [(i, (i + 2 * d) % num_experts) for i in range(num_experts)]
            )
        return pieces

    rows_x = join(places, send(tokens))
    pieces_dy = send(out_grads)
    w_in = w_gate_up[0]
    w_out, rows_x = lax.optimization_barrier((w_down_t[0], rows_x))
    w_out_t = w_out.T

    gate_up = lax.dot_general(
        w_in, rows_x, (((0,), (1,)), ((), ())), preferred_element_type=jnp.float32
    )
    gate = gate_up[:ff]
    upper = gate_up[ff:]
    sig = jax.nn.sigmoid(gate)
    silu = gate * sig
    hidden = (silu * upper).astype(jnp.bfloat16)
    slope = upper * sig * (1.0 + gate * (1.0 - sig))

    me = lax.axis_index("dp")
    at = (me // SIDE, me % SIDE)
    tables = [first_table(at, axis, odd) for axis, odd in FLOWS]

    to_give = jnp.stack([t[0] for t in tables])
    to_keep = jnp.stack([t[1] for t in tables])
    rows_dy, dgu, last_give = make_dgate_up(places, to_give, w_out_t, slope, silu, hidden, pieces_dy)
    dgu = dgu.reshape(2 * ff, rows)
    gives = [*make_gives((0, 1, 2), to_give, dgu, hidden, rows_x, rows_dy), last_give]
    gots = [None] * 4
    for f in (3, 0, 1, 2):
        gots[f] = lax.ppermute(gives[f], "dp", pair_perm(*FLOWS[f]))
    drows = lax.dot_general(
        dgu, w_in, (((0,), (1,)), ((), ())), preferred_element_type=jnp.float32
    ).astype(jnp.bfloat16)
    returned = lax.all_to_all(
        drows.reshape(num_experts, SLOTS, width), "expert", split_axis=0, concat_axis=0, tiled=True
    ).reshape(rows, width)
    token_grads = lax.dot_general(
        one_hot_rows(routed * SLOTS + slots, rows), returned, (((0,), (0,)), ((), ())), preferred_element_type=jnp.float32
    ).astype(jnp.bfloat16)

    halves = [merge(f, to_keep, gots[f], dgu, hidden, rows_x, rows_dy) for f in range(4)]
    for step in range(1, 4):
        for f, (first_axis, first_odd) in enumerate(FLOWS):
            axis = first_axis if step < 2 else 1 - first_axis
            odd = first_odd if step % 2 == 0 else not first_odd
            give, keep = halves[f]
            got = lax.ppermute(give, "dp", pair_perm(axis, odd))
            if step == 3:
                halves[f] = (got, keep)
                continue
            n = keep.shape[1] // 2
            halves[f] = tuple(
                (k.astype(jnp.float32) + g.astype(jnp.float32)).astype(jnp.bfloat16)
                for k, g in ((keep[:, :n], got[:, :n]), (keep[:, n:], got[:, n:]))
            )
    grad_gate_up, grad_down_t = finish([h[1] for h in halves], [h[0] for h in halves])
    return (token_grads, grad_gate_up[None], grad_down_t[None])


def solution(mesh):
    return jax.shard_map(
        local,
        mesh=mesh,
        in_specs=(
            P(("dp", "expert"), None),
            P(("dp", "expert"), None),
            P(("dp", "expert"), None),
            P("expert", None, None),
            P("expert", None, None),
        ),
        out_specs=(P(("dp", "expert"), None), P("expert", "dp", None), P("expert", "dp", None)),
        check_vma=False,
    )
```

profile of v0, /device:TPU:2, one launch (start us, length us, event | category | flops | bytes accessed | tf_op | source)
XLA Modules:
  0.0 221.1 jit_solution(16546255926632873622)
XLA Ops:
  0.7 0.9 convert_reduce_fusion
  1.6 0.7 broadcast_select_fusion.1
  2.9 0.4 convolution_convert_fusion
  3.3 0.6 collective-permute-start.8
  4.5 0.6 broadcast_add_fusion
  5.2 0.6 broadcast_add_fusion.4
  5.9 0.6 broadcast_add_fusion.2
  6.8 4.7 %copy.13 = bf16[1,2048,768]{1,2,0:T(8,128)(2,1)} copy(bf16[1,2048,768]{2,1,0:T(8,128)(2,1)} %param.10) | data formatting | bytes 6291456 | tf_op args[4]
  12.0 1.6 fusion.26
  13.6 5.9 %collective-permute-start.7 = (bf16[2,32,2048]{2,1,0:T(8,128)(2,1)S(1)}, bf16[2,32,2048]{2,1,0:T(8,128)(2,1)S(1)}, u32[]{:S(2)}, u32[]{:S(2)}) collective-permute-start(bf16[2,32,2048]{2,1,0:T(8,128)(2,1)S(1)} %get-tuple-element.53), channel_id=1, source_target_pairs={{0,14},{1,15},{2,0},{3,1},{4,2},{5,3},{6,4},{7,5},{8,6},{9,7},{10,... | collective-permute-start | bytes 786440 | tf_op jit(solution)/shard_map/ppermute | solution.py:311
  19.5 0.4 convolution_convert_fusion.1
  20.1 4.3 %collective-permute-start.3 = (bf16[2,32,2048]{2,1,0:T(8,128)(2,1)S(1)}, bf16[2,32,2048]{2,1,0:T(8,128)(2,1)S(1)}, u32[]{:S(2)}, u32[]{:S(2)}) collective-permute-start(bf16[2,32,2048]{2,1,0:T(8,128)(2,1)S(1)} %get-tuple-element.57), channel_id=1, source_target_pairs={{0,6},{1,7},{2,8},{3,9},{4,10},{5,11},{6,12},{7,13},{8,14},{9,15},... | collective-permute-start | bytes 786440 | tf_op jit(solution)/shard_map/ppermute | solution.py:311
  24.4 2.2 %collective-permute-start.4 = (bf16[2,32,2048]{2,1,0:T(8,128)(2,1)S(1)}, bf16[2,32,2048]{2,1,0:T(8,128)(2,1)S(1)}, u32[]{:S(2)}, u32[]{:S(2)}) collective-permute-start(bf16[2,32,2048]{2,1,0:T(8,128)(2,1)S(1)} %get-tuple-element.58), channel_id=1, source_target_pairs={{0,8},{1,9},{2,10},{3,11},{4,12},{5,13},{6,14},{7,15},{8,0},{9,1},... | collective-permute-start | bytes 786440 | tf_op jit(solution)/shard_map/ppermute | solution.py:311
  26.6 3.3 %collective-permute-start.5 = (bf16[2,32,2048]{2,1,0:T(8,128)(2,1)S(1)}, bf16[2,32,2048]{2,1,0:T(8,128)(2,1)S(1)}, u32[]{:S(2)}, u32[]{:S(2)}) collective-permute-start(bf16[2,32,2048]{2,1,0:T(8,128)(2,1)S(1)} %get-tuple-element.59), channel_id=1, source_target_pairs={{0,10},{1,11},{2,12},{3,13},{4,14},{5,15},{6,0},{7,1},{8,2},{9,3},... | collective-permute-start | bytes 786440 | tf_op jit(solution)/shard_map/ppermute | solution.py:311
  29.9 2.2 collective-permute-done.1.refs_1_
  32.1 0.5 collective-permute-start.6
  32.6 1.6 fusion.25
  34.2 10.7 %collective-permute-done.2.refs_2_ = bf16[2,32,2048]{2,1,0:T(8,128)(2,1)S(1)} collective-permute-done((bf16[2,32,2048]{2,1,0:T(8,128)(2,1)S(1)}, bf16[2,32,2048]{2,1,0:T(8,128)(2,1)S(1)}, u32[]{:S(2)}, u32[]{:S(2)}) %collective-permute-start.2) | collective-permute-done | bytes 262176 | tf_op jit(solution)/shard_map/ppermute | solution.py:311
  44.9 2.8 %collective-permute-start.15 = (bf16[2,32,2048]{2,1,0:T(8,128)(2,1)S(1)}, bf16[2,32,2048]{2,1,0:T(8,128)(2,1)S(1)}, u32[]{:S(2)}, u32[]{:S(2)}) collective-permute-start(bf16[2,32,2048]{2,1,0:T(8,128)(2,1)S(1)} %get-tuple-element.45), channel_id=1, source_target_pairs={{0,14},{1,15},{2,0},{3,1},{4,2},{5,3},{6,4},{7,5},{8,6},{9,7},{10,... | collective-permute-start | bytes 786440 | tf_op jit(solution)/shard_map/ppermute | solution.py:311
  47.7 10.7 %collective-permute-done.3.refs_3_ = bf16[2,32,2048]{2,1,0:T(8,128)(2,1)S(1)} collective-permute-done((bf16[2,32,2048]{2,1,0:T(8,128)(2,1)S(1)}, bf16[2,32,2048]{2,1,0:T(8,128)(2,1)S(1)}, u32[]{:S(2)}, u32[]{:S(2)}) %collective-permute-start.3) | collective-permute-done | bytes 262176 | tf_op jit(solution)/shard_map/ppermute | solution.py:311
  58.3 5.6 %collective-permute-start.9 = (bf16[2,32,2048]{2,1,0:T(8,128)(2,1)S(1)}, bf16[2,32,2048]{2,1,0:T(8,128)(2,1)S(1)}, u32[]{:S(2)}, u32[]{:S(2)}) collective-permute-start(bf16[2,32,2048]{2,1,0:T(8,128)(2,1)S(1)} %get-tuple-element.47), channel_id=1, source_target_pairs={{0,2},{1,3},{2,4},{3,5},{4,6},{5,7},{6,8},{7,9},{8,10},{9,11},{10,... | collective-permute-start | bytes 786440 | tf_op jit(solution)/shard_map/ppermute | solution.py:311
  64.0 5.1 %collective-permute-done.4.refs_4_ = bf16[2,32,2048]{2,1,0:T(8,128)(2,1)S(1)} collective-permute-done((bf16[2,32,2048]{2,1,0:T(8,128)(2,1)S(1)}, bf16[2,32,2048]{2,1,0:T(8,128)(2,1)S(1)}, u32[]{:S(2)}, u32[]{:S(2)}) %collective-permute-start.4) | collective-permute-done | bytes 262176 | tf_op jit(solution)/shard_map/ppermute | solution.py:311
  69.1 1.9 collective-permute-start.10
  71.0 2.2 collective-permute-start.11
  73.2 4.3 %collective-permute-start.12 = (bf16[2,32,2048]{2,1,0:T(8,128)(2,1)S(1)}, bf16[2,32,2048]{2,1,0:T(8,128)(2,1)S(1)}, u32[]{:S(2)}, u32[]{:S(2)}) collective-permute-start(bf16[2,32,2048]{2,1,0:T(8,128)(2,1)S(1)} %get-tuple-element.50), channel_id=1, source_target_pairs={{0,8},{1,9},{2,10},{3,11},{4,12},{5,13},{6,14},{7,15},{8,0},{9,1},... | collective-permute-start | bytes 786440 | tf_op jit(solution)/shard_map/ppermute | solution.py:311
  77.5 3.8 %join.1.refs_3_ = bf16[512,2048]{1,0:T(8,128)(2,1)S(1)} custom-call(s32[16]{0:T(128)S(1)} %add.352.places, bf16[2,32,2048]{2,1,0:T(8,128)(2,1)S(1)} %get-tuple-element.54.refs_0_, bf16[2,32,2048]{2,1,0:T(8,128)(2,1)S(1)} %collective-permute-done.1.refs_1_, bf16[2,32,2048]{2,1,0:T(8,128)(2,1)S(1)} %collective-permute-done.2.refs_2_, ...), custom_call_target="tpu_custom_call" | custom-call | flops 1000000 | bytes 100000 | tf_op jit(solution)/shard_map/join/pallas_call | solution.py:80
  81.3 3.5 %fusion.4 = f32[1536,512]{1,0:T(8,128)S(1)} fusion(bf16[512,2048]{1,0:T(8,128)(2,1)S(1)} %join.1.refs_3_, bf16[1,2048,1536]{2,1,0:T(8,128)(2,1)S(1)} %bitcast.88), kind=kOutput, calls=%fused_computation.32 | convolution fusion | flops 3221225472 | bytes 11534336 | tf_op jit(solution)/shard_map/dot_general | solution.py:322
  85.1 2.6 %collective-permute-start.14 = (bf16[2,32,2048]{2,1,0:T(8,128)(2,1)S(1)}, bf16[2,32,2048]{2,1,0:T(8,128)(2,1)S(1)}, u32[]{:S(2)}, u32[]{:S(2)}) collective-permute-start(bf16[2,32,2048]{2,1,0:T(8,128)(2,1)S(1)} %get-tuple-element.52), channel_id=1, source_target_pairs={{0,12},{1,13},{2,14},{3,15},{4,0},{5,1},{6,2},{7,3},{8,4},{9,5},{1... | collective-permute-start | bytes 786440 | tf_op jit(solution)/shard_map/ppermute | solution.py:311
  87.7 0.8 multiply_convert_fusion
  88.5 1.8 collective-permute-done.10.refs_2_
  90.3 25.6 %collective-permute-done.11.refs_3_ = bf16[2,32,2048]{2,1,0:T(8,128)(2,1)S(1)} collective-permute-done((bf16[2,32,2048]{2,1,0:T(8,128)(2,1)S(1)}, bf16[2,32,2048]{2,1,0:T(8,128)(2,1)S(1)}, u32[]{:S(2)}, u32[]{:S(2)}) %collective-permute-start.11) | collective-permute-done | bytes 262176 | tf_op jit(solution)/shard_map/ppermute | solution.py:311
  115.9 7.5 %dgate_up.1 = (bf16[512,2048]{1,0:T(8,128)(2,1)S(1)}, bf16[2,768,512]{2,1,0:T(8,128)(2,1)S(1)}, bf16[576,1024]{1,0:T(8,128)(2,1)S(1)}) custom-call(s32[16]{0:T(128)S(1)} %add.352.places, s32[4,8]{1,0:T(4,128)S(1)} %pad_add_fusion.table.refs_0_, bf16[768,2048]{1,0:T(8,128)(2,1)S(1)} %bitcast.79, f32[768,512]{1,0:T(8,128)S(1)} %get-tuple-element.43.a_ref, ...), custom_call_target="tpu_custom_call" | custom-call | flops 1000000 | bytes 100000 | tf_op jit(solution)/shard_map/dgate_up/pallas_call | solution.py:126
  123.4 1.4 copy-done.5
  124.8 1.0 copy-done.9
  125.8 4.7 %fusion.7 = bf16[512,2048]{1,0:T(8,128)(2,1)} fusion(bf16[1536,512]{1,0:T(8,128)(2,1)S(1)} %bitcast.74, bf16[1,2048,1536]{2,1,0:T(8,128)(2,1)S(1)} %bitcast.88), kind=kOutput, calls=%fused_computation.33 | convolution fusion | flops 3222274048 | bytes 9961472 | tf_op jit(solution)/shard_map/dot_general | solution.py:344
  130.6 4.9 %all-to-all-start = ((bf16[16,32,2048]{2,1,0:T(8,128)(2,1)}), bf16[16,32,2048]{2,1,0:T(8,128)(2,1)}, u32[]{:S(2)}, u32[]{:S(2)}) async-start(bf16[16,32,2048]{2,1,0:T(8,128)(2,1)} %bitcast.82), calls=%async_computation | async-start | bytes 4194304 | tf_op jit(solution)/shard_map/all_to_all | solution.py:347
  135.4 3.1 %collective-permute-start.25 = (bf16[576,1024]{1,0:T(8,128)(2,1)}, bf16[576,1024]{1,0:T(8,128)(2,1)}, u32[]{:S(2)}, u32[]{:S(2)}) collective-permute-start(bf16[576,1024]{1,0:T(8,128)(2,1)} %copy-done.9), channel_id=1, source_target_pairs={{0,48},{16,32},{32,16},{48,0},{64,112},{80,96},{96,80},{112,64},{1... | collective-permute-start | bytes 3538952 | tf_op jit(solution)/shard_map/ppermute | solution.py:343
  138.5 1.4 copy-done.3
  139.9 1.6 copy-done.6
  141.5 5.8 %give.1 = (bf16[576,1024]{1,0:T(8,128)(2,1)}, bf16[576,1024]{1,0:T(8,128)(2,1)}, bf16[576,1024]{1,0:T(8,128)(2,1)}) custom-call(s32[4,8]{1,0:T(4,128)S(1)} %pad_add_fusion.table.refs_0_, bf16[1536,512]{1,0:T(8,128)(2,1)S(1)} %bitcast.75, bf16[768,512]{1,0:T(8,128)(2,1)S(1)} %get-tuple-element.42.hid_ref.refs_2_.refs_4_, bf16[512,2048]{1,0:T(8,128)(2,1)S(1)} %join.1.refs_3_, ...), custom_call_target="tpu_custom_call" | custom-call | flops 1000000 | bytes 100000 | tf_op jit(solution)/shard_map/give/pallas_call | solution.py:173
  147.3 0.6 collective-permute-start.16
  147.9 2.2 collective-permute-start.19
  150.5 14.7 %collective-permute-done.25.refs_1_ = bf16[576,1024]{1,0:T(8,128)(2,1)} collective-permute-done((bf16[576,1024]{1,0:T(8,128)(2,1)}, bf16[576,1024]{1,0:T(8,128)(2,1)}, u32[]{:S(2)}, u32[]{:S(2)}) %collective-permute-start.25) | collective-permute-done | bytes 1179680 | tf_op jit(solution)/shard_map/ppermute | solution.py:343
  165.2 1.6 copy-done.7
  166.8 2.7 %merge.7 = (bf16[576,512]{1,0:T(8,128)(2,1)S(1)}, bf16[576,512]{1,0:T(8,128)(2,1)S(1)}) custom-call(s32[4,8]{1,0:T(4,128)S(1)} %pad_add_fusion.1.refs_0_, bf16[576,1024]{1,0:T(8,128)(2,1)} %collective-permute-done.25.refs_1_, bf16[768,512]{1,0:T(8,128)(2,1)S(1)} %get-tuple-element.42.hid_ref.refs_2_.refs_4_, bf16[512,2048]{1,0:T(8,128)(2,1)S(1)} %copy-done.7), custom_call_target="tpu_custom_call" | custom-call | flops 1000000 | bytes 100000 | tf_op jit(solution)/shard_map/merge/pallas_call | solution.py:211
  169.9 5.6 %collective-permute-done.16.refs_1_ = bf16[576,1024]{1,0:T(8,128)(2,1)} collective-permute-done((bf16[576,1024]{1,0:T(8,128)(2,1)}, bf16[576,1024]{1,0:T(8,128)(2,1)}, u32[]{:S(2)}, u32[]{:S(2)}) %collective-permute-start.16) | collective-permute-done | bytes 1179680 | tf_op jit(solution)/shard_map/ppermute | solution.py:343
  175.5 2.7 %merge.4 = (bf16[576,512]{1,0:T(8,128)(2,1)S(1)}, bf16[576,512]{1,0:T(8,128)(2,1)S(1)}) custom-call(s32[4,8]{1,0:T(4,128)S(1)} %pad_add_fusion.1.refs_0_, bf16[576,1024]{1,0:T(8,128)(2,1)} %collective-permute-done.16.refs_1_, bf16[1536,512]{1,0:T(8,128)(2,1)S(1)} %bitcast.76, bf16[512,2048]{1,0:T(8,128)(2,1)S(1)} %join.1.refs_3_), custom_call_target="tpu_custom_call" | custom-call | flops 1000000 | bytes 100000 | tf_op jit(solution)/shard_map/merge/pallas_call | solution.py:211
  178.3 1.6 collective-permute-start.17
  179.9 2.7 %merge.5 = (bf16[576,512]{1,0:T(8,128)(2,1)S(1)}, bf16[576,512]{1,0:T(8,128)(2,1)S(1)}) custom-call(s32[4,8]{1,0:T(4,128)S(1)} %pad_add_fusion.1.refs_0_, bf16[576,1024]{1,0:T(8,128)(2,1)} %collective-permute-done.19.refs_1_, bf16[1536,512]{1,0:T(8,128)(2,1)S(1)} %bitcast.77, bf16[512,2048]{1,0:T(8,128)(2,1)S(1)} %join.1.refs_3_), custom_call_target="tpu_custom_call" | custom-call | flops 1000000 | bytes 100000 | tf_op jit(solution)/shard_map/merge/pallas_call | solution.py:211
  182.6 1.9 collective-permute-start.20
  184.5 2.8 %merge.6 = (bf16[576,512]{1,0:T(8,128)(2,1)S(1)}, bf16[576,512]{1,0:T(8,128)(2,1)S(1)}) custom-call(s32[4,8]{1,0:T(4,128)S(1)} %pad_add_fusion.1.refs_0_, bf16[576,1024]{1,0:T(8,128)(2,1)} %collective-permute-done.22.refs_1_, bf16[1536,512]{1,0:T(8,128)(2,1)S(1)} %bitcast.78, bf16[512,2048]{1,0:T(8,128)(2,1)S(1)} %join.1.refs_3_, ...), custom_call_target="tpu_custom_call" | custom-call | flops 1000000 | bytes 100000 | tf_op jit(solution)/shard_map/merge/pallas_call | solution.py:211
  187.6 2.6 %collective-permute-done.26 = bf16[576,512]{1,0:T(8,128)(2,1)S(1)} collective-permute-done((bf16[576,512]{1,0:T(8,128)(2,1)S(1)}, bf16[576,512]{1,0:T(8,128)(2,1)S(1)}, u32[]{:S(2)}, u32[]{:S(2)}) %collective-permute-start.26) | collective-permute-done | bytes 589856 | tf_op jit(solution)/shard_map/ppermute | solution.py:360
  190.7 3.1 %collective-permute-done.17 = bf16[576,512]{1,0:T(8,128)(2,1)S(1)} collective-permute-done((bf16[576,512]{1,0:T(8,128)(2,1)S(1)}, bf16[576,512]{1,0:T(8,128)(2,1)S(1)}, u32[]{:S(2)}, u32[]{:S(2)}) %collective-permute-start.17) | collective-permute-done | bytes 589856 | tf_op jit(solution)/shard_map/ppermute | solution.py:360
  194.1 2.7 %collective-permute-done.20 = bf16[576,512]{1,0:T(8,128)(2,1)S(1)} collective-permute-done((bf16[576,512]{1,0:T(8,128)(2,1)S(1)}, bf16[576,512]{1,0:T(8,128)(2,1)S(1)}, u32[]{:S(2)}, u32[]{:S(2)}) %collective-permute-start.20) | collective-permute-done | bytes 589856 | tf_op jit(solution)/shard_map/ppermute | solution.py:360
  197.0 0.4 collective-permute-start.21
  197.4 7.4 %collective-permute-done.23 = bf16[576,512]{1,0:T(8,128)(2,1)S(1)} collective-permute-done((bf16[576,512]{1,0:T(8,128)(2,1)S(1)}, bf16[576,512]{1,0:T(8,128)(2,1)S(1)}, u32[]{:S(2)}, u32[]{:S(2)}) %collective-permute-start.23) | collective-permute-done | bytes 589856 | tf_op jit(solution)/shard_map/ppermute | solution.py:360
  205.2 2.1 collective-permute-start.31
  207.7 2.6 %collective-permute-done.21 = bf16[576,256]{1,0:T(8,128)(2,1)S(1)} collective-permute-done((bf16[576,256]{1,0:T(8,128)(2,1)S(1)}, bf16[576,256]{1,0:T(8,128)(2,1)S(1)}, u32[]{:S(2)}, u32[]{:S(2)}) %collective-permute-start.21) | collective-permute-done | bytes 294944 | tf_op jit(solution)/shard_map/ppermute | solution.py:360
  210.5 1.3 collective-permute-done.24
  212.0 1.4 collective-permute-done.31.refs_7_
  213.8 1.8 collective-permute-done.29.refs_5_
  215.6 1.5 collective-permute-done.30.refs_6_
  217.1 1.0 finish.1
  218.1 3.0 %convolution_convert_fusion.4 = bf16[160,2048]{1,0:T(8,128)(2,1)} fusion(bf16[512,2048]{1,0:T(8,128)(2,1)} %bitcast.39, s32[160]{0:T(256)S(1)} %get-tuple-element.77), kind=kOutput, calls=%fused_computation.38 | convolution fusion | flops 335953920 | bytes 2753152 | tf_op jit(solution)/shard_map/dot_general | solution.py:350
  (89 shorter events, 6.1 us)
Async XLA Ops:
  0.6 1.7 copy-start
  0.6 2.2 copy-start.10
  2.7 9.2 %collective-permute-start = (bf16[8,32,2048]{2,1,0:T(8,128)(2,1)S(1)}, bf16[8,32,2048]{2,1,0:T(8,128)(2,1)}, u32[]{:S(2)}, u32[]{:S(2)}) collective-permute-start(bf16[8,32,2048]{2,1,0:T(8,128)(2,1)S(1)} %bitcast.84), channel_id=1, source_target_pairs={{0,1},{1,0},{2,3},{3,2},{4,5},{5,4},{6,7},{7,6},{8,9},{9,8},{10,11... | collective-permute-start | bytes 3145736 | tf_op jit(solution)/shard_map/ppermute | solution.py:307
  3.3 21.1 %collective-permute-start.8 = (bf16[8,32,2048]{2,1,0:T(8,128)(2,1)S(1)}, bf16[8,32,2048]{2,1,0:T(8,128)(2,1)}, u32[]{:S(2)}, u32[]{:S(2)}) collective-permute-start(bf16[8,32,2048]{2,1,0:T(8,128)(2,1)S(1)} %bitcast.83), channel_id=1, source_target_pairs={{0,1},{1,0},{2,3},{3,2},{4,5},{5,4},{6,7},{7,6},{8,9},{9,8},{10,11... | collective-permute-start | bytes 3145736 | tf_op jit(solution)/shard_map/ppermute | solution.py:307
  12.0 69.3 %slice-start = ((s8[6291456]{0:T(1024)(128)(4,1)}), s8[4194304]{0:T(1024)(128)(4,1)S(1)}, s32[]{:S(2)}) async-start(s8[6291456]{0:T(1024)(128)(4,1)} %bitcast.87), calls=%async_computation.1 | async-start | bytes 8388608
  13.6 13.1 %collective-permute-start.7 = (bf16[2,32,2048]{2,1,0:T(8,128)(2,1)S(1)}, bf16[2,32,2048]{2,1,0:T(8,128)(2,1)S(1)}, u32[]{:S(2)}, u32[]{:S(2)}) collective-permute-start(bf16[2,32,2048]{2,1,0:T(8,128)(2,1)S(1)} %get-tuple-element.53), channel_id=1, source_target_pairs={{0,14},{1,15},{2,0},{3,1},{4,2},{5,3},{6,4},{7,5},{8,6},{9,7},{10,... | collective-permute-start | bytes 786440 | tf_op jit(solution)/shard_map/ppermute | solution.py:311
  19.5 12.6 %collective-permute-start.1 = (bf16[2,32,2048]{2,1,0:T(8,128)(2,1)S(1)}, bf16[2,32,2048]{2,1,0:T(8,128)(2,1)S(1)}, u32[]{:S(2)}, u32[]{:S(2)}) collective-permute-start(bf16[2,32,2048]{2,1,0:T(8,128)(2,1)S(1)} %get-tuple-element.55), channel_id=1, source_target_pairs={{0,2},{1,3},{2,4},{3,5},{4,6},{5,7},{6,8},{7,9},{8,10},{9,11},{10,... | collective-permute-start | bytes 786440 | tf_op jit(solution)/shard_map/ppermute | solution.py:311
  20.0 24.9 %collective-permute-start.2 = (bf16[2,32,2048]{2,1,0:T(8,128)(2,1)S(1)}, bf16[2,32,2048]{2,1,0:T(8,128)(2,1)S(1)}, u32[]{:S(2)}, u32[]{:S(2)}) collective-permute-start(bf16[2,32,2048]{2,1,0:T(8,128)(2,1)S(1)} %get-tuple-element.56), channel_id=1, source_target_pairs={{0,4},{1,5},{2,6},{3,7},{4,8},{5,9},{6,10},{7,11},{8,12},{9,13},{1... | collective-permute-start | bytes 786440 | tf_op jit(solution)/shard_map/ppermute | solution.py:311
  20.1 38.3 %collective-permute-start.3 = (bf16[2,32,2048]{2,1,0:T(8,128)(2,1)S(1)}, bf16[2,32,2048]{2,1,0:T(8,128)(2,1)S(1)}, u32[]{:S(2)}, u32[]{:S(2)}) collective-permute-start(bf16[2,32,2048]{2,1,0:T(8,128)(2,1)S(1)} %get-tuple-element.57), channel_id=1, source_target_pairs={{0,6},{1,7},{2,8},{3,9},{4,10},{5,11},{6,12},{7,13},{8,14},{9,15},... | collective-permute-start | bytes 786440 | tf_op jit(solution)/shard_map/ppermute | solution.py:311
  24.4 44.7 %collective-permute-start.4 = (bf16[2,32,2048]{2,1,0:T(8,128)(2,1)S(1)}, bf16[2,32,2048]{2,1,0:T(8,128)(2,1)S(1)}, u32[]{:S(2)}, u32[]{:S(2)}) collective-permute-start(bf16[2,32,2048]{2,1,0:T(8,128)(2,1)S(1)} %get-tuple-element.58), channel_id=1, source_target_pairs={{0,8},{1,9},{2,10},{3,11},{4,12},{5,13},{6,14},{7,15},{8,0},{9,1},... | collective-permute-start | bytes 786440 | tf_op jit(solution)/shard_map/ppermute | solution.py:311
  26.6 44.3 %collective-permute-start.5 = (bf16[2,32,2048]{2,1,0:T(8,128)(2,1)S(1)}, bf16[2,32,2048]{2,1,0:T(8,128)(2,1)S(1)}, u32[]{:S(2)}, u32[]{:S(2)}) collective-permute-start(bf16[2,32,2048]{2,1,0:T(8,128)(2,1)S(1)} %get-tuple-element.59), channel_id=1, source_target_pairs={{0,10},{1,11},{2,12},{3,13},{4,14},{5,15},{6,0},{7,1},{8,2},{9,3},... | collective-permute-start | bytes 786440 | tf_op jit(solution)/shard_map/ppermute | solution.py:311
  32.1 41.0 %collective-permute-start.6 = (bf16[2,32,2048]{2,1,0:T(8,128)(2,1)S(1)}, bf16[2,32,2048]{2,1,0:T(8,128)(2,1)S(1)}, u32[]{:S(2)}, u32[]{:S(2)}) collective-permute-start(bf16[2,32,2048]{2,1,0:T(8,128)(2,1)S(1)} %get-tuple-element.60), channel_id=1, source_target_pairs={{0,12},{1,13},{2,14},{3,15},{4,0},{5,1},{6,2},{7,3},{8,4},{9,5},{1... | collective-permute-start | bytes 786440 | tf_op jit(solution)/shard_map/ppermute | solution.py:311
  32.6 48.7 %slice-start.1 = ((s8[6291456]{0:T(1024)(128)(4,1)}), s8[2097152]{0:T(1024)(128)(4,1)S(1)}, s32[]{:S(2)}) async-start(s8[6291456]{0:T(1024)(128)(4,1)} %bitcast.87), calls=%async_computation.2 | async-start | bytes 4194304
  44.9 39.9 %collective-permute-start.15 = (bf16[2,32,2048]{2,1,0:T(8,128)(2,1)S(1)}, bf16[2,32,2048]{2,1,0:T(8,128)(2,1)S(1)}, u32[]{:S(2)}, u32[]{:S(2)}) collective-permute-start(bf16[2,32,2048]{2,1,0:T(8,128)(2,1)S(1)} %get-tuple-element.45), channel_id=1, source_target_pairs={{0,14},{1,15},{2,0},{3,1},{4,2},{5,3},{6,4},{7,5},{8,6},{9,7},{10,... | collective-permute-start | bytes 786440 | tf_op jit(solution)/shard_map/ppermute | solution.py:311
  58.3 26.7 %collective-permute-start.9 = (bf16[2,32,2048]{2,1,0:T(8,128)(2,1)S(1)}, bf16[2,32,2048]{2,1,0:T(8,128)(2,1)S(1)}, u32[]{:S(2)}, u32[]{:S(2)}) collective-permute-start(bf16[2,32,2048]{2,1,0:T(8,128)(2,1)S(1)} %get-tuple-element.47), channel_id=1, source_target_pairs={{0,2},{1,3},{2,4},{3,5},{4,6},{5,7},{6,8},{7,9},{8,10},{9,11},{10,... | collective-permute-start | bytes 786440 | tf_op jit(solution)/shard_map/ppermute | solution.py:311
  69.1 21.2 %collective-permute-start.10 = (bf16[2,32,2048]{2,1,0:T(8,128)(2,1)S(1)}, bf16[2,32,2048]{2,1,0:T(8,128)(2,1)S(1)}, u32[]{:S(2)}, u32[]{:S(2)}) collective-permute-start(bf16[2,32,2048]{2,1,0:T(8,128)(2,1)S(1)} %get-tuple-element.48), channel_id=1, source_target_pairs={{0,4},{1,5},{2,6},{3,7},{4,8},{5,9},{6,10},{7,11},{8,12},{9,13},{1... | collective-permute-start | bytes 786440 | tf_op jit(solution)/shard_map/ppermute | solution.py:311
  71.0 44.9 %collective-permute-start.11 = (bf16[2,32,2048]{2,1,0:T(8,128)(2,1)S(1)}, bf16[2,32,2048]{2,1,0:T(8,128)(2,1)S(1)}, u32[]{:S(2)}, u32[]{:S(2)}) collective-permute-start(bf16[2,32,2048]{2,1,0:T(8,128)(2,1)S(1)} %get-tuple-element.49), channel_id=1, source_target_pairs={{0,6},{1,7},{2,8},{3,9},{4,10},{5,11},{6,12},{7,13},{8,14},{9,15},... | collective-permute-start | bytes 786440 | tf_op jit(solution)/shard_map/ppermute | solution.py:311
  73.2 42.7 %collective-permute-start.12 = (bf16[2,32,2048]{2,1,0:T(8,128)(2,1)S(1)}, bf16[2,32,2048]{2,1,0:T(8,128)(2,1)S(1)}, u32[]{:S(2)}, u32[]{:S(2)}) collective-permute-start(bf16[2,32,2048]{2,1,0:T(8,128)(2,1)S(1)} %get-tuple-element.50), channel_id=1, source_target_pairs={{0,8},{1,9},{2,10},{3,11},{4,12},{5,13},{6,14},{7,15},{8,0},{9,1},... | collective-permute-start | bytes 786440 | tf_op jit(solution)/shard_map/ppermute | solution.py:311
  84.8 31.1 %collective-permute-start.13 = (bf16[2,32,2048]{2,1,0:T(8,128)(2,1)S(1)}, bf16[2,32,2048]{2,1,0:T(8,128)(2,1)S(1)}, u32[]{:S(2)}, u32[]{:S(2)}) collective-permute-start(bf16[2,32,2048]{2,1,0:T(8,128)(2,1)S(1)} %get-tuple-element.51), channel_id=1, source_target_pairs={{0,10},{1,11},{2,12},{3,13},{4,14},{5,15},{6,0},{7,1},{8,2},{9,3},... | collective-permute-start | bytes 786440 | tf_op jit(solution)/shard_map/ppermute | solution.py:311
  85.1 30.8 %copy-start.8 = (bf16[1,2048,768]{1,2,0:T(8,128)(2,1)S(1)}, bf16[1,2048,768]{1,2,0:T(8,128)(2,1)}, u32[]{:S(2)}) copy-start(bf16[1,2048,768]{1,2,0:T(8,128)(2,1)} %copy.13) | copy-start | bytes 9437188
  85.1 30.8 %collective-permute-start.14 = (bf16[2,32,2048]{2,1,0:T(8,128)(2,1)S(1)}, bf16[2,32,2048]{2,1,0:T(8,128)(2,1)S(1)}, u32[]{:S(2)}, u32[]{:S(2)}) collective-permute-start(bf16[2,32,2048]{2,1,0:T(8,128)(2,1)S(1)} %get-tuple-element.52), channel_id=1, source_target_pairs={{0,12},{1,13},{2,14},{3,15},{4,0},{5,1},{6,2},{7,3},{8,4},{9,5},{1... | collective-permute-start | bytes 786440 | tf_op jit(solution)/shard_map/ppermute | solution.py:311
  123.4 1.4 copy-start.5
  124.8 1.0 copy-start.9
  125.8 4.7 %copy-start.2 = (bf16[2,768,512]{2,1,0:T(8,128)(2,1)}, bf16[2,768,512]{2,1,0:T(8,128)(2,1)S(1)}, u32[]{:S(2)}) copy-start(bf16[2,768,512]{2,1,0:T(8,128)(2,1)S(1)} %get-tuple-element.23) | copy-start | bytes 4718596
  130.6 87.5 %all-to-all-start = ((bf16[16,32,2048]{2,1,0:T(8,128)(2,1)}), bf16[16,32,2048]{2,1,0:T(8,128)(2,1)}, u32[]{:S(2)}, u32[]{:S(2)}) async-start(bf16[16,32,2048]{2,1,0:T(8,128)(2,1)} %bitcast.82), calls=%async_computation | async-start | bytes 4194304 | tf_op jit(solution)/shard_map/all_to_all | solution.py:347
  135.4 29.8 %collective-permute-start.25 = (bf16[576,1024]{1,0:T(8,128)(2,1)}, bf16[576,1024]{1,0:T(8,128)(2,1)}, u32[]{:S(2)}, u32[]{:S(2)}) collective-permute-start(bf16[576,1024]{1,0:T(8,128)(2,1)} %copy-done.9), channel_id=1, source_target_pairs={{0,48},{16,32},{32,16},{48,0},{64,112},{80,96},{96,80},{112,64},{1... | collective-permute-start | bytes 3538952 | tf_op jit(solution)/shard_map/ppermute | solution.py:343
  138.5 1.4 copy-start.3
  139.9 1.6 copy-start.6
  141.5 8.8 %copy-start.11 = (s32[2,4]{1,0:T(2,128)S(1)}, s32[2,4]{1,0:T(2,128)}, u32[]{:S(2)}) copy-start(s32[2,4]{1,0:T(2,128)} %get-tuple-element.84) | copy-start | bytes 100
  141.5 8.8 %copy-start.12 = (s32[2,4]{1,0:T(2,128)S(1)}, s32[2,4]{1,0:T(2,128)}, u32[]{:S(2)}) copy-start(s32[2,4]{1,0:T(2,128)} %get-tuple-element.80) | copy-start | bytes 100
  141.5 8.9 %copy-start.13 = (s32[2,4]{1,0:T(2,128)S(1)}, s32[2,4]{1,0:T(2,128)}, u32[]{:S(2)}) copy-start(s32[2,4]{1,0:T(2,128)} %get-tuple-element.82) | copy-start | bytes 100
  147.3 28.3 %collective-permute-start.16 = (bf16[576,1024]{1,0:T(8,128)(2,1)}, bf16[576,1024]{1,0:T(8,128)(2,1)}, u32[]{:S(2)}, u32[]{:S(2)}) collective-permute-start(bf16[576,1024]{1,0:T(8,128)(2,1)} %get-tuple-element.25), channel_id=1, source_target_pairs={{0,64},{16,80},{32,96},{48,112},{64,0},{80,16},{96,32},{112,48},{1... | collective-permute-start | bytes 3538952 | tf_op jit(solution)/shard_map/ppermute | solution.py:343
  147.9 32.0 %collective-permute-start.19 = (bf16[576,1024]{1,0:T(8,128)(2,1)}, bf16[576,1024]{1,0:T(8,128)(2,1)}, u32[]{:S(2)}, u32[]{:S(2)}) collective-permute-start(bf16[576,1024]{1,0:T(8,128)(2,1)} %get-tuple-element.28), channel_id=1, source_target_pairs={{0,192},{16,208},{32,224},{48,240},{64,128},{80,144},{96,160},{112... | collective-permute-start | bytes 3538952 | tf_op jit(solution)/shard_map/ppermute | solution.py:343
  150.1 34.4 %collective-permute-start.22 = (bf16[576,1024]{1,0:T(8,128)(2,1)}, bf16[576,1024]{1,0:T(8,128)(2,1)}, u32[]{:S(2)}, u32[]{:S(2)}) collective-permute-start(bf16[576,1024]{1,0:T(8,128)(2,1)} %get-tuple-element.31), channel_id=1, source_target_pairs={{0,16},{16,0},{32,48},{48,32},{64,80},{80,64},{96,112},{112,96},{1... | collective-permute-start | bytes 3538952 | tf_op jit(solution)/shard_map/ppermute | solution.py:343
  150.5 25.0 %copy-start.4 = (bf16[2,768,512]{2,1,0:T(8,128)(2,1)S(1)}, bf16[2,768,512]{2,1,0:T(8,128)(2,1)}, u32[]{:S(2)}) copy-start(bf16[2,768,512]{2,1,0:T(8,128)(2,1)} %copy-done.2) | copy-start | bytes 4718596
  165.2 1.6 copy-start.7
  169.5 20.7 %collective-permute-start.26 = (bf16[576,512]{1,0:T(8,128)(2,1)S(1)}, bf16[576,512]{1,0:T(8,128)(2,1)S(1)}, u32[]{:S(2)}, u32[]{:S(2)}) collective-permute-start(bf16[576,512]{1,0:T(8,128)(2,1)S(1)} %get-tuple-element.36), channel_id=1, source_target_pairs={{0,16},{16,0},{32,48},{48,32},{64,80},{80,64},{96,112},{112,96},{1... | collective-permute-start | bytes 1769480 | tf_op jit(solution)/shard_map/ppermute | solution.py:360
  178.3 15.6 %collective-permute-start.17 = (bf16[576,512]{1,0:T(8,128)(2,1)S(1)}, bf16[576,512]{1,0:T(8,128)(2,1)S(1)}, u32[]{:S(2)}, u32[]{:S(2)}) collective-permute-start(bf16[576,512]{1,0:T(8,128)(2,1)S(1)} %get-tuple-element.27), channel_id=1, source_target_pairs={{0,192},{16,208},{32,224},{48,240},{64,128},{80,144},{96,160},{112... | collective-permute-start | bytes 1769480 | tf_op jit(solution)/shard_map/ppermute | solution.py:360
  182.6 14.2 %collective-permute-start.20 = (bf16[576,512]{1,0:T(8,128)(2,1)S(1)}, bf16[576,512]{1,0:T(8,128)(2,1)S(1)}, u32[]{:S(2)}, u32[]{:S(2)}) collective-permute-start(bf16[576,512]{1,0:T(8,128)(2,1)S(1)} %get-tuple-element.30), channel_id=1, source_target_pairs={{0,64},{16,80},{32,96},{48,112},{64,0},{80,16},{96,32},{112,48},{1... | collective-permute-start | bytes 1769480 | tf_op jit(solution)/shard_map/ppermute | solution.py:360
  187.3 17.6 %collective-permute-start.23 = (bf16[576,512]{1,0:T(8,128)(2,1)S(1)}, bf16[576,512]{1,0:T(8,128)(2,1)S(1)}, u32[]{:S(2)}, u32[]{:S(2)}) collective-permute-start(bf16[576,512]{1,0:T(8,128)(2,1)S(1)} %get-tuple-element.33), channel_id=1, source_target_pairs={{0,48},{16,32},{32,16},{48,0},{64,112},{80,96},{96,80},{112,64},{1... | collective-permute-start | bytes 1769480 | tf_op jit(solution)/shard_map/ppermute | solution.py:360
  190.4 14.7 %collective-permute-start.27 = (bf16[576,256]{1,0:T(8,128)(2,1)S(1)}, bf16[576,256]{1,0:T(8,128)(2,1)S(1)}, u32[]{:S(2)}, u32[]{:S(2)}) collective-permute-start(bf16[576,256]{1,0:T(8,128)(2,1)S(1)} %get-tuple-element.62), channel_id=1, source_target_pairs={{0,192},{16,208},{32,224},{48,240},{64,128},{80,144},{96,160},{112... | collective-permute-start | bytes 884744 | tf_op jit(solution)/shard_map/ppermute | solution.py:360
  194.0 13.2 %collective-permute-start.18 = (bf16[576,256]{1,0:T(8,128)(2,1)S(1)}, bf16[576,256]{1,0:T(8,128)(2,1)S(1)}, u32[]{:S(2)}, u32[]{:S(2)}) collective-permute-start(bf16[576,256]{1,0:T(8,128)(2,1)S(1)} %get-tuple-element.68), channel_id=1, source_target_pairs={{0,16},{16,0},{32,48},{48,32},{64,80},{80,64},{96,112},{112,96},{1... | collective-permute-start | bytes 884744 | tf_op jit(solution)/shard_map/ppermute | solution.py:360
  197.0 13.3 %collective-permute-start.21 = (bf16[576,256]{1,0:T(8,128)(2,1)S(1)}, bf16[576,256]{1,0:T(8,128)(2,1)S(1)}, u32[]{:S(2)}, u32[]{:S(2)}) collective-permute-start(bf16[576,256]{1,0:T(8,128)(2,1)S(1)} %get-tuple-element.66), channel_id=1, source_target_pairs={{0,48},{16,32},{32,16},{48,0},{64,112},{80,96},{96,80},{112,64},{1... | collective-permute-start | bytes 884744 | tf_op jit(solution)/shard_map/ppermute | solution.py:360
  205.0 6.8 %collective-permute-start.24 = (bf16[576,256]{1,0:T(8,128)(2,1)S(1)}, bf16[576,256]{1,0:T(8,128)(2,1)S(1)}, u32[]{:S(2)}, u32[]{:S(2)}) collective-permute-start(bf16[576,256]{1,0:T(8,128)(2,1)S(1)} %get-tuple-element.64), channel_id=1, source_target_pairs={{0,64},{16,80},{32,96},{48,112},{64,0},{80,16},{96,32},{112,48},{1... | collective-permute-start | bytes 884744 | tf_op jit(solution)/shard_map/ppermute | solution.py:360
  205.2 8.2 %collective-permute-start.31 = (bf16[576,128]{1,0:T(8,128)(2,1)S(1)}, bf16[576,128]{1,0:T(8,128)(2,1)S(1)}, u32[]{:S(2)}, u32[]{:S(2)}) collective-permute-start(bf16[576,128]{1,0:T(8,128)(2,1)S(1)} %get-tuple-element.69), channel_id=1, source_target_pairs={{0,64},{16,80},{32,96},{48,112},{64,0},{80,16},{96,32},{112,48},{1... | collective-permute-start | bytes 442376 | tf_op jit(solution)/shard_map/ppermute | solution.py:360
  207.3 6.4 %collective-permute-start.28 = (bf16[576,128]{1,0:T(8,128)(2,1)S(1)}, bf16[576,128]{1,0:T(8,128)(2,1)S(1)}, u32[]{:S(2)}, u32[]{:S(2)}) collective-permute-start(bf16[576,128]{1,0:T(8,128)(2,1)S(1)} %get-tuple-element.75), channel_id=1, source_target_pairs={{0,48},{16,32},{32,16},{48,0},{64,112},{80,96},{96,80},{112,64},{1... | collective-permute-start | bytes 442376 | tf_op jit(solution)/shard_map/ppermute | solution.py:360
  210.4 5.2 %collective-permute-start.29 = (bf16[576,128]{1,0:T(8,128)(2,1)S(1)}, bf16[576,128]{1,0:T(8,128)(2,1)S(1)}, u32[]{:S(2)}, u32[]{:S(2)}) collective-permute-start(bf16[576,128]{1,0:T(8,128)(2,1)S(1)} %get-tuple-element.73), channel_id=1, source_target_pairs={{0,16},{16,0},{32,48},{48,32},{64,80},{80,64},{96,112},{112,96},{1... | collective-permute-start | bytes 442376 | tf_op jit(solution)/shard_map/ppermute | solution.py:360
  211.8 9.3 %copy-start.1 = (bf16[160,2048]{1,0:T(8,128)(2,1)S(1)}, bf16[160,2048]{1,0:T(8,128)(2,1)}, u32[]{:S(2)}) copy-start(bf16[160,2048]{1,0:T(8,128)(2,1)} %param.6) | copy-start | bytes 1966084
  211.9 5.2 %collective-permute-start.30 = (bf16[576,128]{1,0:T(8,128)(2,1)S(1)}, bf16[576,128]{1,0:T(8,128)(2,1)S(1)}, u32[]{:S(2)}, u32[]{:S(2)}) collective-permute-start(bf16[576,128]{1,0:T(8,128)(2,1)S(1)} %get-tuple-element.71), channel_id=1, source_target_pairs={{0,192},{16,208},{32,224},{48,240},{64,128},{80,144},{96,160},{112... | collective-permute-start | bytes 442376 | tf_op jit(solution)/shard_map/ppermute | solution.py:360
where the time goes:
time: 222 us; the launch traced here: 221 us
  waiting for transfers between devices  101 us (45%)
  starting transfers between devices  55.3 us (25%)
  Pallas kernels  29 us (13%)
  matrix products  12.9 us (6%)
  local copies, waits for them, and re-layouts  12.5 us (6%)
  other arithmetic  9.11 us (4%)
    ppermute x14, waiting for transfers between devices, send(): lax.ppermute(both[d], 'expert', [(i, (i + 2 * d) % num_experts) for i in...  56.1 us
    ppermute x14, starting transfers between devices, send(): lax.ppermute(both[d], 'expert', [(i, (i + 2 * d) % num_experts) for i in...  36 us
    ppermute x12, waiting for transfers between devices, local(): got = lax.ppermute(give, 'dp', pair_perm(axis, odd))  24.9 us
    ppermute x4, waiting for transfers between devices, local(): gots[f] = lax.ppermute(gives[f], 'dp', pair_perm(*FLOWS[f]))  20.3 us
    unnamed x33, local copies, waits for them, and re-layouts  11.7 us
    pallas_call x4, Pallas kernels, merge(): pl.pallas_call(lambda *refs: merge_kernel(f, *refs), in_specs=[pl.BlockSp...  10.9 us
    ppermute x12, starting transfers between devices, local(): got = lax.ppermute(give, 'dp', pair_perm(axis, odd))  7.86 us
    pallas_call x1, Pallas kernels, make_dgate_up(): pl.pallas_call(dgate_up_kernel, in_specs=[small] * 2 + [whole] * 4 + [pl....  7.49 us
  transfers between devices with their start and end apart: 33, of which 18 were waited for; matrix products, arithmetic and copies ran while one was open for 8% of the time, Pallas kernels for 10%

commit v1 on v0

--- a/solution.py
+++ b/solution.py
@@ -9,6 +9,8 @@
 SIDE = 4
 LANE = 128
 CHUNKS = 4
+FLOWS = ((0, False), (0, True), (1, False), (1, True))
+LARGE = pl.CostEstimate(flops=20000000000, bytes_accessed=10000000, transcendentals=0)
 SMALL = pl.CostEstimate(flops=1000000, bytes_accessed=100000, transcendentals=0)
 
 
@@ -54,133 +56,98 @@
     return parts
 
 
-def join_copies(places, pieces, to_ref, sems):
+def join_kernel(order, places, *refs):
+    pieces, outs, sems = refs[: len(order)], refs[len(order) : -1], refs[-1]
     copies = []
-    for d, piece in enumerate(pieces):
+    for d, piece in zip(order, pieces):
         for k in range(2):
             row = pl.multiple_of(places[2 * d + k] * SLOTS, SLOTS)
-            copies.append(
-                pltpu.make_async_copy(piece.at[k], to_ref.at[pl.ds(row, SLOTS)], sems.at[2 * d + k])
-            )
-    return copies
-
-
-def join_kernel(places, *refs):
-    *pieces, out_ref, sems = refs
-    copies = join_copies(places, pieces, out_ref, sems)
+            for n, out in enumerate(outs):
+                copies.append(
+                    pltpu.make_async_copy(piece.at[n, k], out.at[pl.ds(row, SLOTS)], sems.at[n, 2 * d + k])
+                )
     for copy in copies:
         copy.start()
     for copy in copies:
         copy.wait()
 
 
-def join(places, pieces):
-    width = pieces[0].shape[2]
+def join(order, places, pieces):
+    width = pieces[0].shape[3]
     rows = 2 * len(pieces) * SLOTS
     return pl.pallas_call(
-        join_kernel,
+        lambda *refs: join_kernel(order, *refs),
         in_specs=[pl.BlockSpec(memory_space=pltpu.SMEM)] + [pl.BlockSpec(memory_space=pl.ANY)] * len(pieces),
-        out_specs=pl.BlockSpec(memory_space=pltpu.VMEM),
-        out_shape=jax.ShapeDtypeStruct((rows, width), jnp.bfloat16),
-        scratch_shapes=[pltpu.SemaphoreType.DMA((2 * len(pieces),))],
-        compiler_params=pltpu.CompilerParams(vmem_limit_bytes=16 * 1024 * 1024),
+        out_specs=[pl.BlockSpec(memory_space=pltpu.VMEM)] * 2,
+        out_shape=[jax.ShapeDtypeStruct((rows, width), jnp.bfloat16)] * 2,
+        scratch_shapes=[pltpu.SemaphoreType.DMA((2, 2 * len(pieces)))],
+        compiler_params=pltpu.CompilerParams(vmem_limit_bytes=8 * 1024 * 1024),
         cost_estimate=SMALL,
         name="join",
     )(places, *pieces)
 
 
-def dgate_up_kernel(places, table, w_ref, a_ref, s_ref, hid_ref, *refs):
-    *pieces, dy_ref, out_ref, give_ref, sems = refs
-    copies = join_copies(places, pieces, dy_ref, sems)
-    for copy in copies:
-        copy.start()
-    for copy in copies:
-        copy.wait()
-    start = hid_ref.shape[0] - give_ref.shape[0]
-
-    def give(chunk, carry):
-        give_ref[:, lanes(chunk)] = product(hid_ref[start:, :], feature_blocks(dy_ref, table, 3, chunk))
-        return carry
-
-    lax.fori_loop(0, CHUNKS, give, 0)
-    tile = 256
-
-    def dhidden_tile(i, carry):
-        part = pl.ds(pl.multiple_of(i * tile, tile), tile)
-        dhidden = lax.dot_general(
-            w_ref[part, :], dy_ref[...], (((1,), (1,)), ((), ())), preferred_element_type=jnp.float32
-        )
-        out_ref[0, part] = (dhidden * a_ref[part, :]).astype(jnp.bfloat16)
-        out_ref[1, part] = (dhidden * s_ref[part, :]).astype(jnp.bfloat16)
-        return carry
-
-    lax.fori_loop(0, w_ref.shape[0] // tile, dhidden_tile, 0)
-
-
-def make_dgate_up(places, table, w_out_t, slope, silu, hidden, pieces):
-    ff, width = w_out_t.shape
-    rows = 2 * len(pieces) * SLOTS
-    per = 3 * ff // 4
-    whole = pl.BlockSpec(memory_space=pltpu.VMEM)
-    small = pl.BlockSpec(memory_space=pltpu.SMEM)
-    return pl.pallas_call(
-        dgate_up_kernel,
-        in_specs=[small] * 2 + [whole] * 4 + [pl.BlockSpec(memory_space=pl.ANY)] * len(pieces),
-        out_specs=[whole] * 3,
-        out_shape=[
-            jax.ShapeDtypeStruct((rows, width), jnp.bfloat16),
-            jax.ShapeDtypeStruct((2, ff, rows), jnp.bfloat16),
-            jax.ShapeDtypeStruct((per, 2 * CHUNKS * LANE), jnp.bfloat16),
-        ],
-        scratch_shapes=[pltpu.SemaphoreType.DMA((2 * len(pieces),))],
-        compiler_params=pltpu.CompilerParams(vmem_limit_bytes=24 * 1024 * 1024),
-        cost_estimate=SMALL,
-        name="dgate_up",
-    )(places, table, w_out_t, slope, silu, hidden, *pieces)
-
-
-def gives_kernel(flows, table, dgu_ref, hid_ref, x_ref, dy_ref, *refs):
-    n = len(flows)
+def gives_kernel(table, gate_up_ref, dhidden_ref, x_ref, dy_ref, dgu_ref, hid_ref, *refs):
+    n = len(FLOWS)
     outs, stages, sems = refs[:n], refs[n : 2 * n], refs[2 * n]
     per = outs[0].shape[0]
-
-    def copy(i, chunk):
+    ff = dhidden_ref.shape[0]
+    tile = 64
+
+    def gradients(i, carry):
+        part = pl.ds(pl.multiple_of(i * tile, tile), tile)
+        lower = pl.ds(pl.multiple_of(ff + i * tile, tile), tile)
+        gate, upper, dhidden = gate_up_ref[part, :], gate_up_ref[lower, :], dhidden_ref[part, :]
+        sig = jax.nn.sigmoid(gate)
+        silu = gate * sig
+        hid_ref[part, :] = (silu * upper).astype(jnp.bfloat16)
+        dgu_ref[part, :] = (dhidden * upper * sig * (1.0 + gate * (1.0 - sig))).astype(jnp.bfloat16)
+        dgu_ref[lower, :] = (dhidden * silu).astype(jnp.bfloat16)
+        return carry
+
+    lax.fori_loop(0, ff // tile, gradients, 0)
+
+    def copy(f, chunk):
         return pltpu.make_async_copy(
-            stages[i].at[:, lanes(chunk)], outs[i].at[:, lanes(chunk)], sems.at[i, chunk]
+            stages[f].at[:, lanes(chunk)], outs[f].at[:, lanes(chunk)], sems.at[f, chunk]
         )
 
-    for i, f in enumerate(flows):
+    for f in range(n):
 
         def body(chunk, carry):
-            for from_dgu, first, count, row in flow_parts(f, per, dgu_ref.shape[0]):
+            for from_dgu, first, count, row in flow_parts(f, per, 2 * ff):
                 left, right = (dgu_ref, x_ref) if from_dgu else (hid_ref, dy_ref)
-                stages[i][row : row + count, lanes(chunk)] = product(
+                stages[f][row : row + count, lanes(chunk)] = product(
                     left[first : first + count, :], feature_blocks(right, table, f, chunk)
                 )
-            copy(i, chunk).start()
+            copy(f, chunk).start()
             return carry
 
         lax.fori_loop(0, CHUNKS, body, 0)
-    for i in range(n):
+    for f in range(n):
         for chunk in range(CHUNKS):
-            copy(i, chunk).wait()
-
-
-def make_gives(flows, table, dgu, hidden, rows_x, rows_dy):
-    per = (dgu.shape[0] + hidden.shape[0]) // 4
-    size = (per, 2 * CHUNKS * LANE)
+            copy(f, chunk).wait()
+
+
+def make_gives(table, gate_up, dhidden, rows_x, rows_dy):
+    ff, rows = dhidden.shape
+    size = (3 * ff // 4, 2 * CHUNKS * LANE)
     whole = pl.BlockSpec(memory_space=pltpu.VMEM)
+    n = len(FLOWS)
     return pl.pallas_call(
-        lambda *refs: gives_kernel(flows, *refs),
+        gives_kernel,
         in_specs=[pl.BlockSpec(memory_space=pltpu.SMEM)] + [whole] * 4,
-        out_specs=[pl.BlockSpec(memory_space=pl.ANY)] * len(flows),
-        out_shape=[jax.ShapeDtypeStruct(size, jnp.bfloat16)] * len(flows),
-        scratch_shapes=[pltpu.VMEM(size, jnp.bfloat16)] * len(flows)
-        + [pltpu.SemaphoreType.DMA((len(flows), CHUNKS))],
+        out_specs=[whole] * 2 + [pl.BlockSpec(memory_space=pl.ANY)] * n,
+        out_shape=[
+            jax.ShapeDtypeStruct((2 * ff, rows), jnp.bfloat16),
+            jax.ShapeDtypeStruct((ff, rows), jnp.bfloat16),
+        ]
+        + [jax.ShapeDtypeStruct(size, jnp.bfloat16)] * n,
+        scratch_shapes=[pltpu.VMEM(size, jnp.bfloat16)] * n + [pltpu.SemaphoreType.DMA((n, CHUNKS))],
         compiler_params=pltpu.CompilerParams(vmem_limit_bytes=16 * 1024 * 1024),
         cost_estimate=SMALL,
         name="give",
-    )(table, dgu, hidden, rows_x, rows_dy)
+    )(table, gate_up, dhidden, rows_x, rows_dy)
 
 
 def merge_kernel(f, table, got_ref, *refs):
@@ -214,7 +181,7 @@
         out_specs=[whole] * 2,
         out_shape=[jax.ShapeDtypeStruct((per, CHUNKS * LANE), jnp.bfloat16)] * 2,
         compiler_params=pltpu.CompilerParams(vmem_limit_bytes=12 * 1024 * 1024),
-        cost_estimate=SMALL,
+        cost_estimate=LARGE,
         name="merge",
     )(table, got, *sides)
 
@@ -257,9 +224,6 @@
         for x in range(SIDE)
         for y in range(SIDE)
     ]
-
-
-FLOWS = ((0, False), (0, True), (1, False), (1, True))
 
 
 def first_table(at, axis, odd):
@@ -299,45 +263,44 @@
         + core
     ).reshape(-1)
 
-    def send(values):
-        def pack(table):
-            packed = jnp.dot(table, values, preferred_element_type=jnp.float32)
-            return packed.astype(jnp.bfloat16).reshape(chips, SLOTS, width)
-
-        other = lax.ppermute(pack(other_rows), "expert", [(i, i ^ 1) for i in range(num_experts)])
-        both = jnp.stack([pack(mine_rows), other], axis=1)
-        pieces = [both[0]] + [None] * (chips - 1)
-        for d in (4, 3, 5, 2, 6, 1, 7):
-            pieces[d] = lax.ppermute(
-                both[d], "expert", [(i, (i + 2 * d) % num_experts) for i in range(num_experts)]
+    def pack(table, values):
+        packed = jnp.dot(table, values, preferred_element_type=jnp.float32)
+        return packed.astype(jnp.bfloat16).reshape(chips, SLOTS, width)
+
+    swap = [(i, i ^ 1) for i in range(num_experts)]
+    sides = [
+        (pack(mine_rows, values), lax.ppermute(pack(other_rows, values), "expert", swap))
+        for values in (tokens, out_grads)
+    ]
+
+    def piece(d):
+        return jnp.concatenate([side[d] for pair in sides for side in pair]).reshape(2, 2, SLOTS, width)
+
+    order = (0, 3, 5, 2, 6, 1, 7, 4)
+    pieces = [piece(0)]
+    for d in order[1:]:
+        pieces.append(
+            lax.ppermute(
+                piece(d), "expert", [(i, (i + 2 * d) % num_experts) for i in range(num_experts)]
             )
-        return pieces
-
-    rows_x = join(places, send(tokens))
-    pieces_dy = send(out_grads)
+        )
+    rows_x, rows_dy = join(order, places, pieces)
     w_in = w_gate_up[0]
-    w_out, rows_x = lax.optimization_barrier((w_down_t[0], rows_x))
-    w_out_t = w_out.T
+    w_out = w_down_t[0]
 
     gate_up = lax.dot_general(
         w_in, rows_x, (((0,), (1,)), ((), ())), preferred_element_type=jnp.float32
     )
-    gate = gate_up[:ff]
-    upper = gate_up[ff:]
-    sig = jax.nn.sigmoid(gate)
-    silu = gate * sig
-    hidden = (silu * upper).astype(jnp.bfloat16)
-    slope = upper * sig * (1.0 + gate * (1.0 - sig))
-
+    dhidden = lax.dot_general(
+        w_out, rows_dy, (((0,), (1,)), ((), ())), preferred_element_type=jnp.float32
+    )
     me = lax.axis_index("dp")
     at = (me // SIDE, me % SIDE)
     tables = [first_table(at, axis, odd) for axis, odd in FLOWS]
 
     to_give = jnp.stack([t[0] for t in tables])
     to_keep = jnp.stack([t[1] for t in tables])
-    rows_dy, dgu, last_give = make_dgate_up(places, to_give, w_out_t, slope, silu, hidden, pieces_dy)
-    dgu = dgu.reshape(2 * ff, rows)
-    gives = [*make_gives((0, 1, 2), to_give, dgu, hidden, rows_x, rows_dy), last_give]
+    dgu, hidden, *gives = make_gives(to_give, gate_up, dhidden, rows_x, rows_dy)
     gots = [None] * 4
     for f in (3, 0, 1, 2):
         gots[f] = lax.ppermute(gives[f], "dp", pair_perm(*FLOWS[f]))

time: 222 us -> 230 us (1.036)
  matrix products: 12.9 us -> 24.1 us
  Pallas kernels: 29 us -> 24 us
  local copies, waits for them, and re-layouts: 12.5 us -> 15.9 us
  starting transfers between devices: 55.3 us -> 51.9 us
    ppermute x16 -> x9, starting transfers between devices: 36.6 us -> 20.1 us  [the longest x7 19.6 us: local(): lax.ppermute(piece(d), 'expert', [(i, (i + 2 * d) % num_experts) for i in...]
    ppermute x16 -> x9, waiting for transfers between devices: 56.1 us -> 71.2 us  [the longest x7 71.2 us: local(): lax.ppermute(piece(d), 'expert', [(i, (i + 2 * d) % num_experts) for i in...]
    ppermute x12, starting transfers between devices: 7.86 us -> 18.3 us  [local(): got = lax.ppermute(give, 'dp', pair_perm(axis, odd))]
    ppermute x4, waiting for transfers between devices: 20.3 us -> 11.2 us  [local(): gots[f] = lax.ppermute(gives[f], 'dp', pair_perm(*FLOWS[f]))]
    ppermute x12, waiting for transfers between devices: 24.9 us -> 17.5 us  [local(): got = lax.ppermute(give, 'dp', pair_perm(axis, odd))]
    dot_general x4, matrix products: 1.73 us -> 8.08 us  [pack(): packed = jnp.dot(table, values, preferred_element_type=jnp.float32)]
    concatenate x0 -> x8, other arithmetic: none -> 5.25 us  [piece(): jnp.concatenate([side[d] for pair in sides for side in pair])]
    pallas_call x3 -> x2, Pallas kernels: 17 us -> 12.7 us  [the longest x1 7.92 us: make_gives(): pl.pallas_call(gives_kernel, in_specs=[pl.BlockSpec(memory_space=pltpu.SM...]
  transfers between devices with their start and end apart: 33 -> 26, of which waited for: 18 -> 15; matrix products, arithmetic and copies ran while one was open for 8% -> 12% of each run, Pallas kernels for 10% -> 5%
where the time goes in v1:
time: 230 us; the launch traced here: 228 us
  waiting for transfers between devices  100 us (43%)
  starting transfers between devices  51.9 us (23%)
  matrix products  24.1 us (10%)
  Pallas kernels  24 us (10%)
  local copies, waits for them, and re-layouts  15.9 us (7%)
  other arithmetic  11.2 us (5%)
    ppermute x7, waiting for transfers between devices, local(): lax.ppermute(piece(d), 'expert', [(i, (i + 2 * d) % num_experts) for i in...  71.2 us
    ppermute x7, starting transfers between devices, local(): lax.ppermute(piece(d), 'expert', [(i, (i + 2 * d) % num_experts) for i in...  19.6 us
    ppermute x12, starting transfers between devices, local(): got = lax.ppermute(give, 'dp', pair_perm(axis, odd))  18.3 us
    ppermute x12, waiting for transfers between devices, local(): got = lax.ppermute(give, 'dp', pair_perm(axis, odd))  17.5 us
    ppermute x4, waiting for transfers between devices, local(): gots[f] = lax.ppermute(gives[f], 'dp', pair_perm(*FLOWS[f]))  11.2 us
    pallas_call x4, Pallas kernels, merge(): pl.pallas_call(lambda *refs: merge_kernel(f, *refs), in_specs=[pl.BlockSp...  10.3 us
    unnamed x46, local copies, waits for them, and re-layouts  9.38 us
    dot_general x4, matrix products, pack(): packed = jnp.dot(table, values, preferred_element_type=jnp.float32)  8.08 us
  transfers between devices with their start and end apart: 26, of which 15 were waited for; matrix products, arithmetic and copies ran while one was open for 12% of the time, Pallas kernels for 5%

profile of v1, /device:TPU:2, one launch (start us, length us, event | category | flops | bytes accessed | tf_op | source)
XLA Modules:
  0.0 228.1 jit_solution(2807583870531718102)
XLA Ops:
  0.7 0.9 convert_reduce_fusion
  2.4 2.5 %convolution_convert_fusion.2 = bf16[256,2048]{1,0:T(8,128)(2,1)} fusion(bf16[160,2048]{1,0:T(8,128)(2,1)} %param.6, s32[160]{0:T(256)S(1)} %broadcast_select_fusion), kind=kOutput, calls=%fused_computation.10 | convolution fusion | flops 168337408 | bytes 1704576 | tf_op jit(solution)/shard_map/dot_general | solution.py:267
  4.9 1.4 convolution_convert_fusion
  7.3 2.5 %convolution_convert_fusion.1 = bf16[256,2048]{1,0:T(8,128)(2,1)} fusion(bf16[160,2048]{1,0:T(8,128)(2,1)} %param.7, s32[160]{0:T(256)S(1)} %get-tuple-element.39), kind=kOutput, calls=%fused_computation.9 | convolution fusion | flops 168337408 | bytes 1704576 | tf_op jit(solution)/shard_map/dot_general | solution.py:267
  14.4 1.6 convolution_convert_fusion.3
  16.3 1.4 slice_bitcast_fusion.1
  17.7 2.1 slice_bitcast_fusion
  19.8 4.7 %collective-permute-start.2 = (bf16[2,2,32,2048]{3,2,1,0:T(8,128)(2,1)S(1)}, bf16[2,2,32,2048]{3,2,1,0:T(8,128)(2,1)S(1)}, u32[]{:S(2)}, u32[]{:S(2)}) collective-permute-start(bf16[2,2,32,2048]{3,2,1,0:T(8,128)(2,1)S(1)} %bitcast.85), channel_id=1, source_target_pairs={{0,6},{1,7},{2,8},{3,9},{4,10},{5,11},{6,12},{7,13},{8,14},{9,15},... | collective-permute-start | bytes 1572872 | tf_op jit(solution)/shard_map/ppermute | solution.py:283
  24.5 2.2 collective-permute-start.3
  26.7 0.8 pad_maximum_fusion.3
  27.6 1.6 collective-permute-start.4
  29.1 0.8 pad_maximum_fusion.4
  30.0 3.0 %collective-permute-start.5 = (bf16[2,2,32,2048]{3,2,1,0:T(8,128)(2,1)}, bf16[2,2,32,2048]{3,2,1,0:T(8,128)(2,1)}, u32[]{:S(2)}, u32[]{:S(2)}) collective-permute-start(bf16[2,2,32,2048]{3,2,1,0:T(8,128)(2,1)} %bitcast.27), channel_id=1, source_target_pairs={{0,12},{1,13},{2,14},{3,15},{4,0},{5,1},{6,2},{7,3},{8,4},{9,5},{1... | collective-permute-start | bytes 1572872 | tf_op jit(solution)/shard_map/ppermute | solution.py:283
  33.0 0.8 pad_maximum_fusion.5
  34.4 0.9 pad_maximum_fusion.7
  35.3 0.8 pad_maximum_fusion.6
  36.1 23.9 %collective-permute-done.2.refs_2_ = bf16[2,2,32,2048]{3,2,1,0:T(8,128)(2,1)S(1)} collective-permute-done((bf16[2,2,32,2048]{3,2,1,0:T(8,128)(2,1)S(1)}, bf16[2,2,32,2048]{3,2,1,0:T(8,128)(2,1)S(1)}, u32[]{:S(2)}, u32[]{:S(2)}) %collective-permute-start.2) | collective-permute-done | bytes 524320 | tf_op jit(solution)/shard_map/ppermute | solution.py:283
  60.8 3.5 %collective-permute-start.7 = (bf16[2,2,32,2048]{3,2,1,0:T(8,128)(2,1)}, bf16[2,2,32,2048]{3,2,1,0:T(8,128)(2,1)}, u32[]{:S(2)}, u32[]{:S(2)}) collective-permute-start(bf16[2,2,32,2048]{3,2,1,0:T(8,128)(2,1)} %bitcast.33), channel_id=1, source_target_pairs={{0,14},{1,15},{2,0},{3,1},{4,2},{5,3},{6,4},{7,5},{8,6},{9,7},{10,... | collective-permute-start | bytes 1572872 | tf_op jit(solution)/shard_map/ppermute | solution.py:283
  64.4 0.8 copy-done.8
  65.2 4.0 %collective-permute-start.8 = (bf16[2,2,32,2048]{3,2,1,0:T(8,128)(2,1)}, bf16[2,2,32,2048]{3,2,1,0:T(8,128)(2,1)}, u32[]{:S(2)}, u32[]{:S(2)}) collective-permute-start(bf16[2,2,32,2048]{3,2,1,0:T(8,128)(2,1)} %bitcast.36), channel_id=1, source_target_pairs={{0,8},{1,9},{2,10},{3,11},{4,12},{5,13},{6,14},{7,15},{8,0},{9,1},... | collective-permute-start | bytes 1572872 | tf_op jit(solution)/shard_map/ppermute | solution.py:283
  70.0 0.9 pad_maximum_fusion
  71.0 12.0 %collective-permute-done.4.refs_4_ = bf16[2,2,32,2048]{3,2,1,0:T(8,128)(2,1)} collective-permute-done((bf16[2,2,32,2048]{3,2,1,0:T(8,128)(2,1)}, bf16[2,2,32,2048]{3,2,1,0:T(8,128)(2,1)}, u32[]{:S(2)}, u32[]{:S(2)}) %collective-permute-start.4) | collective-permute-done | bytes 524320 | tf_op jit(solution)/shard_map/ppermute | solution.py:283
  83.0 2.9 %collective-permute-done.5.refs_5_ = bf16[2,2,32,2048]{3,2,1,0:T(8,128)(2,1)} collective-permute-done((bf16[2,2,32,2048]{3,2,1,0:T(8,128)(2,1)}, bf16[2,2,32,2048]{3,2,1,0:T(8,128)(2,1)}, u32[]{:S(2)}, u32[]{:S(2)}) %collective-permute-start.5) | collective-permute-done | bytes 524320 | tf_op jit(solution)/shard_map/ppermute | solution.py:283
  85.9 8.3 %collective-permute-done.6.refs_6_ = bf16[2,2,32,2048]{3,2,1,0:T(8,128)(2,1)} collective-permute-done((bf16[2,2,32,2048]{3,2,1,0:T(8,128)(2,1)}, bf16[2,2,32,2048]{3,2,1,0:T(8,128)(2,1)}, u32[]{:S(2)}, u32[]{:S(2)}) %collective-permute-start.6) | collective-permute-done | bytes 524320 | tf_op jit(solution)/shard_map/ppermute | solution.py:283
  94.2 2.6 %collective-permute-done.7.refs_7_ = bf16[2,2,32,2048]{3,2,1,0:T(8,128)(2,1)} collective-permute-done((bf16[2,2,32,2048]{3,2,1,0:T(8,128)(2,1)}, bf16[2,2,32,2048]{3,2,1,0:T(8,128)(2,1)}, u32[]{:S(2)}, u32[]{:S(2)}) %collective-permute-start.7) | collective-permute-done | bytes 524320 | tf_op jit(solution)/shard_map/ppermute | solution.py:283
  96.8 21.5 %collective-permute-done.8.refs_8_ = bf16[2,2,32,2048]{3,2,1,0:T(8,128)(2,1)} collective-permute-done((bf16[2,2,32,2048]{3,2,1,0:T(8,128)(2,1)}, bf16[2,2,32,2048]{3,2,1,0:T(8,128)(2,1)}, u32[]{:S(2)}, u32[]{:S(2)}) %collective-permute-start.8) | collective-permute-done | bytes 524320 | tf_op jit(solution)/shard_map/ppermute | solution.py:283
  118.3 1.0 copy-done.7
  119.3 1.0 copy-done.9
  120.4 4.8 %join.1 = (bf16[512,2048]{1,0:T(8,128)(2,1)S(1)}, bf16[512,2048]{1,0:T(8,128)(2,1)S(1)}) custom-call(s32[16]{0:T(128)S(1)} %add.363.refs_0_, bf16[2,2,32,2048]{3,2,1,0:T(8,128)(2,1)S(1)} %bitcast.83, bf16[2,2,32,2048]{3,2,1,0:T(8,128)(2,1)S(1)} %copy-done.7, bf16[2,2,32,2048]{3,2,1,0:T(8,128)(2,1)S(1)} %copy-done.9, ...), custom_call_target="tpu_custom_call" | custom-call | flops 1000000 | bytes 100000 | tf_op jit(solution)/shard_map/join/pallas_call | solution.py:78
  125.2 1.8 fusion.12.dhidden_ref
  127.0 1.2 slice-done.1
  128.3 3.6 %fusion.4.gate_up_ref = f32[1536,512]{1,0:T(8,128)S(1)} fusion(bf16[512,2048]{1,0:T(8,128)(2,1)S(1)} %get-tuple-element.21.x_ref.refs_3_, bf16[1,2048,1536]{2,1,0:T(8,128)(2,1)S(1)} %bitcast.90), kind=kOutput, calls=%fused_computation.4 | convolution fusion | flops 3221225472 | bytes 11534336 | tf_op jit(solution)/shard_map/dot_general | solution.py:291
  131.9 7.9 %give.1 = (bf16[1536,512]{1,0:T(8,128)(2,1)S(1)}, bf16[768,512]{1,0:T(8,128)(2,1)S(1)}, bf16[576,1024]{1,0:T(8,128)(2,1)}, bf16[576,1024]{1,0:T(8,128)(2,1)S(1)}...) custom-call(s32[4,8]{1,0:T(4,128)S(1)} %pad_add_fusion.table, f32[1536,512]{1,0:T(8,128)S(1)} %fusion.4.gate_up_ref, ...), custom_call_target="tpu_custom_call" | custom-call | flops 1000000 | bytes 100000 | tf_op jit(solution)/shard_map/give/pallas_call | solution.py:137
  139.8 1.0 copy-done.12
  140.8 0.9 copy-done.14
  141.7 1.1 copy-done.13
  143.9 1.9 collective-permute-start.12
  145.8 1.8 collective-permute-start.15
  147.6 7.6 %fusion.9 = bf16[512,2048]{1,0:T(8,128)(2,1)} fusion(bf16[1536,512]{1,0:T(8,128)(2,1)S(1)} %get-tuple-element.23.refs_2_, bf16[1,2048,1536]{2,1,0:T(8,128)(2,1)} %param.9), kind=kOutput, calls=%fused_computation.7 | convolution fusion | flops 3222274048 | bytes 9961472 | tf_op jit(solution)/shard_map/dot_general | solution.py:307
  155.2 6.6 %all-to-all-start = ((bf16[16,32,2048]{2,1,0:T(8,128)(2,1)}), bf16[16,32,2048]{2,1,0:T(8,128)(2,1)}, u32[]{:S(2)}, u32[]{:S(2)}) async-start(bf16[16,32,2048]{2,1,0:T(8,128)(2,1)} %bitcast.84), calls=%async_computation | async-start | bytes 4194304 | tf_op jit(solution)/shard_map/all_to_all | solution.py:310
  161.8 2.5 %collective-permute-start.18 = (bf16[576,1024]{1,0:T(8,128)(2,1)S(1)}, bf16[576,1024]{1,0:T(8,128)(2,1)S(1)}, u32[]{:S(2)}, u32[]{:S(2)}) collective-permute-start(bf16[576,1024]{1,0:T(8,128)(2,1)S(1)} %get-tuple-element.34), channel_id=1, source_target_pairs={{0,48},{16,32},{32,16},{48,0},{64,112},{80,96},{96,80},{112,64},{1... | collective-permute-start | bytes 3538952 | tf_op jit(solution)/shard_map/ppermute | solution.py:306
  164.3 5.3 %collective-permute-done.9.refs_1_ = bf16[576,1024]{1,0:T(8,128)(2,1)} collective-permute-done((bf16[576,1024]{1,0:T(8,128)(2,1)}, bf16[576,1024]{1,0:T(8,128)(2,1)}, u32[]{:S(2)}, u32[]{:S(2)}) %collective-permute-start.9) | collective-permute-done | bytes 1179680 | tf_op jit(solution)/shard_map/ppermute | solution.py:306
  169.6 1.4 copy-done.11
  171.0 2.7 %merge.4 = (bf16[576,512]{1,0:T(8,128)(2,1)S(1)}, bf16[576,512]{1,0:T(8,128)(2,1)S(1)}) custom-call(s32[4,8]{1,0:T(4,128)S(1)} %pad_add_fusion.1.refs_0_, bf16[576,1024]{1,0:T(8,128)(2,1)} %collective-permute-done.9.refs_1_, bf16[1536,512]{1,0:T(8,128)(2,1)S(1)} %copy-done.11, bf16[512,2048]{1,0:T(8,128)(2,1)S(1)} %copy-done.5), custom_call_target="tpu_custom_call" | custom-call | flops 20000000000 | bytes 10000000 | tf_op jit(solution)/shard_map/merge/pallas_call | solution.py:178
  173.8 1.8 collective-permute-start.10
  175.5 2.7 %merge.5 = (bf16[576,512]{1,0:T(8,128)(2,1)S(1)}, bf16[576,512]{1,0:T(8,128)(2,1)S(1)}) custom-call(s32[4,8]{1,0:T(4,128)S(1)} %pad_add_fusion.1.refs_0_, bf16[576,1024]{1,0:T(8,128)(2,1)} %collective-permute-done.12.refs_1_, bf16[1536,512]{1,0:T(8,128)(2,1)S(1)} %copy-done.11, bf16[512,2048]{1,0:T(8,128)(2,1)S(1)} %copy-done.5), custom_call_target="tpu_custom_call" | custom-call | flops 20000000000 | bytes 10000000 | tf_op jit(solution)/shard_map/merge/pallas_call | solution.py:178
  178.3 1.4 collective-permute-start.13
  179.7 2.8 %merge.6 = (bf16[576,512]{1,0:T(8,128)(2,1)S(1)}, bf16[576,512]{1,0:T(8,128)(2,1)S(1)}) custom-call(s32[4,8]{1,0:T(4,128)S(1)} %pad_add_fusion.1.refs_0_, bf16[576,1024]{1,0:T(8,128)(2,1)} %collective-permute-done.15.refs_1_, bf16[1536,512]{1,0:T(8,128)(2,1)S(1)} %copy-done.11, bf16[512,2048]{1,0:T(8,128)(2,1)S(1)} %copy-done.5, ...), custom_call_target="tpu_custom_call" | custom-call | flops 20000000000 | bytes 10000000 | tf_op jit(solution)/shard_map/merge/pallas_call | solution.py:178
  182.5 3.7 %collective-permute-start.16 = (bf16[576,512]{1,0:T(8,128)(2,1)S(1)}, bf16[576,512]{1,0:T(8,128)(2,1)S(1)}, u32[]{:S(2)}, u32[]{:S(2)}) collective-permute-start(bf16[576,512]{1,0:T(8,128)(2,1)S(1)} %get-tuple-element.33), channel_id=1, source_target_pairs={{0,48},{16,32},{32,16},{48,0},{64,112},{80,96},{96,80},{112,64},{1... | collective-permute-start | bytes 1769480 | tf_op jit(solution)/shard_map/ppermute | solution.py:323
  186.2 5.9 %collective-permute-done.18.refs_1_ = bf16[576,1024]{1,0:T(8,128)(2,1)S(1)} collective-permute-done((bf16[576,1024]{1,0:T(8,128)(2,1)S(1)}, bf16[576,1024]{1,0:T(8,128)(2,1)S(1)}, u32[]{:S(2)}, u32[]{:S(2)}) %collective-permute-start.18) | collective-permute-done | bytes 1179680 | tf_op jit(solution)/shard_map/ppermute | solution.py:306
  192.1 2.0 merge.7
  194.4 2.1 collective-permute-start.11
  196.7 2.2 collective-permute-start.14
  198.9 5.8 %collective-permute-done.16 = bf16[576,512]{1,0:T(8,128)(2,1)S(1)} collective-permute-done((bf16[576,512]{1,0:T(8,128)(2,1)S(1)}, bf16[576,512]{1,0:T(8,128)(2,1)S(1)}, u32[]{:S(2)}, u32[]{:S(2)}) %collective-permute-start.16) | collective-permute-done | bytes 589856 | tf_op jit(solution)/shard_map/ppermute | solution.py:323
  204.9 1.5 collective-permute-start.17
  206.4 4.1 %collective-permute-done.19 = bf16[576,512]{1,0:T(8,128)(2,1)S(1)} collective-permute-done((bf16[576,512]{1,0:T(8,128)(2,1)S(1)}, bf16[576,512]{1,0:T(8,128)(2,1)S(1)}, u32[]{:S(2)}, u32[]{:S(2)}) %collective-permute-start.19) | collective-permute-done | bytes 589856 | tf_op jit(solution)/shard_map/ppermute | solution.py:323
  210.9 3.3 %collective-permute-done.11 = bf16[576,256]{1,0:T(8,128)(2,1)S(1)} collective-permute-done((bf16[576,256]{1,0:T(8,128)(2,1)S(1)}, bf16[576,256]{1,0:T(8,128)(2,1)S(1)}, u32[]{:S(2)}, u32[]{:S(2)}) %collective-permute-start.11) | collective-permute-done | bytes 294944 | tf_op jit(solution)/shard_map/ppermute | solution.py:323
  214.3 2.2 collective-permute-start.21
  217.0 1.2 collective-permute-done.20
  218.3 2.7 %collective-permute-start.24 = (bf16[576,128]{1,0:T(8,128)(2,1)S(1)}, bf16[576,128]{1,0:T(8,128)(2,1)S(1)}, u32[]{:S(2)}, u32[]{:S(2)}) collective-permute-start(bf16[576,128]{1,0:T(8,128)(2,1)S(1)} %get-tuple-element.82), channel_id=1, source_target_pairs={{0,64},{16,80},{32,96},{48,112},{64,0},{80,16},{96,32},{112,48},{1... | collective-permute-start | bytes 442376 | tf_op jit(solution)/shard_map/ppermute | solution.py:323
  221.0 0.9 collective-permute-done.22.refs_5_
  222.1 2.0 collective-permute-done.24.refs_7_
  224.1 1.0 finish.1
  225.1 3.0 %convolution_convert_fusion.4 = bf16[160,2048]{1,0:T(8,128)(2,1)} fusion(bf16[512,2048]{1,0:T(8,128)(2,1)} %bitcast.42, s32[160]{0:T(256)S(1)} %get-tuple-element.90), kind=kOutput, calls=%fused_computation.12 | convolution fusion | flops 335953920 | bytes 2753152 | tf_op jit(solution)/shard_map/dot_general | solution.py:313
  (96 shorter events, 11.7 us)
Async XLA Ops:
  0.6 124.5 %copy-start = (bf16[1,2048,768]{2,1,0:T(8,128)(2,1)S(1)}, bf16[1,2048,768]{2,1,0:T(8,128)(2,1)}, u32[]{:S(2)}) copy-start(bf16[1,2048,768]{2,1,0:T(8,128)(2,1)} %param.10) | copy-start | bytes 9437188
  1.6 3.3 %copy-start.17 = (bf16[160,2048]{1,0:T(8,128)(2,1)S(1)}, bf16[160,2048]{1,0:T(8,128)(2,1)}, u32[]{:S(2)}) copy-start(bf16[160,2048]{1,0:T(8,128)(2,1)} %param.7) | copy-start | bytes 1966084
  4.9 11.3 %collective-permute-start = (bf16[8,32,2048]{2,1,0:T(8,128)(2,1)}, bf16[8,32,2048]{2,1,0:T(8,128)(2,1)}, u32[]{:S(2)}, u32[]{:S(2)}) collective-permute-start(bf16[8,32,2048]{2,1,0:T(8,128)(2,1)} %bitcast.11), channel_id=1, source_target_pairs={{0,1},{1,0},{2,3},{3,2},{4,5},{5,4},{6,7},{7,6},{8,9},{9,8},{10,11... | collective-permute-start | bytes 3145736 | tf_op jit(solution)/shard_map/ppermute | solution.py:272
  6.4 11.3 %collective-permute-start.1 = (bf16[8,32,2048]{2,1,0:T(8,128)(2,1)}, bf16[8,32,2048]{2,1,0:T(8,128)(2,1)}, u32[]{:S(2)}, u32[]{:S(2)}) collective-permute-start(bf16[8,32,2048]{2,1,0:T(8,128)(2,1)} %bitcast.13), channel_id=1, source_target_pairs={{0,1},{1,0},{2,3},{3,2},{4,5},{5,4},{6,7},{7,6},{8,9},{9,8},{10,11... | collective-permute-start | bytes 3145736 | tf_op jit(solution)/shard_map/ppermute | solution.py:272
  14.4 1.6 copy-start.16
  19.8 40.3 %collective-permute-start.2 = (bf16[2,2,32,2048]{3,2,1,0:T(8,128)(2,1)S(1)}, bf16[2,2,32,2048]{3,2,1,0:T(8,128)(2,1)S(1)}, u32[]{:S(2)}, u32[]{:S(2)}) collective-permute-start(bf16[2,2,32,2048]{3,2,1,0:T(8,128)(2,1)S(1)} %bitcast.85), channel_id=1, source_target_pairs={{0,6},{1,7},{2,8},{3,9},{4,10},{5,11},{6,12},{7,13},{8,14},{9,15},... | collective-permute-start | bytes 1572872 | tf_op jit(solution)/shard_map/ppermute | solution.py:283
  24.5 39.8 %collective-permute-start.3 = (bf16[2,2,32,2048]{3,2,1,0:T(8,128)(2,1)S(1)}, bf16[2,2,32,2048]{3,2,1,0:T(8,128)(2,1)S(1)}, u32[]{:S(2)}, u32[]{:S(2)}) collective-permute-start(bf16[2,2,32,2048]{3,2,1,0:T(8,128)(2,1)S(1)} %bitcast.86), channel_id=1, source_target_pairs={{0,10},{1,11},{2,12},{3,13},{4,14},{5,15},{6,0},{7,1},{8,2},{9,3},... | collective-permute-start | bytes 1572872 | tf_op jit(solution)/shard_map/ppermute | solution.py:283
  27.6 55.4 %collective-permute-start.4 = (bf16[2,2,32,2048]{3,2,1,0:T(8,128)(2,1)}, bf16[2,2,32,2048]{3,2,1,0:T(8,128)(2,1)}, u32[]{:S(2)}, u32[]{:S(2)}) collective-permute-start(bf16[2,2,32,2048]{3,2,1,0:T(8,128)(2,1)} %bitcast.24), channel_id=1, source_target_pairs={{0,4},{1,5},{2,6},{3,7},{4,8},{5,9},{6,10},{7,11},{8,12},{9,13},{1... | collective-permute-start | bytes 1572872 | tf_op jit(solution)/shard_map/ppermute | solution.py:283
  30.0 55.9 %collective-permute-start.5 = (bf16[2,2,32,2048]{3,2,1,0:T(8,128)(2,1)}, bf16[2,2,32,2048]{3,2,1,0:T(8,128)(2,1)}, u32[]{:S(2)}, u32[]{:S(2)}) collective-permute-start(bf16[2,2,32,2048]{3,2,1,0:T(8,128)(2,1)} %bitcast.27), channel_id=1, source_target_pairs={{0,12},{1,13},{2,14},{3,15},{4,0},{5,1},{6,2},{7,3},{8,4},{9,5},{1... | collective-permute-start | bytes 1572872 | tf_op jit(solution)/shard_map/ppermute | solution.py:283
  33.8 60.4 %collective-permute-start.6 = (bf16[2,2,32,2048]{3,2,1,0:T(8,128)(2,1)}, bf16[2,2,32,2048]{3,2,1,0:T(8,128)(2,1)}, u32[]{:S(2)}, u32[]{:S(2)}) collective-permute-start(bf16[2,2,32,2048]{3,2,1,0:T(8,128)(2,1)} %bitcast.30), channel_id=1, source_target_pairs={{0,2},{1,3},{2,4},{3,5},{4,6},{5,7},{6,8},{7,9},{8,10},{9,11},{10,... | collective-permute-start | bytes 1572872 | tf_op jit(solution)/shard_map/ppermute | solution.py:283
  60.0 0.8 copy-start.6
  60.8 35.9 %collective-permute-start.7 = (bf16[2,2,32,2048]{3,2,1,0:T(8,128)(2,1)}, bf16[2,2,32,2048]{3,2,1,0:T(8,128)(2,1)}, u32[]{:S(2)}, u32[]{:S(2)}) collective-permute-start(bf16[2,2,32,2048]{3,2,1,0:T(8,128)(2,1)} %bitcast.33), channel_id=1, source_target_pairs={{0,14},{1,15},{2,0},{3,1},{4,2},{5,3},{6,4},{7,5},{8,6},{9,7},{10,... | collective-permute-start | bytes 1572872 | tf_op jit(solution)/shard_map/ppermute | solution.py:283
  64.3 0.8 copy-start.8
  65.2 53.1 %collective-permute-start.8 = (bf16[2,2,32,2048]{3,2,1,0:T(8,128)(2,1)}, bf16[2,2,32,2048]{3,2,1,0:T(8,128)(2,1)}, u32[]{:S(2)}, u32[]{:S(2)}) collective-permute-start(bf16[2,2,32,2048]{3,2,1,0:T(8,128)(2,1)} %bitcast.36), channel_id=1, source_target_pairs={{0,8},{1,9},{2,10},{3,11},{4,12},{5,13},{6,14},{7,15},{8,0},{9,1},... | collective-permute-start | bytes 1572872 | tf_op jit(solution)/shard_map/ppermute | solution.py:283
  118.3 1.0 copy-start.7
  119.3 1.0 copy-start.9
  120.4 6.7 %slice-start = ((s8[6291456]{0:T(1024)(128)(4,1)}), s8[4194304]{0:T(1024)(128)(4,1)S(1)}, s32[]{:S(2)}) async-start(s8[6291456]{0:T(1024)(128)(4,1)} %bitcast.89), calls=%async_computation.1 | async-start | bytes 8388608
  125.1 6.7 %copy-start.2 = (bf16[512,2048]{1,0:T(8,128)(2,1)}, bf16[512,2048]{1,0:T(8,128)(2,1)S(1)}, u32[]{:S(2)}) copy-start(bf16[512,2048]{1,0:T(8,128)(2,1)S(1)} %get-tuple-element.22.dy_ref.refs_5_.refs_3_) | copy-start | bytes 6291460
  125.1 6.7 %copy-start.4 = (bf16[512,2048]{1,0:T(8,128)(2,1)}, bf16[512,2048]{1,0:T(8,128)(2,1)S(1)}, u32[]{:S(2)}) copy-start(bf16[512,2048]{1,0:T(8,128)(2,1)S(1)} %get-tuple-element.21.x_ref.refs_3_) | copy-start | bytes 6291460
  125.2 3.1 %slice-start.1 = ((s8[6291456]{0:T(1024)(128)(4,1)}), s8[2097152]{0:T(1024)(128)(4,1)S(1)}, s32[]{:S(2)}) async-start(s8[6291456]{0:T(1024)(128)(4,1)} %bitcast.89), calls=%async_computation.2 | async-start | bytes 4194304
  131.9 11.7 %copy-start.18 = (s32[2,4]{1,0:T(2,128)S(1)}, s32[2,4]{1,0:T(2,128)}, u32[]{:S(2)}) copy-start(s32[2,4]{1,0:T(2,128)} %get-tuple-element.97) | copy-start | bytes 100
  131.9 11.8 %copy-start.19 = (s32[2,4]{1,0:T(2,128)S(1)}, s32[2,4]{1,0:T(2,128)}, u32[]{:S(2)}) copy-start(s32[2,4]{1,0:T(2,128)} %get-tuple-element.93) | copy-start | bytes 100
  131.9 11.9 %copy-start.20 = (s32[2,4]{1,0:T(2,128)S(1)}, s32[2,4]{1,0:T(2,128)}, u32[]{:S(2)}) copy-start(s32[2,4]{1,0:T(2,128)} %get-tuple-element.95) | copy-start | bytes 100
  139.8 1.0 copy-start.12
  140.8 0.9 copy-start.14
  141.7 1.1 copy-start.13
  141.7 13.5 %copy-start.10 = (bf16[1536,512]{1,0:T(8,128)(2,1)}, bf16[1536,512]{1,0:T(8,128)(2,1)S(1)}, u32[]{:S(2)}) copy-start(bf16[1536,512]{1,0:T(8,128)(2,1)S(1)} %get-tuple-element.23.refs_2_) | copy-start | bytes 4718596
  142.8 26.8 %collective-permute-start.9 = (bf16[576,1024]{1,0:T(8,128)(2,1)}, bf16[576,1024]{1,0:T(8,128)(2,1)}, u32[]{:S(2)}, u32[]{:S(2)}) collective-permute-start(bf16[576,1024]{1,0:T(8,128)(2,1)} %get-tuple-element.24), channel_id=1, source_target_pairs={{0,64},{16,80},{32,96},{48,112},{64,0},{80,16},{96,32},{112,48},{1... | collective-permute-start | bytes 3538952 | tf_op jit(solution)/shard_map/ppermute | solution.py:306
  143.9 31.7 %collective-permute-start.12 = (bf16[576,1024]{1,0:T(8,128)(2,1)}, bf16[576,1024]{1,0:T(8,128)(2,1)}, u32[]{:S(2)}, u32[]{:S(2)}) collective-permute-start(bf16[576,1024]{1,0:T(8,128)(2,1)} %copy-done.13), channel_id=1, source_target_pairs={{0,192},{16,208},{32,224},{48,240},{64,128},{80,144},{96,160},{112... | collective-permute-start | bytes 3538952 | tf_op jit(solution)/shard_map/ppermute | solution.py:306
  145.8 33.9 %collective-permute-start.15 = (bf16[576,1024]{1,0:T(8,128)(2,1)}, bf16[576,1024]{1,0:T(8,128)(2,1)}, u32[]{:S(2)}, u32[]{:S(2)}) collective-permute-start(bf16[576,1024]{1,0:T(8,128)(2,1)} %copy-done.12), channel_id=1, source_target_pairs={{0,16},{16,0},{32,48},{48,32},{64,80},{80,64},{96,112},{112,96},{1... | collective-permute-start | bytes 3538952 | tf_op jit(solution)/shard_map/ppermute | solution.py:306
  155.2 14.4 %copy-start.5 = (bf16[512,2048]{1,0:T(8,128)(2,1)S(1)}, bf16[512,2048]{1,0:T(8,128)(2,1)}, u32[]{:S(2)}) copy-start(bf16[512,2048]{1,0:T(8,128)(2,1)} %copy-done.4) | copy-start | bytes 6291460
  155.2 69.9 %all-to-all-start = ((bf16[16,32,2048]{2,1,0:T(8,128)(2,1)}), bf16[16,32,2048]{2,1,0:T(8,128)(2,1)}, u32[]{:S(2)}, u32[]{:S(2)}) async-start(bf16[16,32,2048]{2,1,0:T(8,128)(2,1)} %bitcast.84), calls=%async_computation | async-start | bytes 4194304 | tf_op jit(solution)/shard_map/all_to_all | solution.py:310
  161.8 30.3 %collective-permute-start.18 = (bf16[576,1024]{1,0:T(8,128)(2,1)S(1)}, bf16[576,1024]{1,0:T(8,128)(2,1)S(1)}, u32[]{:S(2)}, u32[]{:S(2)}) collective-permute-start(bf16[576,1024]{1,0:T(8,128)(2,1)S(1)} %get-tuple-element.34), channel_id=1, source_target_pairs={{0,48},{16,32},{32,16},{48,0},{64,112},{80,96},{96,80},{112,64},{1... | collective-permute-start | bytes 3538952 | tf_op jit(solution)/shard_map/ppermute | solution.py:306
  169.6 1.4 copy-start.11
  173.7 6.0 %copy-start.3 = (bf16[512,2048]{1,0:T(8,128)(2,1)S(1)}, bf16[512,2048]{1,0:T(8,128)(2,1)}, u32[]{:S(2)}) copy-start(bf16[512,2048]{1,0:T(8,128)(2,1)} %copy-done.2) | copy-start | bytes 6291460
  173.7 6.0 %copy-start.15 = (bf16[768,512]{1,0:T(8,128)(2,1)S(1)}, bf16[768,512]{1,0:T(8,128)(2,1)}, u32[]{:S(2)}) copy-start(bf16[768,512]{1,0:T(8,128)(2,1)} %copy-done.14) | copy-start | bytes 2359300
  173.8 20.5 %collective-permute-start.10 = (bf16[576,512]{1,0:T(8,128)(2,1)S(1)}, bf16[576,512]{1,0:T(8,128)(2,1)S(1)}, u32[]{:S(2)}, u32[]{:S(2)}) collective-permute-start(bf16[576,512]{1,0:T(8,128)(2,1)S(1)} %get-tuple-element.26), channel_id=1, source_target_pairs={{0,192},{16,208},{32,224},{48,240},{64,128},{80,144},{96,160},{112... | collective-permute-start | bytes 1769480 | tf_op jit(solution)/shard_map/ppermute | solution.py:323
  178.3 18.2 %collective-permute-start.13 = (bf16[576,512]{1,0:T(8,128)(2,1)S(1)}, bf16[576,512]{1,0:T(8,128)(2,1)S(1)}, u32[]{:S(2)}, u32[]{:S(2)}) collective-permute-start(bf16[576,512]{1,0:T(8,128)(2,1)S(1)} %get-tuple-element.29), channel_id=1, source_target_pairs={{0,64},{16,80},{32,96},{48,112},{64,0},{80,16},{96,32},{112,48},{1... | collective-permute-start | bytes 1769480 | tf_op jit(solution)/shard_map/ppermute | solution.py:323
  182.5 22.3 %collective-permute-start.16 = (bf16[576,512]{1,0:T(8,128)(2,1)S(1)}, bf16[576,512]{1,0:T(8,128)(2,1)S(1)}, u32[]{:S(2)}, u32[]{:S(2)}) collective-permute-start(bf16[576,512]{1,0:T(8,128)(2,1)S(1)} %get-tuple-element.33), channel_id=1, source_target_pairs={{0,48},{16,32},{32,16},{48,0},{64,112},{80,96},{96,80},{112,64},{1... | collective-permute-start | bytes 1769480 | tf_op jit(solution)/shard_map/ppermute | solution.py:323
  194.2 16.4 %collective-permute-start.19 = (bf16[576,512]{1,0:T(8,128)(2,1)S(1)}, bf16[576,512]{1,0:T(8,128)(2,1)S(1)}, u32[]{:S(2)}, u32[]{:S(2)}) collective-permute-start(bf16[576,512]{1,0:T(8,128)(2,1)S(1)} %get-tuple-element.36), channel_id=1, source_target_pairs={{0,16},{16,0},{32,48},{48,32},{64,80},{80,64},{96,112},{112,96},{1... | collective-permute-start | bytes 1769480 | tf_op jit(solution)/shard_map/ppermute | solution.py:323
  194.4 19.8 %collective-permute-start.11 = (bf16[576,256]{1,0:T(8,128)(2,1)S(1)}, bf16[576,256]{1,0:T(8,128)(2,1)S(1)}, u32[]{:S(2)}, u32[]{:S(2)}) collective-permute-start(bf16[576,256]{1,0:T(8,128)(2,1)S(1)} %get-tuple-element.49), channel_id=1, source_target_pairs={{0,16},{16,0},{32,48},{48,32},{64,80},{80,64},{96,112},{112,96},{1... | collective-permute-start | bytes 884744 | tf_op jit(solution)/shard_map/ppermute | solution.py:323
  196.7 19.9 %collective-permute-start.14 = (bf16[576,256]{1,0:T(8,128)(2,1)S(1)}, bf16[576,256]{1,0:T(8,128)(2,1)S(1)}, u32[]{:S(2)}, u32[]{:S(2)}) collective-permute-start(bf16[576,256]{1,0:T(8,128)(2,1)S(1)} %get-tuple-element.47), channel_id=1, source_target_pairs={{0,48},{16,32},{32,16},{48,0},{64,112},{80,96},{96,80},{112,64},{1... | collective-permute-start | bytes 884744 | tf_op jit(solution)/shard_map/ppermute | solution.py:323
  204.9 11.8 %collective-permute-start.17 = (bf16[576,256]{1,0:T(8,128)(2,1)S(1)}, bf16[576,256]{1,0:T(8,128)(2,1)S(1)}, u32[]{:S(2)}, u32[]{:S(2)}) collective-permute-start(bf16[576,256]{1,0:T(8,128)(2,1)S(1)} %get-tuple-element.45), channel_id=1, source_target_pairs={{0,64},{16,80},{32,96},{48,112},{64,0},{80,16},{96,32},{112,48},{1... | collective-permute-start | bytes 884744 | tf_op jit(solution)/shard_map/ppermute | solution.py:323
  210.7 7.5 %collective-permute-start.20 = (bf16[576,256]{1,0:T(8,128)(2,1)S(1)}, bf16[576,256]{1,0:T(8,128)(2,1)S(1)}, u32[]{:S(2)}, u32[]{:S(2)}) collective-permute-start(bf16[576,256]{1,0:T(8,128)(2,1)S(1)} %get-tuple-element.43), channel_id=1, source_target_pairs={{0,192},{16,208},{32,224},{48,240},{64,128},{80,144},{96,160},{112... | collective-permute-start | bytes 884744 | tf_op jit(solution)/shard_map/ppermute | solution.py:323
  214.3 6.7 %collective-permute-start.21 = (bf16[576,128]{1,0:T(8,128)(2,1)S(1)}, bf16[576,128]{1,0:T(8,128)(2,1)S(1)}, u32[]{:S(2)}, u32[]{:S(2)}) collective-permute-start(bf16[576,128]{1,0:T(8,128)(2,1)S(1)} %get-tuple-element.88), channel_id=1, source_target_pairs={{0,48},{16,32},{32,16},{48,0},{64,112},{80,96},{96,80},{112,64},{1... | collective-permute-start | bytes 442376 | tf_op jit(solution)/shard_map/ppermute | solution.py:323
  216.6 5.2 %collective-permute-start.22 = (bf16[576,128]{1,0:T(8,128)(2,1)S(1)}, bf16[576,128]{1,0:T(8,128)(2,1)S(1)}, u32[]{:S(2)}, u32[]{:S(2)}) collective-permute-start(bf16[576,128]{1,0:T(8,128)(2,1)S(1)} %get-tuple-element.86), channel_id=1, source_target_pairs={{0,16},{16,0},{32,48},{48,32},{64,80},{80,64},{96,112},{112,96},{1... | collective-permute-start | bytes 442376 | tf_op jit(solution)/shard_map/ppermute | solution.py:323
  216.8 5.2 %collective-permute-start.23 = (bf16[576,128]{1,0:T(8,128)(2,1)S(1)}, bf16[576,128]{1,0:T(8,128)(2,1)S(1)}, u32[]{:S(2)}, u32[]{:S(2)}) collective-permute-start(bf16[576,128]{1,0:T(8,128)(2,1)S(1)} %get-tuple-element.84), channel_id=1, source_target_pairs={{0,192},{16,208},{32,224},{48,240},{64,128},{80,144},{96,160},{112... | collective-permute-start | bytes 442376 | tf_op jit(solution)/shard_map/ppermute | solution.py:323
  218.2 9.9 %copy-start.1 = (bf16[1,2048,768]{2,1,0:T(8,128)(2,1)S(1)}, bf16[1,2048,768]{2,1,0:T(8,128)(2,1)}, u32[]{:S(2)}) copy-start(bf16[1,2048,768]{2,1,0:T(8,128)(2,1)} %param.10) | copy-start | bytes 9437188
  218.3 5.8 %collective-permute-start.24 = (bf16[576,128]{1,0:T(8,128)(2,1)S(1)}, bf16[576,128]{1,0:T(8,128)(2,1)S(1)}, u32[]{:S(2)}, u32[]{:S(2)}) collective-permute-start(bf16[576,128]{1,0:T(8,128)(2,1)S(1)} %get-tuple-element.82), channel_id=1, source_target_pairs={{0,64},{16,80},{32,96},{48,112},{64,0},{80,16},{96,32},{112,48},{1... | collective-permute-start | bytes 442376 | tf_op jit(solution)/shard_map/ppermute | solution.py:323

commit v2 on v1

v2 whole, which is shorter than its diff:
```python
import jax
import jax.numpy as jnp
from jax import lax
from jax.experimental import pallas as pl
from jax.experimental.pallas import tpu as pltpu
from jax.sharding import PartitionSpec as P

SLOTS = 32
SIDE = 4
LANE = 128
GIVE_MIB = 40
CHUNKS = 4
FLOWS = ((0, False), (0, True), (1, False), (1, True))
FINISH = pl.CostEstimate(flops=5000000000, bytes_accessed=100000, transcendentals=0)
SMALL = pl.CostEstimate(flops=1000000, bytes_accessed=100000, transcendentals=0)


def pack_kernel(ids_ref, values_ref, out_ref, target_ref):
    ids = ids_ref[...]
    tokens = ids.shape[1]
    experts = out_ref.shape[0] // SLOTS
    mine = (lax.broadcasted_iota(jnp.int32, (experts, tokens), 0) == ids).astype(jnp.float32)
    earlier = lax.broadcasted_iota(jnp.int32, (tokens, tokens), 0) < lax.broadcasted_iota(
        jnp.int32, (tokens, tokens), 1
    )
    before = dot32(mine.astype(jnp.bfloat16), earlier.astype(jnp.bfloat16))
    slots = jnp.sum(before * mine, axis=0, keepdims=True).astype(jnp.int32)
    target = ids * SLOTS + slots
    target_ref[...] = target
    spots = lax.broadcasted_iota(jnp.int32, (out_ref.shape[0], tokens), 0)
    out_ref[...] = product((spots == target).astype(jnp.bfloat16), values_ref[...])


def pack(ids, values, experts):
    tokens, width = values.shape
    tile = 512
    return pl.pallas_call(
        pack_kernel,
        grid=(width // tile,),
        in_specs=[
            pl.BlockSpec((1, tokens), lambda i: (0, 0)),
            pl.BlockSpec((tokens, tile), lambda i: (0, i)),
        ],
        out_specs=[
            pl.BlockSpec((experts * SLOTS, tile), lambda i: (0, i)),
            pl.BlockSpec((1, tokens), lambda i: (0, 0)),
        ],
        out_shape=[
            jax.ShapeDtypeStruct((experts * SLOTS, width), jnp.bfloat16),
            jax.ShapeDtypeStruct((1, tokens), jnp.int32),
        ],
        compiler_params=pltpu.CompilerParams(vmem_limit_bytes=56 * 1024 * 1024),
        cost_estimate=SMALL,
        name="pack",
    )(ids, values)


def feature_blocks(ref, table, f, chunk):
    pair = [
        ref[:, pl.ds(pl.multiple_of(table[f, 2 * chunk + k] * LANE, LANE), LANE)] for k in range(2)
    ]
    return jnp.concatenate(pair, axis=1)


def lanes(chunk):
    return pl.ds(pl.multiple_of(chunk * (2 * LANE), 2 * LANE), 2 * LANE)


def dot32(left, right):
    return jnp.dot(left, right, preferred_element_type=jnp.float32)


def product(left, right):
    return dot32(left, right).astype(jnp.bfloat16)


def flow_parts(f, per, split):
    low, high = f * per, (f + 1) * per
    parts = []
    if low < split:
        parts.append((True, low, min(high, split) - low, 0))
    if high > split:
        begin = max(low, split)
        parts.append((False, begin - split, high - begin, begin - low))
    return parts


def gives_kernel(table, w_ref, hid_ref, x_ref, slope_in, silu_in, dy_in, dgu_ref, dy_ref, *refs):
    n = len(FLOWS)
    outs, stages, (slope_ref, silu_ref, sems, in_sems) = refs[:n], refs[n : 2 * n], refs[2 * n :]
    per = outs[0].shape[0]
    ff = hid_ref.shape[0]
    tile = 256
    part = dy_in.shape[0] // 4
    arrivals = [
        pltpu.make_async_copy(dy_in.at[pl.ds(k * part, part)], dy_ref.at[pl.ds(k * part, part)], in_sems.at[k])
        for k in range(4)
    ]
    factors = [
        pltpu.make_async_copy(slope_in, slope_ref, in_sems.at[4]),
        pltpu.make_async_copy(silu_in, silu_ref, in_sems.at[5]),
    ]
    for copy in arrivals + factors:
        copy.start()
    for copy in arrivals:
        copy.wait()

    def copy(f, chunk):
        return pltpu.make_async_copy(
            stages[f].at[:, lanes(chunk)], outs[f].at[:, lanes(chunk)], sems.at[f, chunk]
        )

    def give(f):
        def body(chunk, carry):
            for from_dgu, first, count, row in flow_parts(f, per, 2 * ff):
                left, right = (dgu_ref, x_ref) if from_dgu else (hid_ref, dy_ref)
                stages[f][row : row + count, lanes(chunk)] = product(
                    left[first : first + count, :], feature_blocks(right, table, f, chunk)
                )
            copy(f, chunk).start()
            return carry

        lax.fori_loop(0, CHUNKS, body, 0, unroll=True)

    give(3)
    for copy_in in factors:
        copy_in.wait()
    for low in range(0, ff, tile):
        here = slice(low, low + tile)
        dhidden = lax.dot_general(
            w_ref[here, :], dy_ref[...], (((1,), (1,)), ((), ())), preferred_element_type=jnp.float32
        )
        dgu_ref[here, :] = (dhidden * slope_ref[here, :]).astype(jnp.bfloat16)
        dgu_ref[ff + low : ff + low + tile, :] = (dhidden * silu_ref[here, :]).astype(jnp.bfloat16)
    for f in range(3):
        give(f)
    for f in range(n):
        for chunk in range(CHUNKS):
            copy(f, chunk).wait()


def make_gives(table, w_out_t, slope, silu, hidden, rows_x, rows_dy):
    ff, rows = hidden.shape
    size = (3 * ff // 4, 2 * CHUNKS * LANE)
    whole = pl.BlockSpec(memory_space=pltpu.VMEM)
    away = pl.BlockSpec(memory_space=pl.ANY)
    n = len(FLOWS)
    return pl.pallas_call(
        gives_kernel,
        in_specs=[pl.BlockSpec(memory_space=pltpu.SMEM)] + [whole] * 3 + [away] * 3,
        out_specs=[whole] * 2 + [away] * n,
        out_shape=[
            jax.ShapeDtypeStruct((2 * ff, rows), jnp.bfloat16),
            jax.ShapeDtypeStruct(rows_dy.shape, jnp.bfloat16),
        ]
        + [jax.ShapeDtypeStruct(size, jnp.bfloat16)] * n,
        scratch_shapes=[pltpu.VMEM(size, jnp.bfloat16)] * n
        + [pltpu.VMEM((ff, rows), jnp.float32)] * 2
        + [pltpu.SemaphoreType.DMA((n, CHUNKS)), pltpu.SemaphoreType.DMA((6,))],
        compiler_params=pltpu.CompilerParams(vmem_limit_bytes=GIVE_MIB * 1024 * 1024),
        cost_estimate=SMALL,
        name="give",
    )(table, w_out_t, hidden, rows_x, slope, silu, rows_dy)


def keeps_kernel(table, dgu_ref, hid_ref, x_ref, dy_ref, *outs):
    per = outs[0].shape[0]
    for f, out in enumerate(outs):

        def body(chunk, carry):
            for from_dgu, first, count, row in flow_parts(f, per, dgu_ref.shape[0]):
                left, right = (dgu_ref, x_ref) if from_dgu else (hid_ref, dy_ref)
                out[row : row + count, lanes(chunk)] = product(
                    left[first : first + count, :], feature_blocks(right, table, f, chunk)
                )
            return carry

        lax.fori_loop(0, CHUNKS, body, 0, unroll=True)


def make_keeps(table, dgu, hidden, rows_x, rows_dy):
    size = (3 * hidden.shape[0] // 4, 2 * CHUNKS * LANE)
    whole = pl.BlockSpec(memory_space=pltpu.VMEM)
    n = len(FLOWS)
    return pl.pallas_call(
        keeps_kernel,
        in_specs=[pl.BlockSpec(memory_space=pltpu.SMEM)] + [whole] * 4,
        out_specs=[whole] * n,
        out_shape=[jax.ShapeDtypeStruct(size, jnp.bfloat16)] * n,
        compiler_params=pltpu.CompilerParams(vmem_limit_bytes=8 * 1024 * 1024),
        cost_estimate=SMALL,
        name="keep",
    )(table, dgu, hidden, rows_x, rows_dy)


def drows_kernel(g_ref, w_ref, out_ref, turned):
    @pl.when(pl.program_id(0) == 0)
    def _():
        turned[...] = g_ref[...].T

    out_ref[...] = lax.dot_general(
        turned[...], w_ref[...], (((1,), (1,)), ((), ())), preferred_element_type=jnp.float32
    ).astype(jnp.bfloat16)


def make_drows(dgu_t, w_in):
    ff2, rows = dgu_t.shape
    width = w_in.shape[0]
    tile = 512
    return pl.pallas_call(
        drows_kernel,
        grid=(width // tile,),
        in_specs=[
            pl.BlockSpec((ff2, rows), lambda i: (0, 0)),
            pl.BlockSpec((tile, ff2), lambda i: (i, 0)),
        ],
        out_specs=pl.BlockSpec((rows, tile), lambda i: (0, i)),
        out_shape=jax.ShapeDtypeStruct((rows, width), jnp.bfloat16),
        scratch_shapes=[pltpu.VMEM((rows, ff2), jnp.bfloat16)],
        compiler_params=pltpu.CompilerParams(vmem_limit_bytes=16 * 1024 * 1024),
        cost_estimate=SMALL,
        name="drows",
    )(dgu_t, w_in)


def finish_kernel(*refs):
    *parts, up_ref, down_ref = refs
    n = len(parts) // 2
    total = jnp.concatenate(
        [parts[i][...].astype(jnp.float32) + parts[n + i][...].astype(jnp.float32) for i in range(n)], axis=0
    )
    split = up_ref.shape[1]
    up_ref[...] = total[:split].T.astype(jnp.bfloat16)
    down_ref[...] = total[split:].T.astype(jnp.bfloat16)


def finish(keeps, gots):
    per, lane = keeps[0].shape
    whole = pl.BlockSpec(memory_space=pltpu.VMEM)
    return pl.pallas_call(
        finish_kernel,
        in_specs=[whole] * 8,
        out_specs=[whole] * 2,
        out_shape=[
            jax.ShapeDtypeStruct((lane, 8 * per // 3), jnp.bfloat16),
            jax.ShapeDtypeStruct((lane, 4 * per // 3), jnp.bfloat16),
        ],
        compiler_params=pltpu.CompilerParams(vmem_limit_bytes=12 * 1024 * 1024),
        cost_estimate=FINISH,
        name="finish",
    )(*keeps, *gots)


def mate(i, odd):
    return (3 - i) if odd else (i ^ 1)


def pair_perm(axis, odd):
    return [
        (x * SIDE + y, mate(x, odd) * SIDE + y if axis == 0 else x * SIDE + mate(y, odd))
        for x in range(SIDE)
        for y in range(SIDE)
    ]


def first_table(at, axis, odd):
    a, b = at[axis], at[1 - axis]

    def kept(i):
        return [mate(i, not odd), i]

    minor = jnp.stack(kept(mate(b, odd)) + kept(b)).astype(jnp.int32)

    def blocks(i):
        major = jnp.stack(kept(i)).astype(jnp.int32)
        ids = major[:, None] * SIDE + minor[None, :] if axis == 0 else minor[None, :] * SIDE + major[:, None]
        return ids.reshape(-1)

    return blocks(mate(a, odd)), blocks(a)


def local(tokens, out_grads, expert_ids, w_gate_up, w_down_t):
    num_experts = lax.axis_size("expert")
    width = tokens.shape[1]
    ff = w_down_t.shape[2]
    rows = num_experts * SLOTS
    ids = expert_ids.reshape(1, -1)

    def send(packed):
        packed = packed.reshape(num_experts, SLOTS, width)
        got = lax.all_to_all(packed, "expert", split_axis=0, concat_axis=0, tiled=True)
        return got.reshape(rows, width)

    packed_x, target = pack(ids, tokens, num_experts)
    packed_dy, _ = pack(ids, out_grads, num_experts)
    rows_x = send(packed_x)
    rows_x, packed_dy = lax.optimization_barrier((rows_x, packed_dy))
    rows_dy = send(packed_dy)
    w_in = w_gate_up[0]
    w_out_t = w_down_t[0].T

    gate_up = lax.dot_general(
        w_in, rows_x, (((0,), (1,)), ((), ())), preferred_element_type=jnp.float32
    )
    gate = gate_up[:ff]
    upper = gate_up[ff:]
    sig = jax.nn.sigmoid(gate)
    silu = gate * sig
    hidden = (silu * upper).astype(jnp.bfloat16)
    slope = upper * sig * (1.0 + gate * (1.0 - sig))

    me = lax.axis_index("dp")
    at = (me // SIDE, me % SIDE)
    tables = [first_table(at, axis, odd) for axis, odd in FLOWS]

    to_give = jnp.stack([t[0] for t in tables])
    to_keep = jnp.stack([t[1] for t in tables])
    dgu, rows_dy, *gives = make_gives(to_give, w_out_t, slope, silu, hidden, rows_x, rows_dy)
    gots = [None] * 4
    for f in (3, 0, 1, 2):
        gots[f] = lax.ppermute(gives[f], "dp", pair_perm(*FLOWS[f]))
    drows = make_drows(dgu, w_in)
    returned = lax.all_to_all(
        drows.reshape(num_experts, SLOTS, width), "expert", split_axis=0, concat_axis=0, tiled=True
    ).reshape(rows, width)
    spots = jnp.arange(rows, dtype=jnp.int32)
    token_grads = lax.dot_general(
        (spots[:, None] == target).astype(jnp.bfloat16), returned, (((0,), (0,)), ((), ())),
        preferred_element_type=jnp.float32,
    ).astype(jnp.bfloat16)

    def add_halves(keep, got):
        n = keep.shape[1] // 2
        return tuple(
            (k.astype(jnp.float32) + g.astype(jnp.float32)).astype(jnp.bfloat16)
            for k, g in ((keep[:, :n], got[:, :n]), (keep[:, n:], got[:, n:]))
        )

    keeps = make_keeps(to_keep, dgu, hidden, rows_x, rows_dy)
    halves = [add_halves(keep, got) for keep, got in zip(keeps, gots)]
    for step in range(1, 4):
        for f, (first_axis, first_odd) in enumerate(FLOWS):
            axis = first_axis if step < 2 else 1 - first_axis
            odd = first_odd if step % 2 == 0 else not first_odd
            give, keep = halves[f]
            got = lax.ppermute(give, "dp", pair_perm(axis, odd))
            halves[f] = (got, keep) if step == 3 else add_halves(keep, got)
    grad_gate_up, grad_down_t = finish([h[1] for h in halves], [h[0] for h in halves])
    return (token_grads, grad_gate_up[None], grad_down_t[None])


def solution(mesh):
    return jax.shard_map(
        local,
        mesh=mesh,
        in_specs=(
            P(("dp", "expert"), None),
            P(("dp", "expert"), None),
            P(("dp", "expert"), None),
            P("expert", None, None),
            P("expert", None, None),
        ),
        out_specs=(P(("dp", "expert"), None), P("expert", "dp", None), P("expert", "dp", None)),
        check_vma=False,
    )
```

time: 230 us -> 206 us (0.90)
  matrix products: 24.1 us -> 8.59 us
  starting transfers between devices: 51.9 us -> 38.7 us
  Pallas kernels: 24 us -> 27.3 us
  waiting for transfers between devices: 100 us -> 103 us
    all_to_all x0 -> x2, waiting for transfers between devices: none -> 79.9 us  [send(): lax.all_to_all(packed, 'expert', split_axis=0, concat_axis=0, tiled=True)]
    ppermute x9 -> x0, waiting for transfers between devices: 71.2 us -> none  [the longest x7 71.2 us: local(): lax.ppermute(piece(d), 'expert', [(i, (i + 2 * d) % num_experts) for i in...]
    ppermute x9 -> x0, starting transfers between devices: 20.1 us -> none  [the longest x7 19.6 us: local(): lax.ppermute(piece(d), 'expert', [(i, (i + 2 * d) % num_experts) for i in...]
    dot_general x7 -> x1, matrix products: 20.5 us -> 2.99 us  [local(): lax.dot_general((spots[:, None] == target).astype(jnp.bfloat16), returned...]
    all_to_all x0 -> x2, starting transfers between devices: none -> 13.4 us  [send(): lax.all_to_all(packed, 'expert', split_axis=0, concat_axis=0, tiled=True)]
    ppermute x4, waiting for transfers between devices: 11.2 us -> 1.61 us  [local(): gots[f] = lax.ppermute(gives[f], 'dp', pair_perm(*FLOWS[f]))]
    convert_element_type x8 -> x12, other arithmetic: 0.99 us -> 7.24 us  [add_halves(): (k.astype(jnp.float32) + g.astype(jnp.float32)).astype(jnp.bfloat16)]
    unnamed x46 -> x19, local copies, waits for them, and re-layouts: 9.38 us -> 14.7 us
  transfers between devices with their start and end apart: 26 -> 19, of which waited for: 15 -> 11; matrix products, arithmetic and copies ran while one was open for 12% -> 11% of each run, Pallas kernels for 5% -> 7%
where the time goes in v2:
time: 206 us; the launch traced here: 205 us
  waiting for transfers between devices  103 us (50%)
  starting transfers between devices  38.7 us (19%)
  Pallas kernels  27.3 us (13%)
  local copies, waits for them, and re-layouts  15.3 us (7%)
  other arithmetic  10.6 us (5%)
  matrix products  8.59 us (4%)
    all_to_all x2, waiting for transfers between devices, send(): lax.all_to_all(packed, 'expert', split_axis=0, concat_axis=0, tiled=True)  79.9 us
    ppermute x12, waiting for transfers between devices, local(): got = lax.ppermute(give, 'dp', pair_perm(axis, odd))  21.8 us
    unnamed x19, local copies, waits for them, and re-layouts  14.7 us
    ppermute x12, starting transfers between devices, local(): got = lax.ppermute(give, 'dp', pair_perm(axis, odd))  14.1 us
    all_to_all x2, starting transfers between devices, send(): lax.all_to_all(packed, 'expert', split_axis=0, concat_axis=0, tiled=True)  13.4 us
    pallas_call x1, Pallas kernels, make_gives(): pl.pallas_call(gives_kernel, in_specs=[pl.BlockSpec(memory_space=pltpu.SM...  9.48 us
    pallas_call x2, Pallas kernels, pack(): pl.pallas_call(pack_kernel, grid=(width // tile,), in_specs=[pl.BlockSpec...  8.82 us
    convert_element_type x12, other arithmetic, add_halves(): (k.astype(jnp.float32) + g.astype(jnp.float32)).astype(jnp.bfloat16)  7.24 us
  transfers between devices with their start and end apart: 19, of which 11 were waited for; matrix products, arithmetic and copies ran while one was open for 11% of the time, Pallas kernels for 7%

profile of v2, /device:TPU:2, one launch (start us, length us, event | category | flops | bytes accessed | tf_op | source)
XLA Modules:
  0.0 204.8 jit_solution(5804890812787710922)
XLA Ops:
  0.6 4.4 %pack.2 = (bf16[512,2048]{1,0:T(8,128)(2,1)}, s32[1,160]{1,0:T(1,128)}) custom-call(s32[1,160]{1,0:T(1,128)} %bitcast.38, bf16[160,2048]{1,0:T(8,128)(2,1)} %values_ref.2), custom_call_target="tpu_custom_call" | custom-call | flops 1000000 | bytes 100000 | tf_op jit(solution)/shard_map/pack/pallas_call | solution.py:37
  5.0 8.6 %all-to-all-start = ((bf16[16,32,2048]{2,1,0:T(8,128)(2,1)}), bf16[16,32,2048]{2,1,0:T(8,128)(2,1)S(1)}, u32[]{:S(2)}, u32[]{:S(2)}) async-start(bf16[16,32,2048]{2,1,0:T(8,128)(2,1)} %bitcast.37), calls=%async_computation | async-start | bytes 4194304 | tf_op jit(solution)/shard_map/all_to_all | solution.py:291
  13.6 4.4 %pack.3 = (bf16[512,2048]{1,0:T(8,128)(2,1)}, s32[1,160]{1,0:T(1,128)}) custom-call(s32[1,160]{1,0:T(1,128)} %bitcast.39, bf16[160,2048]{1,0:T(8,128)(2,1)} %values_ref.3), custom_call_target="tpu_custom_call" | custom-call | flops 1000000 | bytes 100000 | tf_op jit(solution)/shard_map/pack/pallas_call | solution.py:37
  18.0 44.8 %all-to-all-done = bf16[16,32,2048]{2,1,0:T(8,128)(2,1)S(1)} async-done(((bf16[16,32,2048]{2,1,0:T(8,128)(2,1)}), bf16[16,32,2048]{2,1,0:T(8,128)(2,1)S(1)}, u32[]{:S(2)}, u32[]{:S(2)}) %all-to-all-start) | async-done | bytes 2097184 | tf_op jit(solution)/shard_map/all_to_all | solution.py:291
  62.8 4.8 %all-to-all-start.1 = ((bf16[16,32,2048]{2,1,0:T(8,128)(2,1)}), bf16[16,32,2048]{2,1,0:T(8,128)(2,1)}, u32[]{:S(2)}, u32[]{:S(2)}) async-start(bf16[16,32,2048]{2,1,0:T(8,128)(2,1)} %bitcast.36), calls=%async_computation.1 | async-start | bytes 4194304 | tf_op jit(solution)/shard_map/all_to_all | solution.py:291
  67.9 0.1 add.263
  68.3 0.1 add.275
  68.5 0.1 add.267
  68.6 0.1 add.271
  68.7 4.7 %copy.8 = bf16[1,2048,768]{1,2,0:T(8,128)(2,1)} copy(bf16[1,2048,768]{2,1,0:T(8,128)(2,1)} %param.9) | data formatting | bytes 6291456 | tf_op args[4]
  73.4 5.6 %convolution_bitcast_fusion = f32[1536,512]{1,0:T(8,128)S(1)} fusion(bf16[512,2048]{1,0:T(8,128)(2,1)S(1)} %bitcast.30, bf16[1,2048,1536]{2,1,0:T(8,128)(2,1)} %param.8), kind=kOutput, calls=%fused_computation | convolution fusion | flops 3221225472 | bytes 11534336 | tf_op jit(solution)/shard_map/dot_general | solution.py:302
  79.0 2.6 %fusion = (f32[768,512]{1,0:T(8,128)}, f32[768,512]{1,0:T(8,128)}, bf16[768,512]{1,0:T(8,128)(2,1)S(1)}) fusion(f32[1536,512]{1,0:T(8,128)S(1)} %convolution_bitcast_fusion), kind=kLoop, calls=%fused_computation.5 | loop fusion | flops 4325376 | bytes 7077888 | tf_op jit(solution)/shard_map/mul | solution.py:308
  81.6 35.2 %all-to-all-done.1 = bf16[16,32,2048]{2,1,0:T(8,128)(2,1)} async-done(((bf16[16,32,2048]{2,1,0:T(8,128)(2,1)}), bf16[16,32,2048]{2,1,0:T(8,128)(2,1)}, u32[]{:S(2)}, u32[]{:S(2)}) %all-to-all-start.1) | async-done | bytes 2097184 | tf_op jit(solution)/shard_map/all_to_all | solution.py:291
  116.8 1.4 copy-done.1
  118.2 1.4 copy-done.2
  119.6 9.5 %give.1 = (bf16[1536,512]{1,0:T(8,128)(2,1)S(1)}, bf16[512,2048]{1,0:T(8,128)(2,1)S(1)}, bf16[576,1024]{1,0:T(8,128)(2,1)}, bf16[576,1024]{1,0:T(8,128)(2,1)}, b...) custom-call(s32[4,8]{1,0:T(4,128)S(1)} %pad_add_fusion.table, bf16[768,2048]{1,0:T(8,128)(2,1)} %bitcast.35, ...), custom_call_target="tpu_custom_call" | custom-call | flops 1000000 | bytes 100000 | tf_op jit(solution)/shard_map/give/pallas_call | solution.py:148
  129.2 0.6 collective-permute-start
  129.8 2.2 %collective-permute-start.3 = (bf16[576,1024]{1,0:T(8,128)(2,1)}, bf16[576,1024]{1,0:T(8,128)(2,1)}, u32[]{:S(2)}, u32[]{:S(2)}) collective-permute-start(bf16[576,1024]{1,0:T(8,128)(2,1)} %get-tuple-element.30), channel_id=1, source_target_pairs={{0,192},{16,208},{32,224},{48,240},{64,128},{80,144},{96,160},{112... | collective-permute-start | bytes 3538952 | tf_op jit(solution)/shard_map/ppermute | solution.py:321
  131.9 1.6 collective-permute-start.6
  133.5 2.2 %collective-permute-start.9 = (bf16[576,1024]{1,0:T(8,128)(2,1)}, bf16[576,1024]{1,0:T(8,128)(2,1)}, u32[]{:S(2)}, u32[]{:S(2)}) collective-permute-start(bf16[576,1024]{1,0:T(8,128)(2,1)} %get-tuple-element.34), channel_id=1, source_target_pairs={{0,48},{16,32},{32,16},{48,0},{64,112},{80,96},{96,80},{112,64},{1... | collective-permute-start | bytes 3538952 | tf_op jit(solution)/shard_map/ppermute | solution.py:321
  135.7 2.8 %copy-done.3 = bf16[1,2048,1536]{2,1,0:T(8,128)(2,1)S(1)} copy-done((bf16[1,2048,1536]{2,1,0:T(8,128)(2,1)S(1)}, bf16[1,2048,1536]{2,1,0:T(8,128)(2,1)}, u32[]{:S(2)}) %copy-start.3) | copy-done | bytes 6291480
  138.5 4.6 %drows.1 = bf16[512,2048]{1,0:T(8,128)(2,1)S(1)} custom-call(bf16[1536,512]{1,0:T(8,128)(2,1)S(1)} %get-tuple-element.25.g_ref.dgu_ref, bf16[2048,1536]{1,0:T(8,128)(2,1)S(1)} %bitcast.34), custom_call_target="tpu_custom_call" | custom-call | flops 1000000 | bytes 100000 | tf_op jit(solution)/shard_map/drows/pallas_call | solution.py:210
  143.1 1.4 copy-done
  144.5 4.8 %all-to-all-start.2 = ((bf16[16,32,2048]{2,1,0:T(8,128)(2,1)}), bf16[16,32,2048]{2,1,0:T(8,128)(2,1)}, u32[]{:S(2)}, u32[]{:S(2)}) async-start(bf16[16,32,2048]{2,1,0:T(8,128)(2,1)} %bitcast.33), calls=%async_computation.2 | async-start | bytes 4194304 | tf_op jit(solution)/shard_map/all_to_all | solution.py:323
  149.3 0.1 add.280
  149.4 0.1 add.289
  149.4 0.1 add.283
  149.5 0.1 add.286
  149.6 1.4 copy-done.5
  151.0 1.6 copy-done.7
  152.6 3.4 %keep.1 = (bf16[576,1024]{1,0:T(8,128)(2,1)S(1)}, bf16[576,1024]{1,0:T(8,128)(2,1)S(1)}, bf16[576,1024]{1,0:T(8,128)(2,1)S(1)}, bf16[576,1024]{1,0:T(8,128)(2,1)S(1)}) custom-call(s32[4,8]{1,0:T(4,128)S(1)} %pad_add_fusion.1.table, bf16[1536,512]{1,0:T(8,128)(2,1)S(1)} %copy-done.5, bf16[768,512]{1,0:T(8,128)(2,1)S(1)} %get-tuple-element.39.hid_ref, ...), custom_call_target="tpu_custom_call" | custom-call | flops 1000000 | bytes 100000 | tf_op jit(solution)/shard_map/keep/pallas_call | solution.py:185
  156.0 1.6 collective-permute-done
  157.6 1.6 add_convert_fusion.7
  159.2 1.6 collective-permute-start.1
  160.8 1.6 add_convert_fusion.5
  162.4 1.9 collective-permute-start.4
  164.3 1.6 add_convert_fusion.3
  165.8 3.1 %collective-permute-start.7 = (bf16[576,512]{1,0:T(8,128)(2,1)S(1)}, bf16[576,512]{1,0:T(8,128)(2,1)S(1)}, u32[]{:S(2)}, u32[]{:S(2)}) collective-permute-start(bf16[576,512]{1,0:T(8,128)(2,1)S(1)} %get-tuple-element.43), channel_id=1, source_target_pairs={{0,48},{16,32},{32,16},{48,0},{64,112},{80,96},{96,80},{112,64},{1... | collective-permute-start | bytes 1769480 | tf_op jit(solution)/shard_map/ppermute | solution.py:346
  169.0 1.6 add_convert_fusion.1
  170.6 0.2 collective-permute-start.10
  170.7 3.1 %collective-permute-done.1 = bf16[576,512]{1,0:T(8,128)(2,1)S(1)} collective-permute-done((bf16[576,512]{1,0:T(8,128)(2,1)S(1)}, bf16[576,512]{1,0:T(8,128)(2,1)S(1)}, u32[]{:S(2)}, u32[]{:S(2)}) %collective-permute-start.1) | collective-permute-done | bytes 589856 | tf_op jit(solution)/shard_map/ppermute | solution.py:346
  173.9 0.1 add_convert_fusion.15
  174.0 1.7 collective-permute-start.2
  175.7 1.1 collective-permute-done.4
  176.8 0.1 add_convert_fusion.13
  177.0 3.1 %collective-permute-start.5 = (bf16[576,256]{1,0:T(8,128)(2,1)S(1)}, bf16[576,256]{1,0:T(8,128)(2,1)S(1)}, u32[]{:S(2)}, u32[]{:S(2)}) collective-permute-start(bf16[576,256]{1,0:T(8,128)(2,1)S(1)} %get-tuple-element.53), channel_id=1, source_target_pairs={{0,48},{16,32},{32,16},{48,0},{64,112},{80,96},{96,80},{112,64},{1... | collective-permute-start | bytes 884744 | tf_op jit(solution)/shard_map/ppermute | solution.py:346
  180.1 3.0 %collective-permute-done.7 = bf16[576,512]{1,0:T(8,128)(2,1)S(1)} collective-permute-done((bf16[576,512]{1,0:T(8,128)(2,1)S(1)}, bf16[576,512]{1,0:T(8,128)(2,1)S(1)}, u32[]{:S(2)}, u32[]{:S(2)}) %collective-permute-start.7) | collective-permute-done | bytes 589856 | tf_op jit(solution)/shard_map/ppermute | solution.py:346
  183.2 0.1 add_convert_fusion.11
  183.3 0.1 collective-permute-start.8
  183.4 3.5 %collective-permute-done.10 = bf16[576,512]{1,0:T(8,128)(2,1)S(1)} collective-permute-done((bf16[576,512]{1,0:T(8,128)(2,1)S(1)}, bf16[576,512]{1,0:T(8,128)(2,1)S(1)}, u32[]{:S(2)}, u32[]{:S(2)}) %collective-permute-start.10) | collective-permute-done | bytes 589856 | tf_op jit(solution)/shard_map/ppermute | solution.py:346
  186.9 0.1 add_convert_fusion.9
  187.1 0.1 collective-permute-start.11
  187.2 3.6 %collective-permute-done.2 = bf16[576,256]{1,0:T(8,128)(2,1)S(1)} collective-permute-done((bf16[576,256]{1,0:T(8,128)(2,1)S(1)}, bf16[576,256]{1,0:T(8,128)(2,1)S(1)}, u32[]{:S(2)}, u32[]{:S(2)}) %collective-permute-start.2) | collective-permute-done | bytes 294944 | tf_op jit(solution)/shard_map/ppermute | solution.py:346
  190.7 0.1 add_convert_fusion.19
  190.8 0.4 collective-permute-start.12
  191.2 0.1 add_convert_fusion.18
  191.3 0.3 collective-permute-start.13
  191.7 0.1 collective-permute-start.14
  191.8 3.7 %collective-permute-done.11 = bf16[576,256]{1,0:T(8,128)(2,1)S(1)} collective-permute-done((bf16[576,256]{1,0:T(8,128)(2,1)S(1)}, bf16[576,256]{1,0:T(8,128)(2,1)S(1)}, u32[]{:S(2)}, u32[]{:S(2)}) %collective-permute-start.11) | collective-permute-done | bytes 294944 | tf_op jit(solution)/shard_map/ppermute | solution.py:346
  195.5 1.5 collective-permute-start.15
  197.0 0.2 collective-permute-done.12.refs_4_
  197.3 3.5 %collective-permute-done.15.refs_7_ = bf16[576,128]{1,0:T(8,128)(2,1)S(1)} collective-permute-done((bf16[576,128]{1,0:T(8,128)(2,1)S(1)}, bf16[576,128]{1,0:T(8,128)(2,1)S(1)}, u32[]{:S(2)}, u32[]{:S(2)}) %collective-permute-start.15) | collective-permute-done | bytes 147488 | tf_op jit(solution)/shard_map/ppermute | solution.py:346
  200.8 1.0 finish.1
  201.8 3.0 %convolution_convert_fusion = bf16[160,2048]{1,0:T(8,128)(2,1)} fusion(bf16[512,2048]{1,0:T(8,128)(2,1)} %bitcast.21, s32[160]{0:T(256)S(1)} %bitcast.40), kind=kOutput, calls=%fused_computation.1 | convolution fusion | flops 335953920 | bytes 2753152 | tf_op jit(solution)/shard_map/dot_general | solution.py:327
  (34 shorter events, 1.0 us)
Async XLA Ops:
  5.0 57.8 %all-to-all-start = ((bf16[16,32,2048]{2,1,0:T(8,128)(2,1)}), bf16[16,32,2048]{2,1,0:T(8,128)(2,1)S(1)}, u32[]{:S(2)}, u32[]{:S(2)}) async-start(bf16[16,32,2048]{2,1,0:T(8,128)(2,1)} %bitcast.37), calls=%async_computation | async-start | bytes 4194304 | tf_op jit(solution)/shard_map/all_to_all | solution.py:291
  62.8 54.0 %all-to-all-start.1 = ((bf16[16,32,2048]{2,1,0:T(8,128)(2,1)}), bf16[16,32,2048]{2,1,0:T(8,128)(2,1)}, u32[]{:S(2)}, u32[]{:S(2)}) async-start(bf16[16,32,2048]{2,1,0:T(8,128)(2,1)} %bitcast.36), calls=%async_computation.1 | async-start | bytes 4194304 | tf_op jit(solution)/shard_map/all_to_all | solution.py:291
  116.8 1.4 copy-start.1
  118.2 1.4 copy-start.2
  129.1 14.0 %copy-start.4 = (bf16[1536,512]{1,0:T(8,128)(2,1)}, bf16[1536,512]{1,0:T(8,128)(2,1)S(1)}, u32[]{:S(2)}) copy-start(bf16[1536,512]{1,0:T(8,128)(2,1)S(1)} %get-tuple-element.25.g_ref.dgu_ref) | copy-start | bytes 4718596
  129.1 14.0 %copy-start.6 = (bf16[512,2048]{1,0:T(8,128)(2,1)}, bf16[512,2048]{1,0:T(8,128)(2,1)S(1)}, u32[]{:S(2)}) copy-start(bf16[512,2048]{1,0:T(8,128)(2,1)S(1)} %get-tuple-element.26.dy_ref) | copy-start | bytes 6291460
  129.2 28.5 %collective-permute-start = (bf16[576,1024]{1,0:T(8,128)(2,1)}, bf16[576,1024]{1,0:T(8,128)(2,1)}, u32[]{:S(2)}, u32[]{:S(2)}) collective-permute-start(bf16[576,1024]{1,0:T(8,128)(2,1)} %get-tuple-element.28), channel_id=1, source_target_pairs={{0,64},{16,80},{32,96},{48,112},{64,0},{80,16},{96,32},{112,48},{1... | collective-permute-start | bytes 3538952 | tf_op jit(solution)/shard_map/ppermute | solution.py:321
  129.8 31.0 %collective-permute-start.3 = (bf16[576,1024]{1,0:T(8,128)(2,1)}, bf16[576,1024]{1,0:T(8,128)(2,1)}, u32[]{:S(2)}, u32[]{:S(2)}) collective-permute-start(bf16[576,1024]{1,0:T(8,128)(2,1)} %get-tuple-element.30), channel_id=1, source_target_pairs={{0,192},{16,208},{32,224},{48,240},{64,128},{80,144},{96,160},{112... | collective-permute-start | bytes 3538952 | tf_op jit(solution)/shard_map/ppermute | solution.py:321
  131.9 32.3 %collective-permute-start.6 = (bf16[576,1024]{1,0:T(8,128)(2,1)}, bf16[576,1024]{1,0:T(8,128)(2,1)}, u32[]{:S(2)}, u32[]{:S(2)}) collective-permute-start(bf16[576,1024]{1,0:T(8,128)(2,1)} %get-tuple-element.32), channel_id=1, source_target_pairs={{0,16},{16,0},{32,48},{48,32},{64,80},{80,64},{96,112},{112,96},{1... | collective-permute-start | bytes 3538952 | tf_op jit(solution)/shard_map/ppermute | solution.py:321
  133.5 35.5 %collective-permute-start.9 = (bf16[576,1024]{1,0:T(8,128)(2,1)}, bf16[576,1024]{1,0:T(8,128)(2,1)}, u32[]{:S(2)}, u32[]{:S(2)}) collective-permute-start(bf16[576,1024]{1,0:T(8,128)(2,1)} %get-tuple-element.34), channel_id=1, source_target_pairs={{0,48},{16,32},{32,16},{48,0},{64,112},{80,96},{96,80},{112,64},{1... | collective-permute-start | bytes 3538952 | tf_op jit(solution)/shard_map/ppermute | solution.py:321
  135.7 2.8 %copy-start.3 = (bf16[1,2048,1536]{2,1,0:T(8,128)(2,1)S(1)}, bf16[1,2048,1536]{2,1,0:T(8,128)(2,1)}, u32[]{:S(2)}) copy-start(bf16[1,2048,1536]{2,1,0:T(8,128)(2,1)} %param.8) | copy-start | bytes 18874372
  143.1 1.4 copy-start
  144.5 57.3 %all-to-all-start.2 = ((bf16[16,32,2048]{2,1,0:T(8,128)(2,1)}), bf16[16,32,2048]{2,1,0:T(8,128)(2,1)}, u32[]{:S(2)}, u32[]{:S(2)}) async-start(bf16[16,32,2048]{2,1,0:T(8,128)(2,1)} %bitcast.33), calls=%async_computation.2 | async-start | bytes 4194304 | tf_op jit(solution)/shard_map/all_to_all | solution.py:323
  149.6 1.4 copy-start.5
  151.0 1.6 copy-start.7
  159.2 14.7 %collective-permute-start.1 = (bf16[576,512]{1,0:T(8,128)(2,1)S(1)}, bf16[576,512]{1,0:T(8,128)(2,1)S(1)}, u32[]{:S(2)}, u32[]{:S(2)}) collective-permute-start(bf16[576,512]{1,0:T(8,128)(2,1)S(1)} %get-tuple-element.47), channel_id=1, source_target_pairs={{0,192},{16,208},{32,224},{48,240},{64,128},{80,144},{96,160},{112... | collective-permute-start | bytes 1769480 | tf_op jit(solution)/shard_map/ppermute | solution.py:346
  162.4 14.5 %collective-permute-start.4 = (bf16[576,512]{1,0:T(8,128)(2,1)S(1)}, bf16[576,512]{1,0:T(8,128)(2,1)S(1)}, u32[]{:S(2)}, u32[]{:S(2)}) collective-permute-start(bf16[576,512]{1,0:T(8,128)(2,1)S(1)} %get-tuple-element.45), channel_id=1, source_target_pairs={{0,64},{16,80},{32,96},{48,112},{64,0},{80,16},{96,32},{112,48},{1... | collective-permute-start | bytes 1769480 | tf_op jit(solution)/shard_map/ppermute | solution.py:346
  165.8 17.3 %collective-permute-start.7 = (bf16[576,512]{1,0:T(8,128)(2,1)S(1)}, bf16[576,512]{1,0:T(8,128)(2,1)S(1)}, u32[]{:S(2)}, u32[]{:S(2)}) collective-permute-start(bf16[576,512]{1,0:T(8,128)(2,1)S(1)} %get-tuple-element.43), channel_id=1, source_target_pairs={{0,48},{16,32},{32,16},{48,0},{64,112},{80,96},{96,80},{112,64},{1... | collective-permute-start | bytes 1769480 | tf_op jit(solution)/shard_map/ppermute | solution.py:346
  170.6 16.4 %collective-permute-start.10 = (bf16[576,512]{1,0:T(8,128)(2,1)S(1)}, bf16[576,512]{1,0:T(8,128)(2,1)S(1)}, u32[]{:S(2)}, u32[]{:S(2)}) collective-permute-start(bf16[576,512]{1,0:T(8,128)(2,1)S(1)} %get-tuple-element.41), channel_id=1, source_target_pairs={{0,16},{16,0},{32,48},{48,32},{64,80},{80,64},{96,112},{112,96},{1... | collective-permute-start | bytes 1769480 | tf_op jit(solution)/shard_map/ppermute | solution.py:346
  174.0 16.7 %collective-permute-start.2 = (bf16[576,256]{1,0:T(8,128)(2,1)S(1)}, bf16[576,256]{1,0:T(8,128)(2,1)S(1)}, u32[]{:S(2)}, u32[]{:S(2)}) collective-permute-start(bf16[576,256]{1,0:T(8,128)(2,1)S(1)} %get-tuple-element.55), channel_id=1, source_target_pairs={{0,16},{16,0},{32,48},{48,32},{64,80},{80,64},{96,112},{112,96},{1... | collective-permute-start | bytes 884744 | tf_op jit(solution)/shard_map/ppermute | solution.py:346
  177.0 14.2 %collective-permute-start.5 = (bf16[576,256]{1,0:T(8,128)(2,1)S(1)}, bf16[576,256]{1,0:T(8,128)(2,1)S(1)}, u32[]{:S(2)}, u32[]{:S(2)}) collective-permute-start(bf16[576,256]{1,0:T(8,128)(2,1)S(1)} %get-tuple-element.53), channel_id=1, source_target_pairs={{0,48},{16,32},{32,16},{48,0},{64,112},{80,96},{96,80},{112,64},{1... | collective-permute-start | bytes 884744 | tf_op jit(solution)/shard_map/ppermute | solution.py:346
  183.3 8.3 %collective-permute-start.8 = (bf16[576,256]{1,0:T(8,128)(2,1)S(1)}, bf16[576,256]{1,0:T(8,128)(2,1)S(1)}, u32[]{:S(2)}, u32[]{:S(2)}) collective-permute-start(bf16[576,256]{1,0:T(8,128)(2,1)S(1)} %get-tuple-element.51), channel_id=1, source_target_pairs={{0,64},{16,80},{32,96},{48,112},{64,0},{80,16},{96,32},{112,48},{1... | collective-permute-start | bytes 884744 | tf_op jit(solution)/shard_map/ppermute | solution.py:346
  187.1 8.4 %collective-permute-start.11 = (bf16[576,256]{1,0:T(8,128)(2,1)S(1)}, bf16[576,256]{1,0:T(8,128)(2,1)S(1)}, u32[]{:S(2)}, u32[]{:S(2)}) collective-permute-start(bf16[576,256]{1,0:T(8,128)(2,1)S(1)} %get-tuple-element.49), channel_id=1, source_target_pairs={{0,192},{16,208},{32,224},{48,240},{64,128},{80,144},{96,160},{112... | collective-permute-start | bytes 884744 | tf_op jit(solution)/shard_map/ppermute | solution.py:346
  190.8 6.4 %collective-permute-start.12 = (bf16[576,128]{1,0:T(8,128)(2,1)S(1)}, bf16[576,128]{1,0:T(8,128)(2,1)S(1)}, u32[]{:S(2)}, u32[]{:S(2)}) collective-permute-start(bf16[576,128]{1,0:T(8,128)(2,1)S(1)} %get-tuple-element.62), channel_id=1, source_target_pairs={{0,48},{16,32},{32,16},{48,0},{64,112},{80,96},{96,80},{112,64},{1... | collective-permute-start | bytes 442376 | tf_op jit(solution)/shard_map/ppermute | solution.py:346
  191.3 6.0 %collective-permute-start.13 = (bf16[576,128]{1,0:T(8,128)(2,1)S(1)}, bf16[576,128]{1,0:T(8,128)(2,1)S(1)}, u32[]{:S(2)}, u32[]{:S(2)}) collective-permute-start(bf16[576,128]{1,0:T(8,128)(2,1)S(1)} %get-tuple-element.60), channel_id=1, source_target_pairs={{0,16},{16,0},{32,48},{48,32},{64,80},{80,64},{96,112},{112,96},{1... | collective-permute-start | bytes 442376 | tf_op jit(solution)/shard_map/ppermute | solution.py:346
  191.7 5.6 %collective-permute-start.14 = (bf16[576,128]{1,0:T(8,128)(2,1)S(1)}, bf16[576,128]{1,0:T(8,128)(2,1)S(1)}, u32[]{:S(2)}, u32[]{:S(2)}) collective-permute-start(bf16[576,128]{1,0:T(8,128)(2,1)S(1)} %get-tuple-element.58), channel_id=1, source_target_pairs={{0,192},{16,208},{32,224},{48,240},{64,128},{80,144},{96,160},{112... | collective-permute-start | bytes 442376 | tf_op jit(solution)/shard_map/ppermute | solution.py:346
  195.5 5.2 %collective-permute-start.15 = (bf16[576,128]{1,0:T(8,128)(2,1)S(1)}, bf16[576,128]{1,0:T(8,128)(2,1)S(1)}, u32[]{:S(2)}, u32[]{:S(2)}) collective-permute-start(bf16[576,128]{1,0:T(8,128)(2,1)S(1)} %get-tuple-element.56), channel_id=1, source_target_pairs={{0,64},{16,80},{32,96},{48,112},{64,0},{80,16},{96,32},{112,48},{1... | collective-permute-start | bytes 442376 | tf_op jit(solution)/shard_map/ppermute | solution.py:346
  200.8 1.0 copy-start.8

commit v3 on v2

--- a/solution.py
+++ b/solution.py
@@ -15,20 +15,24 @@
 SMALL = pl.CostEstimate(flops=1000000, bytes_accessed=100000, transcendentals=0)
 
 
-def pack_kernel(ids_ref, values_ref, out_ref, target_ref):
-    ids = ids_ref[...]
-    tokens = ids.shape[1]
-    experts = out_ref.shape[0] // SLOTS
-    mine = (lax.broadcasted_iota(jnp.int32, (experts, tokens), 0) == ids).astype(jnp.float32)
-    earlier = lax.broadcasted_iota(jnp.int32, (tokens, tokens), 0) < lax.broadcasted_iota(
-        jnp.int32, (tokens, tokens), 1
-    )
-    before = dot32(mine.astype(jnp.bfloat16), earlier.astype(jnp.bfloat16))
-    slots = jnp.sum(before * mine, axis=0, keepdims=True).astype(jnp.int32)
-    target = ids * SLOTS + slots
-    target_ref[...] = target
-    spots = lax.broadcasted_iota(jnp.int32, (out_ref.shape[0], tokens), 0)
-    out_ref[...] = product((spots == target).astype(jnp.bfloat16), values_ref[...])
+def pack_kernel(ids_ref, values_ref, out_ref, target_ref, chosen):
+    @pl.when(pl.program_id(0) == 0)
+    def _():
+        ids = ids_ref[...]
+        tokens = ids.shape[1]
+        experts = out_ref.shape[0] // SLOTS
+        mine = (lax.broadcasted_iota(jnp.int32, (experts, tokens), 0) == ids).astype(jnp.float32)
+        earlier = lax.broadcasted_iota(jnp.int32, (tokens, tokens), 0) < lax.broadcasted_iota(
+            jnp.int32, (tokens, tokens), 1
+        )
+        before = dot32(mine.astype(jnp.bfloat16), earlier.astype(jnp.bfloat16))
+        slots = jnp.sum(before * mine, axis=0, keepdims=True).astype(jnp.int32)
+        target = ids * SLOTS + slots
+        target_ref[...] = target
+        spots = lax.broadcasted_iota(jnp.int32, (out_ref.shape[0], tokens), 0)
+        chosen[...] = (spots == target).astype(jnp.bfloat16)
+
+    out_ref[...] = product(chosen[...], values_ref[...])
 
 
 def pack(ids, values, experts):
@@ -49,6 +53,7 @@
             jax.ShapeDtypeStruct((experts * SLOTS, width), jnp.bfloat16),
             jax.ShapeDtypeStruct((1, tokens), jnp.int32),
         ],
+        scratch_shapes=[pltpu.VMEM((experts * SLOTS, tokens), jnp.bfloat16)],
         compiler_params=pltpu.CompilerParams(vmem_limit_bytes=56 * 1024 * 1024),
         cost_estimate=SMALL,
         name="pack",
@@ -155,7 +160,7 @@
         ]
         + [jax.ShapeDtypeStruct(size, jnp.bfloat16)] * n,
         scratch_shapes=[pltpu.VMEM(size, jnp.bfloat16)] * n
-        + [pltpu.VMEM((ff, rows), jnp.float32)] * 2
+        + [pltpu.VMEM((ff, rows), jnp.bfloat16)] * 2
         + [pltpu.SemaphoreType.DMA((n, CHUNKS)), pltpu.SemaphoreType.DMA((6,))],
         compiler_params=pltpu.CompilerParams(vmem_limit_bytes=GIVE_MIB * 1024 * 1024),
         cost_estimate=SMALL,
@@ -307,7 +312,8 @@
     sig = jax.nn.sigmoid(gate)
     silu = gate * sig
     hidden = (silu * upper).astype(jnp.bfloat16)
-    slope = upper * sig * (1.0 + gate * (1.0 - sig))
+    slope = (upper * sig * (1.0 + gate * (1.0 - sig))).astype(jnp.bfloat16)
+    silu = silu.astype(jnp.bfloat16)
 
     me = lax.axis_index("dp")
     at = (me // SIDE, me % SIDE)
@@ -332,7 +338,7 @@
     def add_halves(keep, got):
         n = keep.shape[1] // 2
         return tuple(
-            (k.astype(jnp.float32) + g.astype(jnp.float32)).astype(jnp.bfloat16)
+            k + g
             for k, g in ((keep[:, :n], got[:, :n]), (keep[:, n:], got[:, n:]))
         )
 

time: 206 us -> 204 us (level)
    add x0 -> x12, other arithmetic: none -> 6 us  [add_halves(): k + g]
    convert_element_type x12 -> x1, other arithmetic: 7.24 us -> 1.99 us  [local(): silu = silu.astype(jnp.bfloat16)]
    mul x1 -> x0, other arithmetic: 2.6 us -> none  [local(): silu = gate * sig]
  transfers between devices with their start and end apart: 19 -> 19, of which waited for: 11 -> 11; matrix products, arithmetic and copies ran while one was open for 11% -> 10% of each run, Pallas kernels for 7% -> 7%
where the time goes in v3:
time: 204 us; the launch traced here: 203 us
  waiting for transfers between devices  104 us (51%)
  starting transfers between devices  38.7 us (19%)
  Pallas kernels  27.3 us (13%)
  local copies, waits for them, and re-layouts  14.8 us (7%)
  other arithmetic  8.77 us (4%)
  matrix products  8.59 us (4%)
    all_to_all x2, waiting for transfers between devices, send(): lax.all_to_all(packed, 'expert', split_axis=0, concat_axis=0, tiled=True)  80.6 us
    ppermute x12, waiting for transfers between devices, local(): got = lax.ppermute(give, 'dp', pair_perm(axis, odd))  22.2 us
    unnamed x19, local copies, waits for them, and re-layouts  14.1 us
    ppermute x12, starting transfers between devices, local(): got = lax.ppermute(give, 'dp', pair_perm(axis, odd))  14 us
    all_to_all x2, starting transfers between devices, send(): lax.all_to_all(packed, 'expert', split_axis=0, concat_axis=0, tiled=True)  13.3 us
    pallas_call x1, Pallas kernels, make_gives(): pl.pallas_call(gives_kernel, in_specs=[pl.BlockSpec(memory_space=pltpu.SM...  9.58 us
    pallas_call x2, Pallas kernels, pack(): pl.pallas_call(pack_kernel, grid=(width // tile,), in_specs=[pl.BlockSpec...  8.74 us
    ppermute x4, starting transfers between devices, local(): gots[f] = lax.ppermute(gives[f], 'dp', pair_perm(*FLOWS[f]))  6.53 us
  transfers between devices with their start and end apart: 19, of which 11 were waited for; matrix products, arithmetic and copies ran while one was open for 10% of the time, Pallas kernels for 7%

profile of v3, /device:TPU:2, one launch (start us, length us, event | category | flops | bytes accessed | tf_op | source)
XLA Modules:
  0.0 203.4 jit_solution(600935245706540797)
XLA Ops:
  0.6 4.4 %pack.2 = (bf16[512,2048]{1,0:T(8,128)(2,1)}, s32[1,160]{1,0:T(1,128)}) custom-call(s32[1,160]{1,0:T(1,128)} %bitcast.38, bf16[160,2048]{1,0:T(8,128)(2,1)} %values_ref.2), custom_call_target="tpu_custom_call" | custom-call | flops 1000000 | bytes 100000 | tf_op jit(solution)/shard_map/pack/pallas_call | solution.py:41
  5.0 8.6 %all-to-all-start = ((bf16[16,32,2048]{2,1,0:T(8,128)(2,1)}), bf16[16,32,2048]{2,1,0:T(8,128)(2,1)S(1)}, u32[]{:S(2)}, u32[]{:S(2)}) async-start(bf16[16,32,2048]{2,1,0:T(8,128)(2,1)} %bitcast.37), calls=%async_computation | async-start | bytes 4194304 | tf_op jit(solution)/shard_map/all_to_all | solution.py:296
  13.6 4.4 %pack.3 = (bf16[512,2048]{1,0:T(8,128)(2,1)}, s32[1,160]{1,0:T(1,128)}) custom-call(s32[1,160]{1,0:T(1,128)} %bitcast.39, bf16[160,2048]{1,0:T(8,128)(2,1)} %values_ref.3), custom_call_target="tpu_custom_call" | custom-call | flops 1000000 | bytes 100000 | tf_op jit(solution)/shard_map/pack/pallas_call | solution.py:41
  17.9 44.8 %all-to-all-done = bf16[16,32,2048]{2,1,0:T(8,128)(2,1)S(1)} async-done(((bf16[16,32,2048]{2,1,0:T(8,128)(2,1)}), bf16[16,32,2048]{2,1,0:T(8,128)(2,1)S(1)}, u32[]{:S(2)}, u32[]{:S(2)}) %all-to-all-start) | async-done | bytes 2097184 | tf_op jit(solution)/shard_map/all_to_all | solution.py:296
  62.7 4.8 %all-to-all-start.1 = ((bf16[16,32,2048]{2,1,0:T(8,128)(2,1)}), bf16[16,32,2048]{2,1,0:T(8,128)(2,1)}, u32[]{:S(2)}, u32[]{:S(2)}) async-start(bf16[16,32,2048]{2,1,0:T(8,128)(2,1)} %bitcast.36), calls=%async_computation.1 | async-start | bytes 4194304 | tf_op jit(solution)/shard_map/all_to_all | solution.py:296
  67.6 0.1 add_multiply_fusion
  67.6 0.1 add_multiply_fusion.1
  67.7 0.1 add_add_fusion
  67.9 0.1 add.263
  68.0 0.1 add_multiply_fusion.2
  68.0 0.1 pad_add_fusion.2
  68.1 0.1 pad_add_fusion.3
  68.3 0.1 add.275
  68.4 0.1 add.267
  68.6 0.1 add.271
  68.7 4.7 %copy.8 = bf16[1,2048,768]{1,2,0:T(8,128)(2,1)} copy(bf16[1,2048,768]{2,1,0:T(8,128)(2,1)} %param.9) | data formatting | bytes 6291456 | tf_op args[4]
  73.4 5.6 %convolution_bitcast_fusion = f32[1536,512]{1,0:T(8,128)S(1)} fusion(bf16[512,2048]{1,0:T(8,128)(2,1)S(1)} %bitcast.30, bf16[1,2048,1536]{2,1,0:T(8,128)(2,1)} %param.8), kind=kOutput, calls=%fused_computation | convolution fusion | flops 3221225472 | bytes 11534336 | tf_op jit(solution)/shard_map/dot_general | solution.py:307
  79.0 2.0 fusion.2
  81.0 35.8 %all-to-all-done.1 = bf16[16,32,2048]{2,1,0:T(8,128)(2,1)} async-done(((bf16[16,32,2048]{2,1,0:T(8,128)(2,1)}), bf16[16,32,2048]{2,1,0:T(8,128)(2,1)}, u32[]{:S(2)}, u32[]{:S(2)}) %all-to-all-start.1) | async-done | bytes 2097184 | tf_op jit(solution)/shard_map/all_to_all | solution.py:296
  116.8 1.1 copy-done.4
  117.9 1.1 copy-done.5
  119.0 9.6 %give.1 = (bf16[1536,512]{1,0:T(8,128)(2,1)S(1)}, bf16[512,2048]{1,0:T(8,128)(2,1)S(1)}, bf16[576,1024]{1,0:T(8,128)(2,1)}, bf16[576,1024]{1,0:T(8,128)(2,1)}, b...) custom-call(s32[4,8]{1,0:T(4,128)S(1)} %pad_add_fusion.table, bf16[768,2048]{1,0:T(8,128)(2,1)} %bitcast.35, ...), custom_call_target="tpu_custom_call" | custom-call | flops 1000000 | bytes 100000 | tf_op jit(solution)/shard_map/give/pallas_call | solution.py:153
  128.6 0.6 collective-permute-start
  129.2 2.2 %collective-permute-start.3 = (bf16[576,1024]{1,0:T(8,128)(2,1)}, bf16[576,1024]{1,0:T(8,128)(2,1)}, u32[]{:S(2)}, u32[]{:S(2)}) collective-permute-start(bf16[576,1024]{1,0:T(8,128)(2,1)} %get-tuple-element.30), channel_id=1, source_target_pairs={{0,192},{16,208},{32,224},{48,240},{64,128},{80,144},{96,160},{112... | collective-permute-start | bytes 3538952 | tf_op jit(solution)/shard_map/ppermute | solution.py:327
  131.4 1.5 collective-permute-start.6
  133.0 2.2 %collective-permute-start.9 = (bf16[576,1024]{1,0:T(8,128)(2,1)}, bf16[576,1024]{1,0:T(8,128)(2,1)}, u32[]{:S(2)}, u32[]{:S(2)}) collective-permute-start(bf16[576,1024]{1,0:T(8,128)(2,1)} %get-tuple-element.34), channel_id=1, source_target_pairs={{0,48},{16,32},{32,16},{48,0},{64,112},{80,96},{96,80},{112,64},{1... | collective-permute-start | bytes 3538952 | tf_op jit(solution)/shard_map/ppermute | solution.py:327
  135.2 2.8 %copy-done.1 = bf16[1,2048,1536]{2,1,0:T(8,128)(2,1)S(1)} copy-done((bf16[1,2048,1536]{2,1,0:T(8,128)(2,1)S(1)}, bf16[1,2048,1536]{2,1,0:T(8,128)(2,1)}, u32[]{:S(2)}) %copy-start.1) | copy-done | bytes 6291480
  138.0 4.6 %drows.1 = bf16[512,2048]{1,0:T(8,128)(2,1)S(1)} custom-call(bf16[1536,512]{1,0:T(8,128)(2,1)S(1)} %get-tuple-element.25.g_ref.dgu_ref, bf16[2048,1536]{1,0:T(8,128)(2,1)S(1)} %bitcast.34), custom_call_target="tpu_custom_call" | custom-call | flops 1000000 | bytes 100000 | tf_op jit(solution)/shard_map/drows/pallas_call | solution.py:215
  142.6 1.4 copy-done
  144.0 4.8 %all-to-all-start.2 = ((bf16[16,32,2048]{2,1,0:T(8,128)(2,1)}), bf16[16,32,2048]{2,1,0:T(8,128)(2,1)}, u32[]{:S(2)}, u32[]{:S(2)}) async-start(bf16[16,32,2048]{2,1,0:T(8,128)(2,1)} %bitcast.33), calls=%async_computation.2 | async-start | bytes 4194304 | tf_op jit(solution)/shard_map/all_to_all | solution.py:329
  148.8 0.1 add.280
  148.9 0.1 add.289
  148.9 0.1 add.283
  149.0 0.1 add.286
  149.1 1.4 copy-done.3
  150.5 1.6 copy-done.7
  152.1 3.4 %keep.1 = (bf16[576,1024]{1,0:T(8,128)(2,1)S(1)}, bf16[576,1024]{1,0:T(8,128)(2,1)S(1)}, bf16[576,1024]{1,0:T(8,128)(2,1)S(1)}, bf16[576,1024]{1,0:T(8,128)(2,1)S(1)}) custom-call(s32[4,8]{1,0:T(4,128)S(1)} %pad_add_fusion.1.table, bf16[1536,512]{1,0:T(8,128)(2,1)S(1)} %copy-done.3, bf16[768,512]{1,0:T(8,128)(2,1)S(1)} %get-tuple-element.39.hid_ref, ...), custom_call_target="tpu_custom_call" | custom-call | flops 1000000 | bytes 100000 | tf_op jit(solution)/shard_map/keep/pallas_call | solution.py:190
  155.5 1.6 collective-permute-done
  157.1 1.4 slice_add_fusion.7
  158.5 1.6 collective-permute-start.1
  160.1 1.4 slice_add_fusion.5
  161.5 1.9 collective-permute-start.4
  163.4 1.4 slice_add_fusion.3
  164.8 3.1 %collective-permute-start.7 = (bf16[576,512]{1,0:T(8,128)(2,1)S(1)}, bf16[576,512]{1,0:T(8,128)(2,1)S(1)}, u32[]{:S(2)}, u32[]{:S(2)}) collective-permute-start(bf16[576,512]{1,0:T(8,128)(2,1)S(1)} %get-tuple-element.43), channel_id=1, source_target_pairs={{0,48},{16,32},{32,16},{48,0},{64,112},{80,96},{96,80},{112,64},{1... | collective-permute-start | bytes 1769480 | tf_op jit(solution)/shard_map/ppermute | solution.py:352
  167.9 1.4 slice_add_fusion.1
  169.3 0.2 collective-permute-start.10
  169.5 3.7 %collective-permute-done.1 = bf16[576,512]{1,0:T(8,128)(2,1)S(1)} collective-permute-done((bf16[576,512]{1,0:T(8,128)(2,1)S(1)}, bf16[576,512]{1,0:T(8,128)(2,1)S(1)}, u32[]{:S(2)}, u32[]{:S(2)}) %collective-permute-start.1) | collective-permute-done | bytes 589856 | tf_op jit(solution)/shard_map/ppermute | solution.py:352
  173.2 1.7 collective-permute-start.2
  174.9 1.1 collective-permute-done.4
  176.0 3.1 %collective-permute-start.5 = (bf16[576,256]{1,0:T(8,128)(2,1)S(1)}, bf16[576,256]{1,0:T(8,128)(2,1)S(1)}, u32[]{:S(2)}, u32[]{:S(2)}) collective-permute-start(bf16[576,256]{1,0:T(8,128)(2,1)S(1)} %get-tuple-element.53), channel_id=1, source_target_pairs={{0,48},{16,32},{32,16},{48,0},{64,112},{80,96},{96,80},{112,64},{1... | collective-permute-start | bytes 884744 | tf_op jit(solution)/shard_map/ppermute | solution.py:352
  179.1 2.8 %collective-permute-done.7 = bf16[576,512]{1,0:T(8,128)(2,1)S(1)} collective-permute-done((bf16[576,512]{1,0:T(8,128)(2,1)S(1)}, bf16[576,512]{1,0:T(8,128)(2,1)S(1)}, u32[]{:S(2)}, u32[]{:S(2)}) %collective-permute-start.7) | collective-permute-done | bytes 589856 | tf_op jit(solution)/shard_map/ppermute | solution.py:352
  182.0 0.1 collective-permute-start.8
  182.1 3.5 %collective-permute-done.10 = bf16[576,512]{1,0:T(8,128)(2,1)S(1)} collective-permute-done((bf16[576,512]{1,0:T(8,128)(2,1)S(1)}, bf16[576,512]{1,0:T(8,128)(2,1)S(1)}, u32[]{:S(2)}, u32[]{:S(2)}) %collective-permute-start.10) | collective-permute-done | bytes 589856 | tf_op jit(solution)/shard_map/ppermute | solution.py:352
  185.7 0.1 collective-permute-start.11
  185.8 3.6 %collective-permute-done.2 = bf16[576,256]{1,0:T(8,128)(2,1)S(1)} collective-permute-done((bf16[576,256]{1,0:T(8,128)(2,1)S(1)}, bf16[576,256]{1,0:T(8,128)(2,1)S(1)}, u32[]{:S(2)}, u32[]{:S(2)}) %collective-permute-start.2) | collective-permute-done | bytes 294944 | tf_op jit(solution)/shard_map/ppermute | solution.py:352
  189.5 0.4 collective-permute-start.12
  190.0 0.3 collective-permute-start.13
  190.3 0.1 collective-permute-start.14
  190.4 3.7 %collective-permute-done.11 = bf16[576,256]{1,0:T(8,128)(2,1)S(1)} collective-permute-done((bf16[576,256]{1,0:T(8,128)(2,1)S(1)}, bf16[576,256]{1,0:T(8,128)(2,1)S(1)}, u32[]{:S(2)}, u32[]{:S(2)}) %collective-permute-start.11) | collective-permute-done | bytes 294944 | tf_op jit(solution)/shard_map/ppermute | solution.py:352
  194.2 1.5 collective-permute-start.15
  195.7 0.3 collective-permute-done.12.refs_4_
  196.0 3.4 %collective-permute-done.15.refs_7_ = bf16[576,128]{1,0:T(8,128)(2,1)S(1)} collective-permute-done((bf16[576,128]{1,0:T(8,128)(2,1)S(1)}, bf16[576,128]{1,0:T(8,128)(2,1)S(1)}, u32[]{:S(2)}, u32[]{:S(2)}) %collective-permute-start.15) | collective-permute-done | bytes 147488 | tf_op jit(solution)/shard_map/ppermute | solution.py:352
  199.4 1.0 finish.1
  200.4 3.0 %convolution_convert_fusion = bf16[160,2048]{1,0:T(8,128)(2,1)} fusion(bf16[512,2048]{1,0:T(8,128)(2,1)} %bitcast.21, s32[160]{0:T(256)S(1)} %bitcast.40), kind=kOutput, calls=%fused_computation.1 | convolution fusion | flops 335953920 | bytes 2753152 | tf_op jit(solution)/shard_map/dot_general | solution.py:333
  (34 shorter events, 0.8 us)
Async XLA Ops:
  5.0 57.7 %all-to-all-start = ((bf16[16,32,2048]{2,1,0:T(8,128)(2,1)}), bf16[16,32,2048]{2,1,0:T(8,128)(2,1)S(1)}, u32[]{:S(2)}, u32[]{:S(2)}) async-start(bf16[16,32,2048]{2,1,0:T(8,128)(2,1)} %bitcast.37), calls=%async_computation | async-start | bytes 4194304 | tf_op jit(solution)/shard_map/all_to_all | solution.py:296
  62.7 54.0 %all-to-all-start.1 = ((bf16[16,32,2048]{2,1,0:T(8,128)(2,1)}), bf16[16,32,2048]{2,1,0:T(8,128)(2,1)}, u32[]{:S(2)}, u32[]{:S(2)}) async-start(bf16[16,32,2048]{2,1,0:T(8,128)(2,1)} %bitcast.36), calls=%async_computation.1 | async-start | bytes 4194304 | tf_op jit(solution)/shard_map/all_to_all | solution.py:296
  116.8 1.1 copy-start.4
  117.9 1.1 copy-start.5
  128.6 14.0 %copy-start.2 = (bf16[1536,512]{1,0:T(8,128)(2,1)}, bf16[1536,512]{1,0:T(8,128)(2,1)S(1)}, u32[]{:S(2)}) copy-start(bf16[1536,512]{1,0:T(8,128)(2,1)S(1)} %get-tuple-element.25.g_ref.dgu_ref) | copy-start | bytes 4718596
  128.6 14.0 %copy-start.6 = (bf16[512,2048]{1,0:T(8,128)(2,1)}, bf16[512,2048]{1,0:T(8,128)(2,1)S(1)}, u32[]{:S(2)}) copy-start(bf16[512,2048]{1,0:T(8,128)(2,1)S(1)} %get-tuple-element.26.dy_ref) | copy-start | bytes 6291460
  128.6 28.4 %collective-permute-start = (bf16[576,1024]{1,0:T(8,128)(2,1)}, bf16[576,1024]{1,0:T(8,128)(2,1)}, u32[]{:S(2)}, u32[]{:S(2)}) collective-permute-start(bf16[576,1024]{1,0:T(8,128)(2,1)} %get-tuple-element.28), channel_id=1, source_target_pairs={{0,64},{16,80},{32,96},{48,112},{64,0},{80,16},{96,32},{112,48},{1... | collective-permute-start | bytes 3538952 | tf_op jit(solution)/shard_map/ppermute | solution.py:327
  129.2 30.8 %collective-permute-start.3 = (bf16[576,1024]{1,0:T(8,128)(2,1)}, bf16[576,1024]{1,0:T(8,128)(2,1)}, u32[]{:S(2)}, u32[]{:S(2)}) collective-permute-start(bf16[576,1024]{1,0:T(8,128)(2,1)} %get-tuple-element.30), channel_id=1, source_target_pairs={{0,192},{16,208},{32,224},{48,240},{64,128},{80,144},{96,160},{112... | collective-permute-start | bytes 3538952 | tf_op jit(solution)/shard_map/ppermute | solution.py:327
  131.4 32.0 %collective-permute-start.6 = (bf16[576,1024]{1,0:T(8,128)(2,1)}, bf16[576,1024]{1,0:T(8,128)(2,1)}, u32[]{:S(2)}, u32[]{:S(2)}) collective-permute-start(bf16[576,1024]{1,0:T(8,128)(2,1)} %get-tuple-element.32), channel_id=1, source_target_pairs={{0,16},{16,0},{32,48},{48,32},{64,80},{80,64},{96,112},{112,96},{1... | collective-permute-start | bytes 3538952 | tf_op jit(solution)/shard_map/ppermute | solution.py:327
  133.0 34.9 %collective-permute-start.9 = (bf16[576,1024]{1,0:T(8,128)(2,1)}, bf16[576,1024]{1,0:T(8,128)(2,1)}, u32[]{:S(2)}, u32[]{:S(2)}) collective-permute-start(bf16[576,1024]{1,0:T(8,128)(2,1)} %get-tuple-element.34), channel_id=1, source_target_pairs={{0,48},{16,32},{32,16},{48,0},{64,112},{80,96},{96,80},{112,64},{1... | collective-permute-start | bytes 3538952 | tf_op jit(solution)/shard_map/ppermute | solution.py:327
  135.2 2.8 %copy-start.1 = (bf16[1,2048,1536]{2,1,0:T(8,128)(2,1)S(1)}, bf16[1,2048,1536]{2,1,0:T(8,128)(2,1)}, u32[]{:S(2)}) copy-start(bf16[1,2048,1536]{2,1,0:T(8,128)(2,1)} %param.8) | copy-start | bytes 18874372
  142.6 1.4 copy-start
  144.0 56.4 %all-to-all-start.2 = ((bf16[16,32,2048]{2,1,0:T(8,128)(2,1)}), bf16[16,32,2048]{2,1,0:T(8,128)(2,1)}, u32[]{:S(2)}, u32[]{:S(2)}) async-start(bf16[16,32,2048]{2,1,0:T(8,128)(2,1)} %bitcast.33), calls=%async_computation.2 | async-start | bytes 4194304 | tf_op jit(solution)/shard_map/all_to_all | solution.py:329
  149.1 1.4 copy-start.3
  150.5 1.6 copy-start.7
  158.5 14.7 %collective-permute-start.1 = (bf16[576,512]{1,0:T(8,128)(2,1)S(1)}, bf16[576,512]{1,0:T(8,128)(2,1)S(1)}, u32[]{:S(2)}, u32[]{:S(2)}) collective-permute-start(bf16[576,512]{1,0:T(8,128)(2,1)S(1)} %get-tuple-element.47), channel_id=1, source_target_pairs={{0,192},{16,208},{32,224},{48,240},{64,128},{80,144},{96,160},{112... | collective-permute-start | bytes 1769480 | tf_op jit(solution)/shard_map/ppermute | solution.py:352
  161.5 14.5 %collective-permute-start.4 = (bf16[576,512]{1,0:T(8,128)(2,1)S(1)}, bf16[576,512]{1,0:T(8,128)(2,1)S(1)}, u32[]{:S(2)}, u32[]{:S(2)}) collective-permute-start(bf16[576,512]{1,0:T(8,128)(2,1)S(1)} %get-tuple-element.45), channel_id=1, source_target_pairs={{0,64},{16,80},{32,96},{48,112},{64,0},{80,16},{96,32},{112,48},{1... | collective-permute-start | bytes 1769480 | tf_op jit(solution)/shard_map/ppermute | solution.py:352
  164.8 17.2 %collective-permute-start.7 = (bf16[576,512]{1,0:T(8,128)(2,1)S(1)}, bf16[576,512]{1,0:T(8,128)(2,1)S(1)}, u32[]{:S(2)}, u32[]{:S(2)}) collective-permute-start(bf16[576,512]{1,0:T(8,128)(2,1)S(1)} %get-tuple-element.43), channel_id=1, source_target_pairs={{0,48},{16,32},{32,16},{48,0},{64,112},{80,96},{96,80},{112,64},{1... | collective-permute-start | bytes 1769480 | tf_op jit(solution)/shard_map/ppermute | solution.py:352
  169.3 16.4 %collective-permute-start.10 = (bf16[576,512]{1,0:T(8,128)(2,1)S(1)}, bf16[576,512]{1,0:T(8,128)(2,1)S(1)}, u32[]{:S(2)}, u32[]{:S(2)}) collective-permute-start(bf16[576,512]{1,0:T(8,128)(2,1)S(1)} %get-tuple-element.41), channel_id=1, source_target_pairs={{0,16},{16,0},{32,48},{48,32},{64,80},{80,64},{96,112},{112,96},{1... | collective-permute-start | bytes 1769480 | tf_op jit(solution)/shard_map/ppermute | solution.py:352
  173.2 16.2 %collective-permute-start.2 = (bf16[576,256]{1,0:T(8,128)(2,1)S(1)}, bf16[576,256]{1,0:T(8,128)(2,1)S(1)}, u32[]{:S(2)}, u32[]{:S(2)}) collective-permute-start(bf16[576,256]{1,0:T(8,128)(2,1)S(1)} %get-tuple-element.55), channel_id=1, source_target_pairs={{0,16},{16,0},{32,48},{48,32},{64,80},{80,64},{96,112},{112,96},{1... | collective-permute-start | bytes 884744 | tf_op jit(solution)/shard_map/ppermute | solution.py:352
  176.0 13.9 %collective-permute-start.5 = (bf16[576,256]{1,0:T(8,128)(2,1)S(1)}, bf16[576,256]{1,0:T(8,128)(2,1)S(1)}, u32[]{:S(2)}, u32[]{:S(2)}) collective-permute-start(bf16[576,256]{1,0:T(8,128)(2,1)S(1)} %get-tuple-element.53), channel_id=1, source_target_pairs={{0,48},{16,32},{32,16},{48,0},{64,112},{80,96},{96,80},{112,64},{1... | collective-permute-start | bytes 884744 | tf_op jit(solution)/shard_map/ppermute | solution.py:352
  182.0 8.2 %collective-permute-start.8 = (bf16[576,256]{1,0:T(8,128)(2,1)S(1)}, bf16[576,256]{1,0:T(8,128)(2,1)S(1)}, u32[]{:S(2)}, u32[]{:S(2)}) collective-permute-start(bf16[576,256]{1,0:T(8,128)(2,1)S(1)} %get-tuple-element.51), channel_id=1, source_target_pairs={{0,64},{16,80},{32,96},{48,112},{64,0},{80,16},{96,32},{112,48},{1... | collective-permute-start | bytes 884744 | tf_op jit(solution)/shard_map/ppermute | solution.py:352
  185.7 8.4 %collective-permute-start.11 = (bf16[576,256]{1,0:T(8,128)(2,1)S(1)}, bf16[576,256]{1,0:T(8,128)(2,1)S(1)}, u32[]{:S(2)}, u32[]{:S(2)}) collective-permute-start(bf16[576,256]{1,0:T(8,128)(2,1)S(1)} %get-tuple-element.49), channel_id=1, source_target_pairs={{0,192},{16,208},{32,224},{48,240},{64,128},{80,144},{96,160},{112... | collective-permute-start | bytes 884744 | tf_op jit(solution)/shard_map/ppermute | solution.py:352
  189.5 6.4 %collective-permute-start.12 = (bf16[576,128]{1,0:T(8,128)(2,1)S(1)}, bf16[576,128]{1,0:T(8,128)(2,1)S(1)}, u32[]{:S(2)}, u32[]{:S(2)}) collective-permute-start(bf16[576,128]{1,0:T(8,128)(2,1)S(1)} %get-tuple-element.62), channel_id=1, source_target_pairs={{0,48},{16,32},{32,16},{48,0},{64,112},{80,96},{96,80},{112,64},{1... | collective-permute-start | bytes 442376 | tf_op jit(solution)/shard_map/ppermute | solution.py:352
  190.0 6.0 %collective-permute-start.13 = (bf16[576,128]{1,0:T(8,128)(2,1)S(1)}, bf16[576,128]{1,0:T(8,128)(2,1)S(1)}, u32[]{:S(2)}, u32[]{:S(2)}) collective-permute-start(bf16[576,128]{1,0:T(8,128)(2,1)S(1)} %get-tuple-element.60), channel_id=1, source_target_pairs={{0,16},{16,0},{32,48},{48,32},{64,80},{80,64},{96,112},{112,96},{1... | collective-permute-start | bytes 442376 | tf_op jit(solution)/shard_map/ppermute | solution.py:352
  190.3 5.6 %collective-permute-start.14 = (bf16[576,128]{1,0:T(8,128)(2,1)S(1)}, bf16[576,128]{1,0:T(8,128)(2,1)S(1)}, u32[]{:S(2)}, u32[]{:S(2)}) collective-permute-start(bf16[576,128]{1,0:T(8,128)(2,1)S(1)} %get-tuple-element.58), channel_id=1, source_target_pairs={{0,192},{16,208},{32,224},{48,240},{64,128},{80,144},{96,160},{112... | collective-permute-start | bytes 442376 | tf_op jit(solution)/shard_map/ppermute | solution.py:352
  194.2 5.2 %collective-permute-start.15 = (bf16[576,128]{1,0:T(8,128)(2,1)S(1)}, bf16[576,128]{1,0:T(8,128)(2,1)S(1)}, u32[]{:S(2)}, u32[]{:S(2)}) collective-permute-start(bf16[576,128]{1,0:T(8,128)(2,1)S(1)} %get-tuple-element.56), channel_id=1, source_target_pairs={{0,64},{16,80},{32,96},{48,112},{64,0},{80,16},{96,32},{112,48},{1... | collective-permute-start | bytes 442376 | tf_op jit(solution)/shard_map/ppermute | solution.py:352
  199.4 1.0 copy-start.8

commit v4 on v3

--- a/solution.py
+++ b/solution.py
@@ -90,26 +90,43 @@
     return parts
 
 
-def gives_kernel(table, w_ref, hid_ref, x_ref, slope_in, silu_in, dy_in, dgu_ref, dy_ref, *refs):
+def factors_kernel(gate_up_ref, slope_ref, silu_ref, hid_ref):
+    ff = hid_ref.shape[0]
+    tile = 64
+
+    def body(i, carry):
+        part = pl.ds(pl.multiple_of(i * tile, tile), tile)
+        gate = gate_up_ref[part, :]
+        upper = gate_up_ref[pl.ds(pl.multiple_of(ff + i * tile, tile), tile), :]
+        sig = jax.nn.sigmoid(gate)
+        silu = gate * sig
+        silu_ref[part, :] = silu.astype(jnp.bfloat16)
+        hid_ref[part, :] = (silu * upper).astype(jnp.bfloat16)
+        slope_ref[part, :] = (upper * sig * (1.0 + gate * (1.0 - sig))).astype(jnp.bfloat16)
+        return carry
+
+    lax.fori_loop(0, ff // tile, body, 0)
+
+
+def make_factors(gate_up):
+    whole = pl.BlockSpec(memory_space=pltpu.VMEM)
+    return pl.pallas_call(
+        factors_kernel,
+        in_specs=[whole],
+        out_specs=[whole] * 3,
+        out_shape=[jax.ShapeDtypeStruct((gate_up.shape[0] // 2, gate_up.shape[1]), jnp.bfloat16)] * 3,
+        compiler_params=pltpu.CompilerParams(vmem_limit_bytes=8 * 1024 * 1024),
+        cost_estimate=SMALL,
+        name="factors",
+    )(gate_up)
+
+
+def gives_kernel(table, w_ref, hid_ref, x_ref, dy_ref, slope_ref, silu_ref, dgu_ref, *refs):
     n = len(FLOWS)
-    outs, stages, (slope_ref, silu_ref, sems, in_sems) = refs[:n], refs[n : 2 * n], refs[2 * n :]
+    outs, stages, sems = refs[:n], refs[n : 2 * n], refs[2 * n]
     per = outs[0].shape[0]
     ff = hid_ref.shape[0]
     tile = 256
-    part = dy_in.shape[0] // 4
-    arrivals = [
-        pltpu.make_async_copy(dy_in.at[pl.ds(k * part, part)], dy_ref.at[pl.ds(k * part, part)], in_sems.at[k])
-        for k in range(4)
-    ]
-    factors = [
-        pltpu.make_async_copy(slope_in, slope_ref, in_sems.at[4]),
-        pltpu.make_async_copy(silu_in, silu_ref, in_sems.at[5]),
-    ]
-    for copy in arrivals + factors:
-        copy.start()
-    for copy in arrivals:
-        copy.wait()
-
     def copy(f, chunk):
         return pltpu.make_async_copy(
             stages[f].at[:, lanes(chunk)], outs[f].at[:, lanes(chunk)], sems.at[f, chunk]
@@ -128,8 +145,6 @@
         lax.fori_loop(0, CHUNKS, body, 0, unroll=True)
 
     give(3)
-    for copy_in in factors:
-        copy_in.wait()
     for low in range(0, ff, tile):
         here = slice(low, low + tile)
         dhidden = lax.dot_general(
@@ -152,20 +167,15 @@
     n = len(FLOWS)
     return pl.pallas_call(
         gives_kernel,
-        in_specs=[pl.BlockSpec(memory_space=pltpu.SMEM)] + [whole] * 3 + [away] * 3,
-        out_specs=[whole] * 2 + [away] * n,
-        out_shape=[
-            jax.ShapeDtypeStruct((2 * ff, rows), jnp.bfloat16),
-            jax.ShapeDtypeStruct(rows_dy.shape, jnp.bfloat16),
-        ]
+        in_specs=[pl.BlockSpec(memory_space=pltpu.SMEM)] + [whole] * 6,
+        out_specs=[whole] + [away] * n,
+        out_shape=[jax.ShapeDtypeStruct((2 * ff, rows), jnp.bfloat16)]
         + [jax.ShapeDtypeStruct(size, jnp.bfloat16)] * n,
-        scratch_shapes=[pltpu.VMEM(size, jnp.bfloat16)] * n
-        + [pltpu.VMEM((ff, rows), jnp.bfloat16)] * 2
-        + [pltpu.SemaphoreType.DMA((n, CHUNKS)), pltpu.SemaphoreType.DMA((6,))],
+        scratch_shapes=[pltpu.VMEM(size, jnp.bfloat16)] * n + [pltpu.SemaphoreType.DMA((n, CHUNKS))],
         compiler_params=pltpu.CompilerParams(vmem_limit_bytes=GIVE_MIB * 1024 * 1024),
         cost_estimate=SMALL,
         name="give",
-    )(table, w_out_t, hidden, rows_x, slope, silu, rows_dy)
+    )(table, w_out_t, hidden, rows_x, rows_dy, slope, silu)
 
 
 def keeps_kernel(table, dgu_ref, hid_ref, x_ref, dy_ref, *outs):
@@ -307,13 +317,7 @@
     gate_up = lax.dot_general(
         w_in, rows_x, (((0,), (1,)), ((), ())), preferred_element_type=jnp.float32
     )
-    gate = gate_up[:ff]
-    upper = gate_up[ff:]
-    sig = jax.nn.sigmoid(gate)
-    silu = gate * sig
-    hidden = (silu * upper).astype(jnp.bfloat16)
-    slope = (upper * sig * (1.0 + gate * (1.0 - sig))).astype(jnp.bfloat16)
-    silu = silu.astype(jnp.bfloat16)
+    slope, silu, hidden = make_factors(gate_up)
 
     me = lax.axis_index("dp")
     at = (me // SIDE, me % SIDE)
@@ -321,7 +325,7 @@
 
     to_give = jnp.stack([t[0] for t in tables])
     to_keep = jnp.stack([t[1] for t in tables])
-    dgu, rows_dy, *gives = make_gives(to_give, w_out_t, slope, silu, hidden, rows_x, rows_dy)
+    dgu, *gives = make_gives(to_give, w_out_t, slope, silu, hidden, rows_x, rows_dy)
     gots = [None] * 4
     for f in (3, 0, 1, 2):
         gots[f] = lax.ppermute(gives[f], "dp", pair_perm(*FLOWS[f]))

time: 204 us -> 203 us (level)
  transfers between devices with their start and end apart: 19 -> 19, of which waited for: 11 -> 11; matrix products, arithmetic and copies ran while one was open for 10% -> 9% of each run, Pallas kernels for 7% -> 8%
where the time goes in v4:
time: 203 us; the launch traced here: 202 us
  waiting for transfers between devices  104 us (51%)
  starting transfers between devices  38.7 us (19%)
  Pallas kernels  28.1 us (14%)
  local copies, waits for them, and re-layouts  15 us (7%)
  matrix products  8.59 us (4%)
  other arithmetic  6.78 us (3%)
    all_to_all x2, waiting for transfers between devices, send(): lax.all_to_all(packed, 'expert', split_axis=0, concat_axis=0, tiled=True)  79.9 us
    ppermute x12, waiting for transfers between devices, local(): got = lax.ppermute(give, 'dp', pair_perm(axis, odd))  22.2 us
    unnamed x19, local copies, waits for them, and re-layouts  14.3 us
    ppermute x12, starting transfers between devices, local(): got = lax.ppermute(give, 'dp', pair_perm(axis, odd))  14.1 us
    all_to_all x2, starting transfers between devices, send(): lax.all_to_all(packed, 'expert', split_axis=0, concat_axis=0, tiled=True)  13.3 us
    pallas_call x2, Pallas kernels, pack(): pl.pallas_call(pack_kernel, grid=(width // tile,), in_specs=[pl.BlockSpec...  8.74 us
    pallas_call x1, Pallas kernels, make_gives(): pl.pallas_call(gives_kernel, in_specs=[pl.BlockSpec(memory_space=pltpu.SM...  8.49 us
    ppermute x4, starting transfers between devices, local(): gots[f] = lax.ppermute(gives[f], 'dp', pair_perm(*FLOWS[f]))  6.52 us
  transfers between devices with their start and end apart: 19, of which 11 were waited for; matrix products, arithmetic and copies ran while one was open for 9% of the time, Pallas kernels for 8%

profile of v4, /device:TPU:2, one launch (start us, length us, event | category | flops | bytes accessed | tf_op | source)
XLA Modules:
  0.0 202.3 jit_solution(14081897307634982495)
XLA Ops:
  0.6 4.4 %pack.2 = (bf16[512,2048]{1,0:T(8,128)(2,1)}, s32[1,160]{1,0:T(1,128)}) custom-call(s32[1,160]{1,0:T(1,128)} %bitcast.38, bf16[160,2048]{1,0:T(8,128)(2,1)} %values_ref.2), custom_call_target="tpu_custom_call" | custom-call | flops 1000000 | bytes 100000 | tf_op jit(solution)/shard_map/pack/pallas_call | solution.py:41
  5.0 8.6 %all-to-all-start = ((bf16[16,32,2048]{2,1,0:T(8,128)(2,1)}), bf16[16,32,2048]{2,1,0:T(8,128)(2,1)S(1)}, u32[]{:S(2)}, u32[]{:S(2)}) async-start(bf16[16,32,2048]{2,1,0:T(8,128)(2,1)} %bitcast.37), calls=%async_computation | async-start | bytes 4194304 | tf_op jit(solution)/shard_map/all_to_all | solution.py:306
  13.6 4.4 %pack.3 = (bf16[512,2048]{1,0:T(8,128)(2,1)}, s32[1,160]{1,0:T(1,128)}) custom-call(s32[1,160]{1,0:T(1,128)} %bitcast.39, bf16[160,2048]{1,0:T(8,128)(2,1)} %values_ref.3), custom_call_target="tpu_custom_call" | custom-call | flops 1000000 | bytes 100000 | tf_op jit(solution)/shard_map/pack/pallas_call | solution.py:41
  17.9 44.8 %all-to-all-done = bf16[16,32,2048]{2,1,0:T(8,128)(2,1)S(1)} async-done(((bf16[16,32,2048]{2,1,0:T(8,128)(2,1)}), bf16[16,32,2048]{2,1,0:T(8,128)(2,1)S(1)}, u32[]{:S(2)}, u32[]{:S(2)}) %all-to-all-start) | async-done | bytes 2097184 | tf_op jit(solution)/shard_map/all_to_all | solution.py:306
  62.7 4.8 %all-to-all-start.1 = ((bf16[16,32,2048]{2,1,0:T(8,128)(2,1)}), bf16[16,32,2048]{2,1,0:T(8,128)(2,1)}, u32[]{:S(2)}, u32[]{:S(2)}) async-start(bf16[16,32,2048]{2,1,0:T(8,128)(2,1)} %bitcast.36), calls=%async_computation.1 | async-start | bytes 4194304 | tf_op jit(solution)/shard_map/all_to_all | solution.py:306
  67.6 0.1 add_multiply_fusion
  67.6 0.1 add_multiply_fusion.1
  67.9 0.1 add.257
  68.0 0.1 add_multiply_fusion.2
  68.0 0.1 pad_add_fusion.2
  68.1 0.1 pad_add_fusion.3
  68.3 0.1 add.269
  68.4 0.1 add.261
  68.6 0.1 add.265
  68.7 4.8 %copy.8 = bf16[1,2048,768]{1,2,0:T(8,128)(2,1)} copy(bf16[1,2048,768]{2,1,0:T(8,128)(2,1)} %param.9) | data formatting | bytes 6291456 | tf_op args[4]
  73.4 5.6 %convolution_bitcast_fusion.gate_up_ref = f32[1536,512]{1,0:T(8,128)S(1)} fusion(bf16[512,2048]{1,0:T(8,128)(2,1)S(1)} %bitcast.30, bf16[1,2048,1536]{2,1,0:T(8,128)(2,1)} %param.8), kind=kOutput, calls=%fused_computation | convolution fusion | flops 3221225472 | bytes 11534336 | tf_op jit(solution)/shard_map/dot_general | solution.py:317
  79.0 0.8 factors.1
  79.9 0.9 copy-done.4
  80.8 0.9 copy-done.6
  81.7 35.1 %all-to-all-done.1 = bf16[16,32,2048]{2,1,0:T(8,128)(2,1)} async-done(((bf16[16,32,2048]{2,1,0:T(8,128)(2,1)}), bf16[16,32,2048]{2,1,0:T(8,128)(2,1)}, u32[]{:S(2)}, u32[]{:S(2)}) %all-to-all-start.1) | async-done | bytes 2097184 | tf_op jit(solution)/shard_map/all_to_all | solution.py:306
  116.8 1.1 copy-done.5
  117.9 1.1 copy-done.7
  119.0 8.5 %give.1 = (bf16[1536,512]{1,0:T(8,128)(2,1)S(1)}, bf16[576,1024]{1,0:T(8,128)(2,1)}, bf16[576,1024]{1,0:T(8,128)(2,1)}, bf16[576,1024]{1,0:T(8,128)(2,1)}, bf16[576,1024]{1,0:T(8,128)(2,1)}) custom-call(s32[4,8]{1,0:T(4,128)S(1)} %pad_add_fusion.table, bf16[768,2048]{1,0:T(8,128)(2,1)} %bitcast.35, bf16[768,512]{1,0:T(8,128)(2,1)S(1)} %get-tuple-element.26.hid_ref, ...), custom_call_target="tpu_custom_call" | custom-call | flops 1000000 | bytes 100000 | tf_op jit(solution)/shard_map/give/pallas_call | solution.py:168
  127.5 0.6 collective-permute-start
  128.1 2.2 %collective-permute-start.3 = (bf16[576,1024]{1,0:T(8,128)(2,1)}, bf16[576,1024]{1,0:T(8,128)(2,1)}, u32[]{:S(2)}, u32[]{:S(2)}) collective-permute-start(bf16[576,1024]{1,0:T(8,128)(2,1)} %get-tuple-element.34), channel_id=1, source_target_pairs={{0,192},{16,208},{32,224},{48,240},{64,128},{80,144},{96,160},{112... | collective-permute-start | bytes 3538952 | tf_op jit(solution)/shard_map/ppermute | solution.py:331
  130.3 1.6 collective-permute-start.6
  131.9 2.2 %collective-permute-start.9 = (bf16[576,1024]{1,0:T(8,128)(2,1)}, bf16[576,1024]{1,0:T(8,128)(2,1)}, u32[]{:S(2)}, u32[]{:S(2)}) collective-permute-start(bf16[576,1024]{1,0:T(8,128)(2,1)} %get-tuple-element.38), channel_id=1, source_target_pairs={{0,48},{16,32},{32,16},{48,0},{64,112},{80,96},{96,80},{112,64},{1... | collective-permute-start | bytes 3538952 | tf_op jit(solution)/shard_map/ppermute | solution.py:331
  134.1 2.8 %copy-done.1 = bf16[1,2048,1536]{2,1,0:T(8,128)(2,1)S(1)} copy-done((bf16[1,2048,1536]{2,1,0:T(8,128)(2,1)S(1)}, bf16[1,2048,1536]{2,1,0:T(8,128)(2,1)}, u32[]{:S(2)}) %copy-start.1) | copy-done | bytes 6291480
  136.9 4.6 %drows.1 = bf16[512,2048]{1,0:T(8,128)(2,1)S(1)} custom-call(bf16[1536,512]{1,0:T(8,128)(2,1)S(1)} %get-tuple-element.30.g_ref.dgu_ref, bf16[2048,1536]{1,0:T(8,128)(2,1)S(1)} %bitcast.34), custom_call_target="tpu_custom_call" | custom-call | flops 1000000 | bytes 100000 | tf_op jit(solution)/shard_map/drows/pallas_call | solution.py:225
  141.5 1.3 copy-done
  142.8 4.8 %all-to-all-start.2 = ((bf16[16,32,2048]{2,1,0:T(8,128)(2,1)}), bf16[16,32,2048]{2,1,0:T(8,128)(2,1)}, u32[]{:S(2)}, u32[]{:S(2)}) async-start(bf16[16,32,2048]{2,1,0:T(8,128)(2,1)} %bitcast.33), calls=%async_computation.2 | async-start | bytes 4194304 | tf_op jit(solution)/shard_map/all_to_all | solution.py:333
  147.6 0.1 add.272
  147.7 0.1 add.281
  147.8 0.1 add.275
  147.9 0.1 add.278
  148.0 1.4 copy-done.3
  149.4 4.4 %keep.1 = (bf16[576,1024]{1,0:T(8,128)(2,1)S(1)}, bf16[576,1024]{1,0:T(8,128)(2,1)S(1)}, bf16[576,1024]{1,0:T(8,128)(2,1)S(1)}, bf16[576,1024]{1,0:T(8,128)(2,1)S(1)}) custom-call(s32[4,8]{1,0:T(4,128)S(1)} %pad_add_fusion.1.table, bf16[1536,512]{1,0:T(8,128)(2,1)S(1)} %copy-done.3, bf16[768,512]{1,0:T(8,128)(2,1)S(1)} %get-tuple-element.26.hid_ref, ...), custom_call_target="tpu_custom_call" | custom-call | flops 1000000 | bytes 100000 | tf_op jit(solution)/shard_map/keep/pallas_call | solution.py:200
  153.8 2.2 %collective-permute-done = bf16[576,1024]{1,0:T(8,128)(2,1)} collective-permute-done((bf16[576,1024]{1,0:T(8,128)(2,1)}, bf16[576,1024]{1,0:T(8,128)(2,1)}, u32[]{:S(2)}, u32[]{:S(2)}) %collective-permute-start) | collective-permute-done | bytes 1179680 | tf_op jit(solution)/shard_map/ppermute | solution.py:331
  156.0 1.4 slice_add_fusion.7
  157.4 1.6 collective-permute-start.1
  159.0 1.4 slice_add_fusion.5
  160.4 1.9 collective-permute-start.4
  162.3 1.4 slice_add_fusion.3
  163.7 3.1 %collective-permute-start.7 = (bf16[576,512]{1,0:T(8,128)(2,1)S(1)}, bf16[576,512]{1,0:T(8,128)(2,1)S(1)}, u32[]{:S(2)}, u32[]{:S(2)}) collective-permute-start(bf16[576,512]{1,0:T(8,128)(2,1)S(1)} %get-tuple-element.44), channel_id=1, source_target_pairs={{0,48},{16,32},{32,16},{48,0},{64,112},{80,96},{96,80},{112,64},{1... | collective-permute-start | bytes 1769480 | tf_op jit(solution)/shard_map/ppermute | solution.py:356
  166.8 1.4 slice_add_fusion.1
  168.2 0.2 collective-permute-start.10
  168.4 3.6 %collective-permute-done.1 = bf16[576,512]{1,0:T(8,128)(2,1)S(1)} collective-permute-done((bf16[576,512]{1,0:T(8,128)(2,1)S(1)}, bf16[576,512]{1,0:T(8,128)(2,1)S(1)}, u32[]{:S(2)}, u32[]{:S(2)}) %collective-permute-start.1) | collective-permute-done | bytes 589856 | tf_op jit(solution)/shard_map/ppermute | solution.py:356
  172.1 1.6 collective-permute-start.2
  173.8 1.1 collective-permute-done.4
  174.9 3.1 %collective-permute-start.5 = (bf16[576,256]{1,0:T(8,128)(2,1)S(1)}, bf16[576,256]{1,0:T(8,128)(2,1)S(1)}, u32[]{:S(2)}, u32[]{:S(2)}) collective-permute-start(bf16[576,256]{1,0:T(8,128)(2,1)S(1)} %get-tuple-element.54), channel_id=1, source_target_pairs={{0,48},{16,32},{32,16},{48,0},{64,112},{80,96},{96,80},{112,64},{1... | collective-permute-start | bytes 884744 | tf_op jit(solution)/shard_map/ppermute | solution.py:356
  178.0 2.8 %collective-permute-done.7 = bf16[576,512]{1,0:T(8,128)(2,1)S(1)} collective-permute-done((bf16[576,512]{1,0:T(8,128)(2,1)S(1)}, bf16[576,512]{1,0:T(8,128)(2,1)S(1)}, u32[]{:S(2)}, u32[]{:S(2)}) %collective-permute-start.7) | collective-permute-done | bytes 589856 | tf_op jit(solution)/shard_map/ppermute | solution.py:356
  180.9 0.1 collective-permute-start.8
  181.0 3.5 %collective-permute-done.10 = bf16[576,512]{1,0:T(8,128)(2,1)S(1)} collective-permute-done((bf16[576,512]{1,0:T(8,128)(2,1)S(1)}, bf16[576,512]{1,0:T(8,128)(2,1)S(1)}, u32[]{:S(2)}, u32[]{:S(2)}) %collective-permute-start.10) | collective-permute-done | bytes 589856 | tf_op jit(solution)/shard_map/ppermute | solution.py:356
  184.6 0.1 collective-permute-start.11
  184.7 3.6 %collective-permute-done.2 = bf16[576,256]{1,0:T(8,128)(2,1)S(1)} collective-permute-done((bf16[576,256]{1,0:T(8,128)(2,1)S(1)}, bf16[576,256]{1,0:T(8,128)(2,1)S(1)}, u32[]{:S(2)}, u32[]{:S(2)}) %collective-permute-start.2) | collective-permute-done | bytes 294944 | tf_op jit(solution)/shard_map/ppermute | solution.py:356
  188.4 0.4 collective-permute-start.12
  188.9 0.3 collective-permute-start.13
  189.2 0.1 collective-permute-start.14
  189.3 3.7 %collective-permute-done.11 = bf16[576,256]{1,0:T(8,128)(2,1)S(1)} collective-permute-done((bf16[576,256]{1,0:T(8,128)(2,1)S(1)}, bf16[576,256]{1,0:T(8,128)(2,1)S(1)}, u32[]{:S(2)}, u32[]{:S(2)}) %collective-permute-start.11) | collective-permute-done | bytes 294944 | tf_op jit(solution)/shard_map/ppermute | solution.py:356
  193.1 1.5 collective-permute-start.15
  194.6 0.3 collective-permute-done.12.refs_4_
  194.9 3.4 %collective-permute-done.15.refs_7_ = bf16[576,128]{1,0:T(8,128)(2,1)S(1)} collective-permute-done((bf16[576,128]{1,0:T(8,128)(2,1)S(1)}, bf16[576,128]{1,0:T(8,128)(2,1)S(1)}, u32[]{:S(2)}, u32[]{:S(2)}) %collective-permute-start.15) | collective-permute-done | bytes 147488 | tf_op jit(solution)/shard_map/ppermute | solution.py:356
  198.3 1.0 finish.1
  199.3 3.0 %convolution_convert_fusion = bf16[160,2048]{1,0:T(8,128)(2,1)} fusion(bf16[512,2048]{1,0:T(8,128)(2,1)} %bitcast.21, s32[160]{0:T(256)S(1)} %bitcast.40), kind=kOutput, calls=%fused_computation.1 | convolution fusion | flops 335953920 | bytes 2753152 | tf_op jit(solution)/shard_map/dot_general | solution.py:337
  (34 shorter events, 0.8 us)
Async XLA Ops:
  5.0 57.7 %all-to-all-start = ((bf16[16,32,2048]{2,1,0:T(8,128)(2,1)}), bf16[16,32,2048]{2,1,0:T(8,128)(2,1)S(1)}, u32[]{:S(2)}, u32[]{:S(2)}) async-start(bf16[16,32,2048]{2,1,0:T(8,128)(2,1)} %bitcast.37), calls=%async_computation | async-start | bytes 4194304 | tf_op jit(solution)/shard_map/all_to_all | solution.py:306
  62.7 54.0 %all-to-all-start.1 = ((bf16[16,32,2048]{2,1,0:T(8,128)(2,1)}), bf16[16,32,2048]{2,1,0:T(8,128)(2,1)}, u32[]{:S(2)}, u32[]{:S(2)}) async-start(bf16[16,32,2048]{2,1,0:T(8,128)(2,1)} %bitcast.36), calls=%async_computation.1 | async-start | bytes 4194304 | tf_op jit(solution)/shard_map/all_to_all | solution.py:306
  79.9 0.9 copy-start.4
  80.8 0.9 copy-start.6
  116.8 1.1 copy-start.5
  117.9 1.1 copy-start.7
  127.5 13.9 %copy-start.2 = (bf16[1536,512]{1,0:T(8,128)(2,1)}, bf16[1536,512]{1,0:T(8,128)(2,1)S(1)}, u32[]{:S(2)}) copy-start(bf16[1536,512]{1,0:T(8,128)(2,1)S(1)} %get-tuple-element.30.g_ref.dgu_ref) | copy-start | bytes 4718596
  127.5 28.4 %collective-permute-start = (bf16[576,1024]{1,0:T(8,128)(2,1)}, bf16[576,1024]{1,0:T(8,128)(2,1)}, u32[]{:S(2)}, u32[]{:S(2)}) collective-permute-start(bf16[576,1024]{1,0:T(8,128)(2,1)} %get-tuple-element.32), channel_id=1, source_target_pairs={{0,64},{16,80},{32,96},{48,112},{64,0},{80,16},{96,32},{112,48},{1... | collective-permute-start | bytes 3538952 | tf_op jit(solution)/shard_map/ppermute | solution.py:331
  128.1 30.8 %collective-permute-start.3 = (bf16[576,1024]{1,0:T(8,128)(2,1)}, bf16[576,1024]{1,0:T(8,128)(2,1)}, u32[]{:S(2)}, u32[]{:S(2)}) collective-permute-start(bf16[576,1024]{1,0:T(8,128)(2,1)} %get-tuple-element.34), channel_id=1, source_target_pairs={{0,192},{16,208},{32,224},{48,240},{64,128},{80,144},{96,160},{112... | collective-permute-start | bytes 3538952 | tf_op jit(solution)/shard_map/ppermute | solution.py:331
  130.3 32.0 %collective-permute-start.6 = (bf16[576,1024]{1,0:T(8,128)(2,1)}, bf16[576,1024]{1,0:T(8,128)(2,1)}, u32[]{:S(2)}, u32[]{:S(2)}) collective-permute-start(bf16[576,1024]{1,0:T(8,128)(2,1)} %get-tuple-element.36), channel_id=1, source_target_pairs={{0,16},{16,0},{32,48},{48,32},{64,80},{80,64},{96,112},{112,96},{1... | collective-permute-start | bytes 3538952 | tf_op jit(solution)/shard_map/ppermute | solution.py:331
  131.9 34.9 %collective-permute-start.9 = (bf16[576,1024]{1,0:T(8,128)(2,1)}, bf16[576,1024]{1,0:T(8,128)(2,1)}, u32[]{:S(2)}, u32[]{:S(2)}) collective-permute-start(bf16[576,1024]{1,0:T(8,128)(2,1)} %get-tuple-element.38), channel_id=1, source_target_pairs={{0,48},{16,32},{32,16},{48,0},{64,112},{80,96},{96,80},{112,64},{1... | collective-permute-start | bytes 3538952 | tf_op jit(solution)/shard_map/ppermute | solution.py:331
  134.1 2.8 %copy-start.1 = (bf16[1,2048,1536]{2,1,0:T(8,128)(2,1)S(1)}, bf16[1,2048,1536]{2,1,0:T(8,128)(2,1)}, u32[]{:S(2)}) copy-start(bf16[1,2048,1536]{2,1,0:T(8,128)(2,1)} %param.8) | copy-start | bytes 18874372
  141.5 1.3 copy-start
  142.8 56.5 %all-to-all-start.2 = ((bf16[16,32,2048]{2,1,0:T(8,128)(2,1)}), bf16[16,32,2048]{2,1,0:T(8,128)(2,1)}, u32[]{:S(2)}, u32[]{:S(2)}) async-start(bf16[16,32,2048]{2,1,0:T(8,128)(2,1)} %bitcast.33), calls=%async_computation.2 | async-start | bytes 4194304 | tf_op jit(solution)/shard_map/all_to_all | solution.py:333
  148.0 1.4 copy-start.3
  157.4 14.7 %collective-permute-start.1 = (bf16[576,512]{1,0:T(8,128)(2,1)S(1)}, bf16[576,512]{1,0:T(8,128)(2,1)S(1)}, u32[]{:S(2)}, u32[]{:S(2)}) collective-permute-start(bf16[576,512]{1,0:T(8,128)(2,1)S(1)} %get-tuple-element.48), channel_id=1, source_target_pairs={{0,192},{16,208},{32,224},{48,240},{64,128},{80,144},{96,160},{112... | collective-permute-start | bytes 1769480 | tf_op jit(solution)/shard_map/ppermute | solution.py:356
  160.4 14.5 %collective-permute-start.4 = (bf16[576,512]{1,0:T(8,128)(2,1)S(1)}, bf16[576,512]{1,0:T(8,128)(2,1)S(1)}, u32[]{:S(2)}, u32[]{:S(2)}) collective-permute-start(bf16[576,512]{1,0:T(8,128)(2,1)S(1)} %get-tuple-element.46), channel_id=1, source_target_pairs={{0,64},{16,80},{32,96},{48,112},{64,0},{80,16},{96,32},{112,48},{1... | collective-permute-start | bytes 1769480 | tf_op jit(solution)/shard_map/ppermute | solution.py:356
  163.7 17.2 %collective-permute-start.7 = (bf16[576,512]{1,0:T(8,128)(2,1)S(1)}, bf16[576,512]{1,0:T(8,128)(2,1)S(1)}, u32[]{:S(2)}, u32[]{:S(2)}) collective-permute-start(bf16[576,512]{1,0:T(8,128)(2,1)S(1)} %get-tuple-element.44), channel_id=1, source_target_pairs={{0,48},{16,32},{32,16},{48,0},{64,112},{80,96},{96,80},{112,64},{1... | collective-permute-start | bytes 1769480 | tf_op jit(solution)/shard_map/ppermute | solution.py:356
  168.2 16.4 %collective-permute-start.10 = (bf16[576,512]{1,0:T(8,128)(2,1)S(1)}, bf16[576,512]{1,0:T(8,128)(2,1)S(1)}, u32[]{:S(2)}, u32[]{:S(2)}) collective-permute-start(bf16[576,512]{1,0:T(8,128)(2,1)S(1)} %get-tuple-element.42), channel_id=1, source_target_pairs={{0,16},{16,0},{32,48},{48,32},{64,80},{80,64},{96,112},{112,96},{1... | collective-permute-start | bytes 1769480 | tf_op jit(solution)/shard_map/ppermute | solution.py:356
  172.1 16.3 %collective-permute-start.2 = (bf16[576,256]{1,0:T(8,128)(2,1)S(1)}, bf16[576,256]{1,0:T(8,128)(2,1)S(1)}, u32[]{:S(2)}, u32[]{:S(2)}) collective-permute-start(bf16[576,256]{1,0:T(8,128)(2,1)S(1)} %get-tuple-element.56), channel_id=1, source_target_pairs={{0,16},{16,0},{32,48},{48,32},{64,80},{80,64},{96,112},{112,96},{1... | collective-permute-start | bytes 884744 | tf_op jit(solution)/shard_map/ppermute | solution.py:356
  174.9 13.9 %collective-permute-start.5 = (bf16[576,256]{1,0:T(8,128)(2,1)S(1)}, bf16[576,256]{1,0:T(8,128)(2,1)S(1)}, u32[]{:S(2)}, u32[]{:S(2)}) collective-permute-start(bf16[576,256]{1,0:T(8,128)(2,1)S(1)} %get-tuple-element.54), channel_id=1, source_target_pairs={{0,48},{16,32},{32,16},{48,0},{64,112},{80,96},{96,80},{112,64},{1... | collective-permute-start | bytes 884744 | tf_op jit(solution)/shard_map/ppermute | solution.py:356
  180.9 8.2 %collective-permute-start.8 = (bf16[576,256]{1,0:T(8,128)(2,1)S(1)}, bf16[576,256]{1,0:T(8,128)(2,1)S(1)}, u32[]{:S(2)}, u32[]{:S(2)}) collective-permute-start(bf16[576,256]{1,0:T(8,128)(2,1)S(1)} %get-tuple-element.52), channel_id=1, source_target_pairs={{0,64},{16,80},{32,96},{48,112},{64,0},{80,16},{96,32},{112,48},{1... | collective-permute-start | bytes 884744 | tf_op jit(solution)/shard_map/ppermute | solution.py:356
  184.6 8.4 %collective-permute-start.11 = (bf16[576,256]{1,0:T(8,128)(2,1)S(1)}, bf16[576,256]{1,0:T(8,128)(2,1)S(1)}, u32[]{:S(2)}, u32[]{:S(2)}) collective-permute-start(bf16[576,256]{1,0:T(8,128)(2,1)S(1)} %get-tuple-element.50), channel_id=1, source_target_pairs={{0,192},{16,208},{32,224},{48,240},{64,128},{80,144},{96,160},{112... | collective-permute-start | bytes 884744 | tf_op jit(solution)/shard_map/ppermute | solution.py:356
  188.4 6.4 %collective-permute-start.12 = (bf16[576,128]{1,0:T(8,128)(2,1)S(1)}, bf16[576,128]{1,0:T(8,128)(2,1)S(1)}, u32[]{:S(2)}, u32[]{:S(2)}) collective-permute-start(bf16[576,128]{1,0:T(8,128)(2,1)S(1)} %get-tuple-element.63), channel_id=1, source_target_pairs={{0,48},{16,32},{32,16},{48,0},{64,112},{80,96},{96,80},{112,64},{1... | collective-permute-start | bytes 442376 | tf_op jit(solution)/shard_map/ppermute | solution.py:356
  188.9 6.0 %collective-permute-start.13 = (bf16[576,128]{1,0:T(8,128)(2,1)S(1)}, bf16[576,128]{1,0:T(8,128)(2,1)S(1)}, u32[]{:S(2)}, u32[]{:S(2)}) collective-permute-start(bf16[576,128]{1,0:T(8,128)(2,1)S(1)} %get-tuple-element.61), channel_id=1, source_target_pairs={{0,16},{16,0},{32,48},{48,32},{64,80},{80,64},{96,112},{112,96},{1... | collective-permute-start | bytes 442376 | tf_op jit(solution)/shard_map/ppermute | solution.py:356
  189.2 5.6 %collective-permute-start.14 = (bf16[576,128]{1,0:T(8,128)(2,1)S(1)}, bf16[576,128]{1,0:T(8,128)(2,1)S(1)}, u32[]{:S(2)}, u32[]{:S(2)}) collective-permute-start(bf16[576,128]{1,0:T(8,128)(2,1)S(1)} %get-tuple-element.59), channel_id=1, source_target_pairs={{0,192},{16,208},{32,224},{48,240},{64,128},{80,144},{96,160},{112... | collective-permute-start | bytes 442376 | tf_op jit(solution)/shard_map/ppermute | solution.py:356
  193.1 5.2 %collective-permute-start.15 = (bf16[576,128]{1,0:T(8,128)(2,1)S(1)}, bf16[576,128]{1,0:T(8,128)(2,1)S(1)}, u32[]{:S(2)}, u32[]{:S(2)}) collective-permute-start(bf16[576,128]{1,0:T(8,128)(2,1)S(1)} %get-tuple-element.57), channel_id=1, source_target_pairs={{0,64},{16,80},{32,96},{48,112},{64,0},{80,16},{96,32},{112,48},{1... | collective-permute-start | bytes 442376 | tf_op jit(solution)/shard_map/ppermute | solution.py:356
  198.3 1.0 copy-start.8

commit v5 on v4

--- a/solution.py
+++ b/solution.py
@@ -232,7 +232,7 @@
         out_specs=pl.BlockSpec((rows, tile), lambda i: (0, i)),
         out_shape=jax.ShapeDtypeStruct((rows, width), jnp.bfloat16),
         scratch_shapes=[pltpu.VMEM((rows, ff2), jnp.bfloat16)],
-        compiler_params=pltpu.CompilerParams(vmem_limit_bytes=16 * 1024 * 1024),
+        compiler_params=pltpu.CompilerParams(vmem_limit_bytes=50 * 1024 * 1024),
         cost_estimate=SMALL,
         name="drows",
     )(dgu_t, w_in)

time: 203 us -> 203 us (level)
  local copies, waits for them, and re-layouts: 15 us -> 12.2 us
    unnamed x19 -> x17, local copies, waits for them, and re-layouts: 14.3 us -> 11.6 us
where the time goes in v5:
time: 203 us; the launch traced here: 202 us
  waiting for transfers between devices  105 us (52%)
  starting transfers between devices  38.7 us (19%)
  Pallas kernels  29.9 us (15%)
  local copies, waits for them, and re-layouts  12.2 us (6%)
  matrix products  8.59 us (4%)
  other arithmetic  6.78 us (3%)
    all_to_all x2, waiting for transfers between devices, send(): lax.all_to_all(packed, 'expert', split_axis=0, concat_axis=0, tiled=True)  79.9 us
    ppermute x12, waiting for transfers between devices, local(): got = lax.ppermute(give, 'dp', pair_perm(axis, odd))  22.2 us
    ppermute x12, starting transfers between devices, local(): got = lax.ppermute(give, 'dp', pair_perm(axis, odd))  14 us
    all_to_all x2, starting transfers between devices, send(): lax.all_to_all(packed, 'expert', split_axis=0, concat_axis=0, tiled=True)  13.4 us
    unnamed x17, local copies, waits for them, and re-layouts  11.6 us
    pallas_call x2, Pallas kernels, pack(): pl.pallas_call(pack_kernel, grid=(width // tile,), in_specs=[pl.BlockSpec...  8.74 us
    pallas_call x1, Pallas kernels, make_gives(): pl.pallas_call(gives_kernel, in_specs=[pl.BlockSpec(memory_space=pltpu.SM...  8.48 us
    ppermute x4, starting transfers between devices, local(): gots[f] = lax.ppermute(gives[f], 'dp', pair_perm(*FLOWS[f]))  6.54 us
  transfers between devices with their start and end apart: 19, of which 11 were waited for; matrix products, arithmetic and copies ran while one was open for 9% of the time, Pallas kernels for 8%

profile of v5, /device:TPU:2, one launch (start us, length us, event | category | flops | bytes accessed | tf_op | source)
XLA Modules:
  0.0 202.3 jit_solution(17728916106124353383)
XLA Ops:
  0.6 4.4 %pack.2 = (bf16[512,2048]{1,0:T(8,128)(2,1)}, s32[1,160]{1,0:T(1,128)}) custom-call(s32[1,160]{1,0:T(1,128)} %bitcast.38, bf16[160,2048]{1,0:T(8,128)(2,1)} %values_ref.2), custom_call_target="tpu_custom_call" | custom-call | flops 1000000 | bytes 100000 | tf_op jit(solution)/shard_map/pack/pallas_call | solution.py:41
  5.0 8.6 %all-to-all-start = ((bf16[16,32,2048]{2,1,0:T(8,128)(2,1)}), bf16[16,32,2048]{2,1,0:T(8,128)(2,1)S(1)}, u32[]{:S(2)}, u32[]{:S(2)}) async-start(bf16[16,32,2048]{2,1,0:T(8,128)(2,1)} %bitcast.37), calls=%async_computation | async-start | bytes 4194304 | tf_op jit(solution)/shard_map/all_to_all | solution.py:306
  13.6 4.4 %pack.3 = (bf16[512,2048]{1,0:T(8,128)(2,1)}, s32[1,160]{1,0:T(1,128)}) custom-call(s32[1,160]{1,0:T(1,128)} %bitcast.39, bf16[160,2048]{1,0:T(8,128)(2,1)} %values_ref.3), custom_call_target="tpu_custom_call" | custom-call | flops 1000000 | bytes 100000 | tf_op jit(solution)/shard_map/pack/pallas_call | solution.py:41
  17.9 44.8 %all-to-all-done = bf16[16,32,2048]{2,1,0:T(8,128)(2,1)S(1)} async-done(((bf16[16,32,2048]{2,1,0:T(8,128)(2,1)}), bf16[16,32,2048]{2,1,0:T(8,128)(2,1)S(1)}, u32[]{:S(2)}, u32[]{:S(2)}) %all-to-all-start) | async-done | bytes 2097184 | tf_op jit(solution)/shard_map/all_to_all | solution.py:306
  62.8 4.8 %all-to-all-start.1 = ((bf16[16,32,2048]{2,1,0:T(8,128)(2,1)}), bf16[16,32,2048]{2,1,0:T(8,128)(2,1)}, u32[]{:S(2)}, u32[]{:S(2)}) async-start(bf16[16,32,2048]{2,1,0:T(8,128)(2,1)} %bitcast.36), calls=%async_computation.1 | async-start | bytes 4194304 | tf_op jit(solution)/shard_map/all_to_all | solution.py:306
  67.6 0.1 add_multiply_fusion
  67.7 0.1 add_multiply_fusion.1
  67.7 0.1 add_add_fusion
  67.9 0.1 add.257
  68.0 0.1 add_multiply_fusion.2
  68.0 0.1 pad_add_fusion.2
  68.1 0.1 pad_add_fusion.3
  68.3 0.1 add.269
  68.4 0.1 add.261
  68.6 0.1 add.265
  68.7 4.8 %copy.8 = bf16[1,2048,768]{1,2,0:T(8,128)(2,1)} copy(bf16[1,2048,768]{2,1,0:T(8,128)(2,1)} %param.9) | data formatting | bytes 6291456 | tf_op args[4]
  73.5 5.6 %convolution_bitcast_fusion.gate_up_ref = f32[1536,512]{1,0:T(8,128)S(1)} fusion(bf16[512,2048]{1,0:T(8,128)(2,1)S(1)} %bitcast.30, bf16[1,2048,1536]{2,1,0:T(8,128)(2,1)} %param.8), kind=kOutput, calls=%fused_computation | convolution fusion | flops 3221225472 | bytes 11534336 | tf_op jit(solution)/shard_map/dot_general | solution.py:317
  79.1 0.8 factors.1
  79.9 0.9 copy-done.3
  80.8 0.9 copy-done.5
  81.7 35.1 %all-to-all-done.1 = bf16[16,32,2048]{2,1,0:T(8,128)(2,1)} async-done(((bf16[16,32,2048]{2,1,0:T(8,128)(2,1)}), bf16[16,32,2048]{2,1,0:T(8,128)(2,1)}, u32[]{:S(2)}, u32[]{:S(2)}) %all-to-all-start.1) | async-done | bytes 2097184 | tf_op jit(solution)/shard_map/all_to_all | solution.py:306
  116.8 1.1 copy-done.4
  117.9 1.1 copy-done.6
  119.1 8.5 %give.1 = (bf16[1536,512]{1,0:T(8,128)(2,1)S(1)}, bf16[576,1024]{1,0:T(8,128)(2,1)}, bf16[576,1024]{1,0:T(8,128)(2,1)}, bf16[576,1024]{1,0:T(8,128)(2,1)}, bf16[576,1024]{1,0:T(8,128)(2,1)}) custom-call(s32[4,8]{1,0:T(4,128)S(1)} %pad_add_fusion.table, bf16[768,2048]{1,0:T(8,128)(2,1)} %bitcast.34, bf16[768,512]{1,0:T(8,128)(2,1)S(1)} %get-tuple-element.26.hid_ref, ...), custom_call_target="tpu_custom_call" | custom-call | flops 1000000 | bytes 100000 | tf_op jit(solution)/shard_map/give/pallas_call | solution.py:168
  127.5 0.6 collective-permute-start
  128.2 2.2 %collective-permute-start.3 = (bf16[576,1024]{1,0:T(8,128)(2,1)}, bf16[576,1024]{1,0:T(8,128)(2,1)}, u32[]{:S(2)}, u32[]{:S(2)}) collective-permute-start(bf16[576,1024]{1,0:T(8,128)(2,1)} %get-tuple-element.34), channel_id=1, source_target_pairs={{0,192},{16,208},{32,224},{48,240},{64,128},{80,144},{96,160},{112... | collective-permute-start | bytes 3538952 | tf_op jit(solution)/shard_map/ppermute | solution.py:331
  130.3 1.6 collective-permute-start.6
  131.9 2.2 %collective-permute-start.9 = (bf16[576,1024]{1,0:T(8,128)(2,1)}, bf16[576,1024]{1,0:T(8,128)(2,1)}, u32[]{:S(2)}, u32[]{:S(2)}) collective-permute-start(bf16[576,1024]{1,0:T(8,128)(2,1)} %get-tuple-element.38), channel_id=1, source_target_pairs={{0,48},{16,32},{32,16},{48,0},{64,112},{80,96},{96,80},{112,64},{1... | collective-permute-start | bytes 3538952 | tf_op jit(solution)/shard_map/ppermute | solution.py:331
  134.1 6.5 %drows.1 = bf16[512,2048]{1,0:T(8,128)(2,1)S(1)} custom-call(bf16[1536,512]{1,0:T(8,128)(2,1)S(1)} %get-tuple-element.30.g_ref.dgu_ref, bf16[2048,1536]{1,0:T(8,128)(2,1)} %bitcast.35), custom_call_target="tpu_custom_call" | custom-call | flops 1000000 | bytes 100000 | tf_op jit(solution)/shard_map/drows/pallas_call | solution.py:225
  140.6 1.3 copy-done
  141.9 4.8 %all-to-all-start.2 = ((bf16[16,32,2048]{2,1,0:T(8,128)(2,1)}), bf16[16,32,2048]{2,1,0:T(8,128)(2,1)}, u32[]{:S(2)}, u32[]{:S(2)}) async-start(bf16[16,32,2048]{2,1,0:T(8,128)(2,1)} %bitcast.33), calls=%async_computation.2 | async-start | bytes 4194304 | tf_op jit(solution)/shard_map/all_to_all | solution.py:333
  146.7 0.1 add.272
  146.8 0.1 add.281
  146.9 0.1 add.275
  147.0 0.1 add.278
  147.1 1.4 copy-done.2
  148.5 4.4 %keep.1 = (bf16[576,1024]{1,0:T(8,128)(2,1)S(1)}, bf16[576,1024]{1,0:T(8,128)(2,1)S(1)}, bf16[576,1024]{1,0:T(8,128)(2,1)S(1)}, bf16[576,1024]{1,0:T(8,128)(2,1)S(1)}) custom-call(s32[4,8]{1,0:T(4,128)S(1)} %pad_add_fusion.1.table, bf16[1536,512]{1,0:T(8,128)(2,1)S(1)} %copy-done.2, bf16[768,512]{1,0:T(8,128)(2,1)S(1)} %get-tuple-element.26.hid_ref, ...), custom_call_target="tpu_custom_call" | custom-call | flops 1000000 | bytes 100000 | tf_op jit(solution)/shard_map/keep/pallas_call | solution.py:200
  152.9 3.1 %collective-permute-done = bf16[576,1024]{1,0:T(8,128)(2,1)} collective-permute-done((bf16[576,1024]{1,0:T(8,128)(2,1)}, bf16[576,1024]{1,0:T(8,128)(2,1)}, u32[]{:S(2)}, u32[]{:S(2)}) %collective-permute-start) | collective-permute-done | bytes 1179680 | tf_op jit(solution)/shard_map/ppermute | solution.py:331
  156.0 1.4 slice_add_fusion.7
  157.4 1.6 collective-permute-start.1
  159.0 1.4 slice_add_fusion.5
  160.4 1.9 collective-permute-start.4
  162.3 1.4 slice_add_fusion.3
  163.7 3.1 %collective-permute-start.7 = (bf16[576,512]{1,0:T(8,128)(2,1)S(1)}, bf16[576,512]{1,0:T(8,128)(2,1)S(1)}, u32[]{:S(2)}, u32[]{:S(2)}) collective-permute-start(bf16[576,512]{1,0:T(8,128)(2,1)S(1)} %get-tuple-element.44), channel_id=1, source_target_pairs={{0,48},{16,32},{32,16},{48,0},{64,112},{80,96},{96,80},{112,64},{1... | collective-permute-start | bytes 1769480 | tf_op jit(solution)/shard_map/ppermute | solution.py:356
  166.8 1.4 slice_add_fusion.1
  168.2 0.2 collective-permute-start.10
  168.4 3.7 %collective-permute-done.1 = bf16[576,512]{1,0:T(8,128)(2,1)S(1)} collective-permute-done((bf16[576,512]{1,0:T(8,128)(2,1)S(1)}, bf16[576,512]{1,0:T(8,128)(2,1)S(1)}, u32[]{:S(2)}, u32[]{:S(2)}) %collective-permute-start.1) | collective-permute-done | bytes 589856 | tf_op jit(solution)/shard_map/ppermute | solution.py:356
  172.2 1.6 collective-permute-start.2
  173.8 1.1 collective-permute-done.4
  175.0 3.1 %collective-permute-start.5 = (bf16[576,256]{1,0:T(8,128)(2,1)S(1)}, bf16[576,256]{1,0:T(8,128)(2,1)S(1)}, u32[]{:S(2)}, u32[]{:S(2)}) collective-permute-start(bf16[576,256]{1,0:T(8,128)(2,1)S(1)} %get-tuple-element.54), channel_id=1, source_target_pairs={{0,48},{16,32},{32,16},{48,0},{64,112},{80,96},{96,80},{112,64},{1... | collective-permute-start | bytes 884744 | tf_op jit(solution)/shard_map/ppermute | solution.py:356
  178.1 2.8 %collective-permute-done.7 = bf16[576,512]{1,0:T(8,128)(2,1)S(1)} collective-permute-done((bf16[576,512]{1,0:T(8,128)(2,1)S(1)}, bf16[576,512]{1,0:T(8,128)(2,1)S(1)}, u32[]{:S(2)}, u32[]{:S(2)}) %collective-permute-start.7) | collective-permute-done | bytes 589856 | tf_op jit(solution)/shard_map/ppermute | solution.py:356
  181.0 0.1 collective-permute-start.8
  181.1 3.5 %collective-permute-done.10 = bf16[576,512]{1,0:T(8,128)(2,1)S(1)} collective-permute-done((bf16[576,512]{1,0:T(8,128)(2,1)S(1)}, bf16[576,512]{1,0:T(8,128)(2,1)S(1)}, u32[]{:S(2)}, u32[]{:S(2)}) %collective-permute-start.10) | collective-permute-done | bytes 589856 | tf_op jit(solution)/shard_map/ppermute | solution.py:356
  184.7 0.1 collective-permute-start.11
  184.8 3.6 %collective-permute-done.2 = bf16[576,256]{1,0:T(8,128)(2,1)S(1)} collective-permute-done((bf16[576,256]{1,0:T(8,128)(2,1)S(1)}, bf16[576,256]{1,0:T(8,128)(2,1)S(1)}, u32[]{:S(2)}, u32[]{:S(2)}) %collective-permute-start.2) | collective-permute-done | bytes 294944 | tf_op jit(solution)/shard_map/ppermute | solution.py:356
  188.4 0.4 collective-permute-start.12
  188.9 0.3 collective-permute-start.13
  189.3 0.1 collective-permute-start.14
  189.4 3.7 %collective-permute-done.11 = bf16[576,256]{1,0:T(8,128)(2,1)S(1)} collective-permute-done((bf16[576,256]{1,0:T(8,128)(2,1)S(1)}, bf16[576,256]{1,0:T(8,128)(2,1)S(1)}, u32[]{:S(2)}, u32[]{:S(2)}) %collective-permute-start.11) | collective-permute-done | bytes 294944 | tf_op jit(solution)/shard_map/ppermute | solution.py:356
  193.1 1.5 collective-permute-start.15
  194.6 0.3 collective-permute-done.12.refs_4_
  194.9 3.4 %collective-permute-done.15.refs_7_ = bf16[576,128]{1,0:T(8,128)(2,1)S(1)} collective-permute-done((bf16[576,128]{1,0:T(8,128)(2,1)S(1)}, bf16[576,128]{1,0:T(8,128)(2,1)S(1)}, u32[]{:S(2)}, u32[]{:S(2)}) %collective-permute-start.15) | collective-permute-done | bytes 147488 | tf_op jit(solution)/shard_map/ppermute | solution.py:356
  198.3 1.0 finish.1
  199.3 3.0 %convolution_convert_fusion = bf16[160,2048]{1,0:T(8,128)(2,1)} fusion(bf16[512,2048]{1,0:T(8,128)(2,1)} %bitcast.21, s32[160]{0:T(256)S(1)} %bitcast.40), kind=kOutput, calls=%fused_computation.1 | convolution fusion | flops 335953920 | bytes 2753152 | tf_op jit(solution)/shard_map/dot_general | solution.py:337
  (32 shorter events, 0.8 us)
Async XLA Ops:
  5.0 57.7 %all-to-all-start = ((bf16[16,32,2048]{2,1,0:T(8,128)(2,1)}), bf16[16,32,2048]{2,1,0:T(8,128)(2,1)S(1)}, u32[]{:S(2)}, u32[]{:S(2)}) async-start(bf16[16,32,2048]{2,1,0:T(8,128)(2,1)} %bitcast.37), calls=%async_computation | async-start | bytes 4194304 | tf_op jit(solution)/shard_map/all_to_all | solution.py:306
  62.8 54.0 %all-to-all-start.1 = ((bf16[16,32,2048]{2,1,0:T(8,128)(2,1)}), bf16[16,32,2048]{2,1,0:T(8,128)(2,1)}, u32[]{:S(2)}, u32[]{:S(2)}) async-start(bf16[16,32,2048]{2,1,0:T(8,128)(2,1)} %bitcast.36), calls=%async_computation.1 | async-start | bytes 4194304 | tf_op jit(solution)/shard_map/all_to_all | solution.py:306
  79.9 0.9 copy-start.3
  80.8 0.9 copy-start.5
  116.8 1.1 copy-start.4
  117.9 1.1 copy-start.6
  127.5 13.1 %copy-start.1 = (bf16[1536,512]{1,0:T(8,128)(2,1)}, bf16[1536,512]{1,0:T(8,128)(2,1)S(1)}, u32[]{:S(2)}) copy-start(bf16[1536,512]{1,0:T(8,128)(2,1)S(1)} %get-tuple-element.30.g_ref.dgu_ref) | copy-start | bytes 4718596
  127.5 28.5 %collective-permute-start = (bf16[576,1024]{1,0:T(8,128)(2,1)}, bf16[576,1024]{1,0:T(8,128)(2,1)}, u32[]{:S(2)}, u32[]{:S(2)}) collective-permute-start(bf16[576,1024]{1,0:T(8,128)(2,1)} %get-tuple-element.32), channel_id=1, source_target_pairs={{0,64},{16,80},{32,96},{48,112},{64,0},{80,16},{96,32},{112,48},{1... | collective-permute-start | bytes 3538952 | tf_op jit(solution)/shard_map/ppermute | solution.py:331
  128.2 30.8 %collective-permute-start.3 = (bf16[576,1024]{1,0:T(8,128)(2,1)}, bf16[576,1024]{1,0:T(8,128)(2,1)}, u32[]{:S(2)}, u32[]{:S(2)}) collective-permute-start(bf16[576,1024]{1,0:T(8,128)(2,1)} %get-tuple-element.34), channel_id=1, source_target_pairs={{0,192},{16,208},{32,224},{48,240},{64,128},{80,144},{96,160},{112... | collective-permute-start | bytes 3538952 | tf_op jit(solution)/shard_map/ppermute | solution.py:331
  130.3 32.0 %collective-permute-start.6 = (bf16[576,1024]{1,0:T(8,128)(2,1)}, bf16[576,1024]{1,0:T(8,128)(2,1)}, u32[]{:S(2)}, u32[]{:S(2)}) collective-permute-start(bf16[576,1024]{1,0:T(8,128)(2,1)} %get-tuple-element.36), channel_id=1, source_target_pairs={{0,16},{16,0},{32,48},{48,32},{64,80},{80,64},{96,112},{112,96},{1... | collective-permute-start | bytes 3538952 | tf_op jit(solution)/shard_map/ppermute | solution.py:331
  131.9 34.9 %collective-permute-start.9 = (bf16[576,1024]{1,0:T(8,128)(2,1)}, bf16[576,1024]{1,0:T(8,128)(2,1)}, u32[]{:S(2)}, u32[]{:S(2)}) collective-permute-start(bf16[576,1024]{1,0:T(8,128)(2,1)} %get-tuple-element.38), channel_id=1, source_target_pairs={{0,48},{16,32},{32,16},{48,0},{64,112},{80,96},{96,80},{112,64},{1... | collective-permute-start | bytes 3538952 | tf_op jit(solution)/shard_map/ppermute | solution.py:331
  140.6 1.3 copy-start
  141.9 57.4 %all-to-all-start.2 = ((bf16[16,32,2048]{2,1,0:T(8,128)(2,1)}), bf16[16,32,2048]{2,1,0:T(8,128)(2,1)}, u32[]{:S(2)}, u32[]{:S(2)}) async-start(bf16[16,32,2048]{2,1,0:T(8,128)(2,1)} %bitcast.33), calls=%async_computation.2 | async-start | bytes 4194304 | tf_op jit(solution)/shard_map/all_to_all | solution.py:333
  147.1 1.4 copy-start.2
  157.4 14.7 %collective-permute-start.1 = (bf16[576,512]{1,0:T(8,128)(2,1)S(1)}, bf16[576,512]{1,0:T(8,128)(2,1)S(1)}, u32[]{:S(2)}, u32[]{:S(2)}) collective-permute-start(bf16[576,512]{1,0:T(8,128)(2,1)S(1)} %get-tuple-element.48), channel_id=1, source_target_pairs={{0,192},{16,208},{32,224},{48,240},{64,128},{80,144},{96,160},{112... | collective-permute-start | bytes 1769480 | tf_op jit(solution)/shard_map/ppermute | solution.py:356
  160.4 14.5 %collective-permute-start.4 = (bf16[576,512]{1,0:T(8,128)(2,1)S(1)}, bf16[576,512]{1,0:T(8,128)(2,1)S(1)}, u32[]{:S(2)}, u32[]{:S(2)}) collective-permute-start(bf16[576,512]{1,0:T(8,128)(2,1)S(1)} %get-tuple-element.46), channel_id=1, source_target_pairs={{0,64},{16,80},{32,96},{48,112},{64,0},{80,16},{96,32},{112,48},{1... | collective-permute-start | bytes 1769480 | tf_op jit(solution)/shard_map/ppermute | solution.py:356
  163.7 17.2 %collective-permute-start.7 = (bf16[576,512]{1,0:T(8,128)(2,1)S(1)}, bf16[576,512]{1,0:T(8,128)(2,1)S(1)}, u32[]{:S(2)}, u32[]{:S(2)}) collective-permute-start(bf16[576,512]{1,0:T(8,128)(2,1)S(1)} %get-tuple-element.44), channel_id=1, source_target_pairs={{0,48},{16,32},{32,16},{48,0},{64,112},{80,96},{96,80},{112,64},{1... | collective-permute-start | bytes 1769480 | tf_op jit(solution)/shard_map/ppermute | solution.py:356
  168.2 16.4 %collective-permute-start.10 = (bf16[576,512]{1,0:T(8,128)(2,1)S(1)}, bf16[576,512]{1,0:T(8,128)(2,1)S(1)}, u32[]{:S(2)}, u32[]{:S(2)}) collective-permute-start(bf16[576,512]{1,0:T(8,128)(2,1)S(1)} %get-tuple-element.42), channel_id=1, source_target_pairs={{0,16},{16,0},{32,48},{48,32},{64,80},{80,64},{96,112},{112,96},{1... | collective-permute-start | bytes 1769480 | tf_op jit(solution)/shard_map/ppermute | solution.py:356
  172.2 16.2 %collective-permute-start.2 = (bf16[576,256]{1,0:T(8,128)(2,1)S(1)}, bf16[576,256]{1,0:T(8,128)(2,1)S(1)}, u32[]{:S(2)}, u32[]{:S(2)}) collective-permute-start(bf16[576,256]{1,0:T(8,128)(2,1)S(1)} %get-tuple-element.56), channel_id=1, source_target_pairs={{0,16},{16,0},{32,48},{48,32},{64,80},{80,64},{96,112},{112,96},{1... | collective-permute-start | bytes 884744 | tf_op jit(solution)/shard_map/ppermute | solution.py:356
  175.0 13.9 %collective-permute-start.5 = (bf16[576,256]{1,0:T(8,128)(2,1)S(1)}, bf16[576,256]{1,0:T(8,128)(2,1)S(1)}, u32[]{:S(2)}, u32[]{:S(2)}) collective-permute-start(bf16[576,256]{1,0:T(8,128)(2,1)S(1)} %get-tuple-element.54), channel_id=1, source_target_pairs={{0,48},{16,32},{32,16},{48,0},{64,112},{80,96},{96,80},{112,64},{1... | collective-permute-start | bytes 884744 | tf_op jit(solution)/shard_map/ppermute | solution.py:356
  181.0 8.3 %collective-permute-start.8 = (bf16[576,256]{1,0:T(8,128)(2,1)S(1)}, bf16[576,256]{1,0:T(8,128)(2,1)S(1)}, u32[]{:S(2)}, u32[]{:S(2)}) collective-permute-start(bf16[576,256]{1,0:T(8,128)(2,1)S(1)} %get-tuple-element.52), channel_id=1, source_target_pairs={{0,64},{16,80},{32,96},{48,112},{64,0},{80,16},{96,32},{112,48},{1... | collective-permute-start | bytes 884744 | tf_op jit(solution)/shard_map/ppermute | solution.py:356
  184.7 8.4 %collective-permute-start.11 = (bf16[576,256]{1,0:T(8,128)(2,1)S(1)}, bf16[576,256]{1,0:T(8,128)(2,1)S(1)}, u32[]{:S(2)}, u32[]{:S(2)}) collective-permute-start(bf16[576,256]{1,0:T(8,128)(2,1)S(1)} %get-tuple-element.50), channel_id=1, source_target_pairs={{0,192},{16,208},{32,224},{48,240},{64,128},{80,144},{96,160},{112... | collective-permute-start | bytes 884744 | tf_op jit(solution)/shard_map/ppermute | solution.py:356
  188.4 6.4 %collective-permute-start.12 = (bf16[576,128]{1,0:T(8,128)(2,1)S(1)}, bf16[576,128]{1,0:T(8,128)(2,1)S(1)}, u32[]{:S(2)}, u32[]{:S(2)}) collective-permute-start(bf16[576,128]{1,0:T(8,128)(2,1)S(1)} %get-tuple-element.63), channel_id=1, source_target_pairs={{0,48},{16,32},{32,16},{48,0},{64,112},{80,96},{96,80},{112,64},{1... | collective-permute-start | bytes 442376 | tf_op jit(solution)/shard_map/ppermute | solution.py:356
  188.9 6.0 %collective-permute-start.13 = (bf16[576,128]{1,0:T(8,128)(2,1)S(1)}, bf16[576,128]{1,0:T(8,128)(2,1)S(1)}, u32[]{:S(2)}, u32[]{:S(2)}) collective-permute-start(bf16[576,128]{1,0:T(8,128)(2,1)S(1)} %get-tuple-element.61), channel_id=1, source_target_pairs={{0,16},{16,0},{32,48},{48,32},{64,80},{80,64},{96,112},{112,96},{1... | collective-permute-start | bytes 442376 | tf_op jit(solution)/shard_map/ppermute | solution.py:356
  189.3 5.6 %collective-permute-start.14 = (bf16[576,128]{1,0:T(8,128)(2,1)S(1)}, bf16[576,128]{1,0:T(8,128)(2,1)S(1)}, u32[]{:S(2)}, u32[]{:S(2)}) collective-permute-start(bf16[576,128]{1,0:T(8,128)(2,1)S(1)} %get-tuple-element.59), channel_id=1, source_target_pairs={{0,192},{16,208},{32,224},{48,240},{64,128},{80,144},{96,160},{112... | collective-permute-start | bytes 442376 | tf_op jit(solution)/shard_map/ppermute | solution.py:356
  193.1 5.2 %collective-permute-start.15 = (bf16[576,128]{1,0:T(8,128)(2,1)S(1)}, bf16[576,128]{1,0:T(8,128)(2,1)S(1)}, u32[]{:S(2)}, u32[]{:S(2)}) collective-permute-start(bf16[576,128]{1,0:T(8,128)(2,1)S(1)} %get-tuple-element.57), channel_id=1, source_target_pairs={{0,64},{16,80},{32,96},{48,112},{64,0},{80,16},{96,32},{112,48},{1... | collective-permute-start | bytes 442376 | tf_op jit(solution)/shard_map/ppermute | solution.py:356
  198.3 1.0 copy-start.7
